TPU v7x, 32 devices: a whole 2x2x4 slice. The times are simulated.
32 devices in a mesh: ctx: 16 (over z, x, core), fsdp: 2 (over y).
Axes of the slice: x: 2, y: 2, z: 4, core: 2. Of those that a mesh axis runs over, the one named last changes fastest.
Arguments:
- tokens: bfloat16 [4, 1024, 768], P('fsdp', 'ctx'), may hold values from -6 to 6
- w_qkv: bfloat16 [2, 768, 2304], P(None, ('ctx', 'fsdp')), may hold values from -0.21875 to 0.21875
- b_qv: bfloat16 [2, 1536], P(None, ('ctx', 'fsdp')), may hold values from -0.75 to 0.75
- w_proj: bfloat16 [2, 768, 768], P(None, ('ctx', 'fsdp')), may hold values from -6 to 6
- b_proj: bfloat16 [2, 768], P(None, ('ctx', 'fsdp')), may hold values from -4 to 4
- ln1_gain: bfloat16 [2, 768], P(None, ('ctx', 'fsdp')), may hold values from 0.5 to 1.5
- ln1_bias: bfloat16 [2, 768], P(None, ('ctx', 'fsdp')), may hold values from -1.5 to 1.5
- ln2_gain: bfloat16 [2, 768], P(None, ('ctx', 'fsdp')), may hold values from 0.5 to 1.5
- ln2_bias: bfloat16 [2, 768], P(None, ('ctx', 'fsdp')), may hold values from -1.5 to 1.5
- w_fc: bfloat16 [2, 768, 3072], P(None, ('ctx', 'fsdp')), may hold values from -0.21875 to 0.21875
- b_fc: bfloat16 [2, 3072], P(None, ('ctx', 'fsdp')), may hold values from -4 to 4
- w_out: bfloat16 [2, 3072, 768], P(None, ('ctx', 'fsdp')), may hold values from -0.109375 to 0.109375
- b_out: bfloat16 [2, 768], P(None, ('ctx', 'fsdp')), may hold values from -4 to 4
- d_out: bfloat16 [4, 1024, 768], P('fsdp', 'ctx'), may hold values from -6 to 6
Outputs:
- output_tokens: bfloat16 [4, 1024, 768], P('fsdp', 'ctx')
- grad_tokens: float32 [4, 1024, 768], P('fsdp', 'ctx')
- grad_w_qkv: float32 [2, 768, 2304], P(None, ('ctx', 'fsdp'))
- grad_b_qv: float32 [2, 1536], P(None, ('ctx', 'fsdp'))
- grad_w_proj: float32 [2, 768, 768], P(None, ('ctx', 'fsdp'))
- grad_b_proj: float32 [2, 768], P(None, ('ctx', 'fsdp'))
- grad_ln1_gain: float32 [2, 768], P(None, ('ctx', 'fsdp'))
- grad_ln1_bias: float32 [2, 768], P(None, ('ctx', 'fsdp'))
- grad_ln2_gain: float32 [2, 768], P(None, ('ctx', 'fsdp'))
- grad_ln2_bias: float32 [2, 768], P(None, ('ctx', 'fsdp'))
- grad_w_fc: float32 [2, 768, 3072], P(None, ('ctx', 'fsdp'))
- grad_b_fc: float32 [2, 3072], P(None, ('ctx', 'fsdp'))
- grad_w_out: float32 [2, 3072, 768], P(None, ('ctx', 'fsdp'))
- grad_b_out: float32 [2, 768], P(None, ('ctx', 'fsdp'))
All inputs are finite; a program needn't handle non-finite values.
Results may differ from a plain program's by a relative error of at most 0.025.
Values may be sent and summed in bfloat16 or wider, within the bound.
No kernel may reach another device: no remote copies, remote signals or barrier semaphores. Data moves between devices by JAX's collectives and lax.ppermute only.
A program may use at most 448 MiB of HBM per device.

v0:
```python
import jax
import jax.numpy as jnp
from jax import lax
from jax.sharding import PartitionSpec as P

D = 768
H = 12
HD = 64
LAYERS = 2


masked_score = -1e30


def norm_rows(values, gain, shift):
    center = values - jnp.mean(values, -1, keepdims=True)
    spread = jnp.mean(center * center, -1, keepdims=True)
    return center * lax.rsqrt(spread + 1e-05) * gain + shift


def norm_grad(values, gain, shift, cotangent):
    _, pull = jax.vjp(norm_rows, values, gain, shift)
    return pull(cotangent)


def gelu_tanh(values):
    return jax.nn.gelu(values, approximate=True)


def gelu_grad(values, cotangent):
    _, pull = jax.vjp(gelu_tanh, values)
    return pull(cotangent)[0]


def fetch_layer(layer_no, params):
    local = tuple((item[layer_no] for item in params))
    whole = (
        lax.all_gather(local[0], ("ctx", "fsdp"), axis=0, tiled=True),
        lax.all_gather(local[1], ("ctx", "fsdp"), axis=0, tiled=True),
        lax.all_gather(local[2], ("ctx", "fsdp"), axis=0, tiled=True),
        lax.all_gather(local[3], ("ctx", "fsdp"), axis=0, tiled=True),
        lax.all_gather(local[4], ("ctx", "fsdp"), axis=0, tiled=True),
        lax.all_gather(local[5], ("ctx", "fsdp"), axis=0, tiled=True),
        lax.all_gather(local[6], ("ctx", "fsdp"), axis=0, tiled=True),
        lax.all_gather(local[7], ("ctx", "fsdp"), axis=0, tiled=True),
        lax.all_gather(local[8], ("ctx", "fsdp"), axis=0, tiled=True),
        lax.all_gather(local[9], ("ctx", "fsdp"), axis=0, tiled=True),
        lax.all_gather(local[10], ("ctx", "fsdp"), axis=0, tiled=True),
        lax.all_gather(local[11], ("ctx", "fsdp"), axis=0, tiled=True),
    )
    return tuple(whole)


def attend_forward(queries, keys, values, own_first):
    sequences, block_rows, head_count, head_dim = queries.shape
    query_pos = own_first + jnp.arange(block_rows)
    own_last = own_first + block_rows - 1
    start_state = (
        jnp.full((sequences, head_count, block_rows), masked_score, jnp.float32),
        jnp.zeros((sequences, head_count, block_rows), jnp.float32),
        jnp.zeros((sequences, head_count, block_rows, head_dim), jnp.float32),
    )
    shards = (
        lax.all_gather(keys, "ctx", axis=1, tiled=True),
        lax.all_gather(values, "ctx", axis=1, tiled=True),
    )

    def attend_update(state_old):
        running_max, totals, weighted = state_old
        key_part, value_part = shards
        key_pos = jnp.arange(key_part.shape[1])
        allowed = (key_pos[None, :] <= query_pos[:, None])[None, None]
        scores = (
            jnp.einsum("sqhe,skhe->shqk", queries, key_part, preferred_element_type=jnp.float32)
            * 0.125
        )
        scores = jnp.where(allowed, scores, masked_score)
        new_max = jnp.maximum(running_max, jnp.max(scores, -1))
        weights = jnp.where(allowed, jnp.exp(scores - new_max[..., None]), 0.0)
        totals = jnp.sum(weights, -1)
        weighted = jnp.einsum(
            "shqk,skhe->shqe",
            weights.astype(jnp.bfloat16),
            value_part,
            preferred_element_type=jnp.float32,
        )
        return (new_max, totals, weighted)

    running_max, totals, weighted = lax.cond(
        jnp.int32(0) <= own_last, attend_update, lambda unchanged: unchanged, start_state
    )
    attended = jnp.transpose(weighted / totals[..., None], (0, 2, 1, 3))
    log_total = jnp.transpose(running_max + jnp.log(totals), (0, 2, 1))
    return (attended, log_total)


def query_grads(queries, keys, values, grad_attended, log_total, products, own_first):
    block_rows = queries.shape[1]
    query_pos = own_first + jnp.arange(block_rows)
    own_last = own_first + block_rows - 1
    total_t = jnp.transpose(log_total, (0, 2, 1))
    product_t = jnp.transpose(products, (0, 2, 1))
    shards = (
        lax.all_gather(keys, "ctx", axis=1, tiled=True),
        lax.all_gather(values, "ctx", axis=1, tiled=True),
    )

    def query_update(grad_old):
        key_part, value_part = shards
        key_pos = jnp.arange(key_part.shape[1])
        allowed = (key_pos[None, :] <= query_pos[:, None])[None, None]
        scores = (
            jnp.einsum("sqhe,skhe->shqk", queries, key_part, preferred_element_type=jnp.float32)
            * 0.125
        )
        probs = jnp.where(allowed, jnp.exp(scores - total_t[..., None]), 0.0)
        grad_probs = jnp.einsum(
            "sqhe,skhe->shqk", grad_attended, value_part, preferred_element_type=jnp.float32
        )
        grad_scores = (probs * (grad_probs - product_t[..., None])).astype(jnp.bfloat16)
        return 0.125 * jnp.einsum(
            "shqk,skhe->sqhe", grad_scores, key_part, preferred_element_type=jnp.float32
        )

    return lax.cond(
        jnp.int32(0) <= own_last,
        query_update,
        lambda unchanged: unchanged,
        jnp.zeros(queries.shape, jnp.float32),
    )


def key_grads(queries, keys, values, grad_attended, log_total, products, own_first):
    block_rows = keys.shape[1]
    key_pos = own_first + jnp.arange(block_rows)
    total_all, product_all = (
        lax.all_gather(log_total, "ctx", axis=1, tiled=True),
        lax.all_gather(products, "ctx", axis=1, tiled=True),
    )
    start_state = (jnp.zeros(keys.shape, jnp.float32), jnp.zeros(values.shape, jnp.float32))
    query_part = lax.all_gather(queries, "ctx", axis=1, tiled=True)
    grad_part = lax.all_gather(grad_attended, "ctx", axis=1, tiled=True)
    span_rows = query_part.shape[1]

    def key_update(grad_old):
        query_pos = jnp.arange(span_rows)
        allowed = (key_pos[None, :] <= query_pos[:, None])[None, None]
        total_part = jnp.transpose(total_all, (0, 2, 1))
        product_part = jnp.transpose(product_all, (0, 2, 1))
        scores = (
            jnp.einsum("sqhe,skhe->shqk", query_part, keys, preferred_element_type=jnp.float32)
            * 0.125
        )
        probs = jnp.where(allowed, jnp.exp(scores - total_part[..., None]), 0.0)
        grad_value = jnp.einsum(
            "shqk,sqhe->skhe",
            probs.astype(jnp.bfloat16),
            grad_part,
            preferred_element_type=jnp.float32,
        )
        grad_probs = jnp.einsum(
            "sqhe,skhe->shqk", grad_part, values, preferred_element_type=jnp.float32
        )
        grad_scores = (probs * (grad_probs - product_part[..., None])).astype(jnp.bfloat16)
        grad_key = 0.125 * jnp.einsum(
            "shqk,sqhe->skhe", grad_scores, query_part, preferred_element_type=jnp.float32
        )
        return (grad_key, grad_value)

    return lax.cond(
        jnp.int32(0) + span_rows - 1 >= own_first,
        key_update,
        lambda unchanged: unchanged,
        start_state,
    )


def layer_forward(inputs, weights, own_first):
    (
        w_qkv,
        b_qv,
        w_proj,
        b_proj,
        gain_one,
        shift_one,
        gain_two,
        shift_two,
        w_fc,
        b_fc,
        w_out,
        b_out,
    ) = weights
    sequences, block_rows, _ = inputs.shape
    token_count = sequences * block_rows
    flat_in = inputs.reshape(token_count, D)
    normed = norm_rows(flat_in, gain_one.astype(jnp.float32), shift_one.astype(jnp.float32)).astype(
        jnp.bfloat16
    )
    projected = jnp.dot(normed, w_qkv, preferred_element_type=jnp.float32)
    queries = (
        (projected[:, :D] + b_qv[:D].astype(jnp.float32))
        .astype(jnp.bfloat16)
        .reshape(sequences, block_rows, H, HD)
    )
    keys = projected[:, D : 2 * D].astype(jnp.bfloat16).reshape(sequences, block_rows, H, HD)
    values = (
        (projected[:, 2 * D :] + b_qv[D:].astype(jnp.float32))
        .astype(jnp.bfloat16)
        .reshape(sequences, block_rows, H, HD)
    )
    attended, log_total = attend_forward(queries, keys, values, own_first)
    attended_low = attended.astype(jnp.bfloat16).reshape(token_count, D)
    middle = (
        flat_in
        + jnp.dot(attended_low, w_proj, preferred_element_type=jnp.float32)
        + b_proj.astype(jnp.float32)
    )
    normed_two = norm_rows(
        middle, gain_two.astype(jnp.float32), shift_two.astype(jnp.float32)
    ).astype(jnp.bfloat16)
    up_proj = jnp.dot(normed_two, w_fc, preferred_element_type=jnp.float32) + b_fc.astype(
        jnp.float32
    )
    act_low = gelu_tanh(up_proj).astype(jnp.bfloat16)
    result = (
        middle
        + jnp.dot(act_low, w_out, preferred_element_type=jnp.float32)
        + b_out.astype(jnp.float32)
    )
    saved = (
        flat_in,
        normed,
        queries,
        keys,
        values,
        attended,
        log_total,
        attended_low,
        middle,
        normed_two,
        up_proj,
        act_low,
    )
    return (result.reshape(sequences, block_rows, D), saved)


def layer_backward(grad_in, weights, saved, own_first):
    (
        w_qkv,
        b_qv,
        w_proj,
        b_proj,
        gain_one,
        shift_one,
        gain_two,
        shift_two,
        w_fc,
        b_fc,
        w_out,
        b_out,
    ) = weights
    (
        flat_in,
        normed,
        queries,
        keys,
        values,
        attended,
        log_total,
        attended_low,
        middle,
        normed_two,
        up_proj,
        act_low,
    ) = saved
    sequences, block_rows = (queries.shape[0], queries.shape[1])
    token_count = sequences * block_rows
    grad_flat = grad_in.reshape(token_count, D)
    grad_branch = grad_flat.astype(jnp.bfloat16)
    grad_w_out = jnp.dot(act_low.T, grad_branch, preferred_element_type=jnp.float32)
    grad_b_out = jnp.sum(grad_branch.astype(jnp.float32), 0)
    grad_act = jnp.dot(grad_branch, w_out.T, preferred_element_type=jnp.float32)
    grad_up = gelu_grad(up_proj, grad_act).astype(jnp.bfloat16)
    grad_w_fc = jnp.dot(normed_two.T, grad_up, preferred_element_type=jnp.float32)
    grad_b_fc = jnp.sum(grad_up.astype(jnp.float32), 0)
    grad_normed_two = jnp.dot(grad_up, w_fc.T, preferred_element_type=jnp.float32)
    grad_mid_norm, grad_gain_two, grad_shift_two = norm_grad(
        middle, gain_two.astype(jnp.float32), shift_two.astype(jnp.float32), grad_normed_two
    )
    grad_mid = grad_flat + grad_mid_norm
    grad_attn = grad_mid.astype(jnp.bfloat16)
    grad_w_proj = jnp.dot(attended_low.T, grad_attn, preferred_element_type=jnp.float32)
    grad_b_proj = jnp.sum(grad_attn.astype(jnp.float32), 0)
    grad_attended = (
        jnp.dot(grad_attn, w_proj.T, preferred_element_type=jnp.float32)
        .astype(jnp.bfloat16)
        .reshape(sequences, block_rows, H, HD)
    )
    products = jnp.sum(grad_attended.astype(jnp.float32) * attended, -1)
    grad_query = query_grads(queries, keys, values, grad_attended, log_total, products, own_first)
    grad_key, grad_value = key_grads(
        queries, keys, values, grad_attended, log_total, products, own_first
    )
    grad_joined = jnp.concatenate(
        [
            grad_query.reshape(token_count, D),
            grad_key.reshape(token_count, D),
            grad_value.reshape(token_count, D),
        ],
        1,
    ).astype(jnp.bfloat16)
    grad_w_qkv = jnp.dot(normed.T, grad_joined, preferred_element_type=jnp.float32)
    joined_sums = jnp.sum(grad_joined.astype(jnp.float32), 0)
    grad_b_qv = jnp.concatenate([joined_sums[:D], joined_sums[2 * D :]])
    grad_normed = jnp.dot(grad_joined, w_qkv.T, preferred_element_type=jnp.float32)
    grad_in_norm, grad_gain_one, grad_shift_one = norm_grad(
        flat_in, gain_one.astype(jnp.float32), shift_one.astype(jnp.float32), grad_normed
    )
    grad_out = grad_mid + grad_in_norm
    gradients = (
        grad_w_qkv,
        grad_b_qv,
        grad_w_proj,
        grad_b_proj,
        grad_gain_one,
        grad_shift_one,
        grad_gain_two,
        grad_shift_two,
        grad_w_fc,
        grad_b_fc,
        grad_w_out,
        grad_b_out,
    )
    return (grad_out.reshape(sequences, block_rows, D), gradients)


def pair_major(item, wide_count, pair_count):
    shape = item.shape
    grouped = item.reshape(
        (wide_count, pair_count, shape[0] // (wide_count * pair_count)) + shape[1:]
    )
    return jnp.swapaxes(grouped, 0, 1).reshape(shape)


def reduce_layer(gradients):
    wide_count = lax.axis_size("ctx")
    pair_count = lax.axis_size("fsdp")
    moved = tuple((pair_major(item, wide_count, pair_count) for item in gradients))
    halves = (
        lax.psum_scatter(
            moved[0].astype(jnp.bfloat16), "fsdp", scatter_dimension=0, tiled=True
        ).astype(jnp.float32),
        lax.psum_scatter(
            moved[1].astype(jnp.bfloat16), "fsdp", scatter_dimension=0, tiled=True
        ).astype(jnp.float32),
        lax.psum_scatter(
            moved[2].astype(jnp.bfloat16), "fsdp", scatter_dimension=0, tiled=True
        ).astype(jnp.float32),
        lax.psum_scatter(
            moved[3].astype(jnp.bfloat16), "fsdp", scatter_dimension=0, tiled=True
        ).astype(jnp.float32),
        lax.psum_scatter(
            moved[4].astype(jnp.bfloat16), "fsdp", scatter_dimension=0, tiled=True
        ).astype(jnp.float32),
        lax.psum_scatter(
            moved[5].astype(jnp.bfloat16), "fsdp", scatter_dimension=0, tiled=True
        ).astype(jnp.float32),
        lax.psum_scatter(
            moved[6].astype(jnp.bfloat16), "fsdp", scatter_dimension=0, tiled=True
        ).astype(jnp.float32),
        lax.psum_scatter(
            moved[7].astype(jnp.bfloat16), "fsdp", scatter_dimension=0, tiled=True
        ).astype(jnp.float32),
        lax.psum_scatter(
            moved[8].astype(jnp.bfloat16), "fsdp", scatter_dimension=0, tiled=True
        ).astype(jnp.float32),
        lax.psum_scatter(
            moved[9].astype(jnp.bfloat16), "fsdp", scatter_dimension=0, tiled=True
        ).astype(jnp.float32),
        lax.psum_scatter(
            moved[10].astype(jnp.bfloat16), "fsdp", scatter_dimension=0, tiled=True
        ).astype(jnp.float32),
        lax.psum_scatter(
            moved[11].astype(jnp.bfloat16), "fsdp", scatter_dimension=0, tiled=True
        ).astype(jnp.float32),
    )
    reduced = (
        lax.psum_scatter(halves[0], "ctx", scatter_dimension=0, tiled=True),
        lax.psum_scatter(halves[1], "ctx", scatter_dimension=0, tiled=True),
        lax.psum_scatter(halves[2], "ctx", scatter_dimension=0, tiled=True),
        lax.psum_scatter(halves[3], "ctx", scatter_dimension=0, tiled=True),
        lax.psum_scatter(halves[4], "ctx", scatter_dimension=0, tiled=True),
        lax.psum_scatter(halves[5], "ctx", scatter_dimension=0, tiled=True),
        lax.psum_scatter(halves[6], "ctx", scatter_dimension=0, tiled=True),
        lax.psum_scatter(halves[7], "ctx", scatter_dimension=0, tiled=True),
        lax.psum_scatter(halves[8], "ctx", scatter_dimension=0, tiled=True),
        lax.psum_scatter(halves[9], "ctx", scatter_dimension=0, tiled=True),
        lax.psum_scatter(halves[10], "ctx", scatter_dimension=0, tiled=True),
        lax.psum_scatter(halves[11], "ctx", scatter_dimension=0, tiled=True),
    )
    return tuple(reduced)


def body(
    tokens,
    w_qkv,
    b_qv,
    w_proj,
    b_proj,
    ln1_gain,
    ln1_bias,
    ln2_gain,
    ln2_bias,
    w_fc,
    b_fc,
    w_out,
    b_out,
    d_out,
):
    params = (
        w_qkv,
        b_qv,
        w_proj,
        b_proj,
        ln1_gain,
        ln1_bias,
        ln2_gain,
        ln2_bias,
        w_fc,
        b_fc,
        w_out,
        b_out,
    )
    own_first = lax.axis_index("ctx") * tokens.shape[1]
    hidden = tokens.astype(jnp.float32)
    stored = []
    forward_weights = []
    for layer_no in range(LAYERS):
        weights = fetch_layer(layer_no, params)
        forward_weights.append(weights)
        hidden, saved = layer_forward(hidden, weights, own_first)
        stored.append(saved)
    grad_hidden = d_out.astype(jnp.float32)
    collected = [None] * LAYERS
    for layer_no in reversed(range(LAYERS)):
        weights = fetch_layer(layer_no, params)
        grad_hidden, gradients = layer_backward(grad_hidden, weights, stored[layer_no], own_first)
        collected[layer_no] = reduce_layer(gradients)
    stacked = tuple(
        (jnp.stack([collected[layer_no][slot] for layer_no in range(LAYERS)]) for slot in range(12))
    )
    return (
        hidden.astype(jnp.bfloat16),
        grad_hidden,
        stacked[0],
        stacked[1],
        stacked[2],
        stacked[3],
        stacked[4],
        stacked[5],
        stacked[6],
        stacked[7],
        stacked[8],
        stacked[9],
        stacked[10],
        stacked[11],
    )


def solution(mesh):
    in_specs = (
        P("fsdp", "ctx", None),
        P(None, ("ctx", "fsdp"), None),
        P(None, ("ctx", "fsdp")),
        P(None, ("ctx", "fsdp"), None),
        P(None, ("ctx", "fsdp")),
        P(None, ("ctx", "fsdp")),
        P(None, ("ctx", "fsdp")),
        P(None, ("ctx", "fsdp")),
        P(None, ("ctx", "fsdp")),
        P(None, ("ctx", "fsdp"), None),
        P(None, ("ctx", "fsdp")),
        P(None, ("ctx", "fsdp"), None),
        P(None, ("ctx", "fsdp")),
        P("fsdp", "ctx", None),
    )
    out_specs = (
        P("fsdp", "ctx", None),
        P("fsdp", "ctx", None),
        P(None, ("ctx", "fsdp"), None),
        P(None, ("ctx", "fsdp")),
        P(None, ("ctx", "fsdp"), None),
        P(None, ("ctx", "fsdp")),
        P(None, ("ctx", "fsdp")),
        P(None, ("ctx", "fsdp")),
        P(None, ("ctx", "fsdp")),
        P(None, ("ctx", "fsdp")),
        P(None, ("ctx", "fsdp"), None),
        P(None, ("ctx", "fsdp")),
        P(None, ("ctx", "fsdp"), None),
        P(None, ("ctx", "fsdp")),
    )
    return jax.shard_map(body, mesh=mesh, in_specs=in_specs, out_specs=out_specs, check_vma=False)
```

profile of v0, /device:TPU:0, one launch (start us, length us, event | category | flops | bytes accessed | tf_op | source)
XLA Modules:
  0.0 2074.5 jit_solution(8372499558750997149)
XLA Ops:
  86.6 55.7 %all-gather.43.cloned.1.call-done = bf16[2,1024,12,64]{3,0,2,1:T(2,128)(2,1)} async-done(((bf16[2,64,12,64]{3,0,2,1:T(2,128)(2,1)}), bf16[2,1024,12,64]{3,0,2,1:T(2,128)(2,1)}) %all-gather.43.cloned.1.call-update) | async-done | bytes 3145744 | tf_op jit(solution)/shard_map/all_gather | solution.py:65
  142.3 63.3 %all-gather.41.cloned.1.call-done = bf16[2,1024,12,64]{3,0,2,1:T(2,128)(2,1)} async-done(((bf16[2,64,12,64]{3,0,2,1:T(2,128)(2,1)}), bf16[2,1024,12,64]{3,0,2,1:T(2,128)(2,1)}) %all-gather.41.cloned.1.call-update) | async-done | bytes 3145744 | tf_op jit(solution)/shard_map/all_gather | solution.py:64
  263.2 64.0 %all-gather.61.cloned.1.call-done = bf16[1,768,3072]{2,1,0:T(8,128)(2,1)} async-done(((bf16[1,24,3072]{2,1,0:T(8,128)(2,1)}), bf16[1,768,3072]{2,1,0:T(8,128)(2,1)}) %all-gather.61.cloned.1.call-update) | async-done | bytes 4718608 | tf_op jit(solution)/shard_map/all_gather | solution.py:46
  330.4 62.6 %all-gather.63.cloned.1.call-done = bf16[1,3072,768]{2,1,0:T(8,128)(2,1)} async-done(((bf16[1,96,768]{2,1,0:T(8,128)(2,1)}), bf16[1,3072,768]{2,1,0:T(8,128)(2,1)}) %all-gather.63.cloned.1.call-update) | async-done | bytes 4718608 | tf_op jit(solution)/shard_map/all_gather | solution.py:48
  396.7 58.2 %all-gather.65.cloned.1.call-done = bf16[1,768,2304]{2,1,0:T(8,128)(2,1)} async-done(((bf16[1,24,2304]{2,1,0:T(8,128)(2,1)}), bf16[1,768,2304]{2,1,0:T(8,128)(2,1)}) %all-gather.65.cloned.1.call-update) | async-done | bytes 3538960 | tf_op jit(solution)/shard_map/all_gather | solution.py:38
  473.5 49.1 %all-gather.47.cloned.1.call-done = bf16[2,1024,12,64]{3,0,2,1:T(2,128)(2,1)} async-done(((bf16[2,64,12,64]{3,0,2,1:T(2,128)(2,1)}), bf16[2,1024,12,64]{3,0,2,1:T(2,128)(2,1)}) %all-gather.47.cloned.1.call-update) | async-done | bytes 3145744 | tf_op jit(solution)/shard_map/all_gather | solution.py:65
  522.6 63.3 %all-gather.45.cloned.1.call-done = bf16[2,1024,12,64]{3,0,2,1:T(2,128)(2,1)} async-done(((bf16[2,64,12,64]{3,0,2,1:T(2,128)(2,1)}), bf16[2,1024,12,64]{3,0,2,1:T(2,128)(2,1)}) %all-gather.45.cloned.1.call-update) | async-done | bytes 3145744 | tf_op jit(solution)/shard_map/all_gather | solution.py:64
  643.4 63.6 %all-gather.69.cloned.1.call-done = bf16[1,768,3072]{2,1,0:T(8,128)(2,1)} async-done(((bf16[1,24,3072]{2,1,0:T(8,128)(2,1)}), bf16[1,768,3072]{2,1,0:T(8,128)(2,1)}) %all-gather.69.cloned.1.call-update) | async-done | bytes 4718608 | tf_op jit(solution)/shard_map/all_gather | solution.py:46
  712.1 60.7 %all-gather.71.cloned.1.call-done = bf16[1,3072,768]{2,1,0:T(8,128)(2,1)} async-done(((bf16[1,96,768]{2,1,0:T(8,128)(2,1)}), bf16[1,3072,768]{2,1,0:T(8,128)(2,1)}) %all-gather.71.cloned.1.call-update) | async-done | bytes 4718608 | tf_op jit(solution)/shard_map/all_gather | solution.py:48
  903.6 62.4 %conditional.9 = (bf16[128,768]{0,1:T(8,128)(2,1)S(1)}, bf16[128,768]{0,1:T(8,128)(2,1)S(1)}) conditional(s32[]{:T(128)} %convert_element_type.552, () %tuple.74, (s32[64]{0:T(128)}, bf16[2,1024,12,64]{3,0,2,1:T(2,128)(2,1)}, bf16[2,64,12,64]{1,0,3,2:T(2,128)(2,1)S(1)}, f32[2,1024,12]{2,0,1:T(2,128)}, bf16[2,1024,12,64]{3,0,2,1:T(2,128)(2,1)}, ...), branch_computations={%region_21.22_spmd, %region_22.23_spmd} | conditional | flops 821395456 | bytes 48070956 | solution.py:170
  1137.9 53.3 %conditional.11 = (bf16[128,768]{1,0:T(8,128)(2,1)S(1)}, bf16[128,768]{1,0:T(8,128)(2,1)S(1)}) conditional(s32[]{:T(128)} %convert_element_type.552, () %tuple.78, (s32[64]{0:T(128)}, bf16[2,1024,12,64]{3,0,2,1:T(2,128)(2,1)}, bf16[2,64,12,64]{1,0,3,2:T(2,128)(2,1)S(1)}, f32[2,1024,12]{2,0,1:T(2,128)S(1)}, bf16[2,1024,12,64]{3,0,2,1:T(2,128)(2,1)}, ...), branch_computations={%region_30.31_spmd, %region_31.32_spmd} | conditional | flops 821395456 | bytes 48070956 | solution.py:170
  1203.1 58.0 %reduce-scatter.41.cloned.1.call-done = bf16[1536,768]{1,0:T(8,128)(2,1)} async-done(((bf16[3072,768]{1,0:T(8,128)(2,1)}), bf16[1536,768]{1,0:T(8,128)(2,1)}) %reduce-scatter.41.cloned.1.call-update) | async-done | bytes 2359312 | tf_op jit(solution)/shard_map/reduce_scatter | solution.py:380
  1265.4 58.1 %reduce-scatter.37.cloned.1.call-done = bf16[384,3072]{1,0:T(8,128)(2,1)} async-done(((bf16[768,3072]{1,0:T(8,128)(2,1)}), bf16[384,3072]{1,0:T(8,128)(2,1)}) %reduce-scatter.37.cloned.1.call-update) | async-done | bytes 2359312 | tf_op jit(solution)/shard_map/reduce_scatter | solution.py:374
  1328.0 57.9 %reduce-scatter.33.cloned.1.call-done = bf16[384,3072]{1,0:T(8,128)(2,1)} async-done(((bf16[768,3072]{1,0:T(8,128)(2,1)}), bf16[384,3072]{1,0:T(8,128)(2,1)}) %reduce-scatter.33.cloned.1.call-update) | async-done | bytes 2359312 | tf_op jit(solution)/shard_map/reduce_scatter | solution.py:374
  1390.5 45.4 %reduce-scatter.21.cloned.1.call-done = bf16[384,2304]{1,0:T(8,128)(2,1)} async-done(((bf16[768,2304]{1,0:T(8,128)(2,1)}), bf16[384,2304]{1,0:T(8,128)(2,1)}) %reduce-scatter.21.cloned.1.call-update) | async-done | bytes 1769488 | tf_op jit(solution)/shard_map/reduce_scatter | solution.py:350
  1453.7 44.3 %reduce-scatter.31.cloned.1.call-done = f32[24,768]{1,0:T(8,128)} async-done(((f32[384,768]{1,0:T(8,128)}), f32[24,768]{1,0:T(8,128)}) %reduce-scatter.31.cloned.1.call-update) | async-done | bytes 73744 | tf_op jit(solution)/shard_map/reduce_scatter | solution.py:390
  1498.0 61.1 %reduce-scatter.27.cloned.1.call-done = f32[24,768]{1,0:T(8,128)} async-done(((f32[384,768]{1,0:T(8,128)}), f32[24,768]{1,0:T(8,128)}) %reduce-scatter.27.cloned.1.call-update) | async-done | bytes 73744 | tf_op jit(solution)/shard_map/reduce_scatter | solution.py:390
  1561.0 47.0 %reduce-scatter.17.cloned.1.call-done = bf16[384,2304]{1,0:T(8,128)(2,1)} async-done(((bf16[768,2304]{1,0:T(8,128)(2,1)}), bf16[384,2304]{1,0:T(8,128)(2,1)}) %reduce-scatter.17.cloned.1.call-update) | async-done | bytes 1769488 | tf_op jit(solution)/shard_map/reduce_scatter | solution.py:350
  1624.0 60.9 %all-reduce.48 = (f32[768]{0:T(1024)S(1)}, f32[768]{0:T(1024)S(1)}, f32[384]{0:T(512)S(1)}, f32[384]{0:T(512)S(1)}, f32[384]{0:T(512)S(1)}, /*index=5*/f32[384]{...) all-reduce(f32[768]{0:T(1024)S(1)} %get-tuple-element.457, ...), channel_id=33, replica_groups=mesh['ctx'=16,'fsdp'=2] {'ctx'}, use_global_device_ids=true, to_apply=%region_43.44.clone | all-reduce | flops 9216 | bytes 73728
  1691.5 75.3 %reduce-scatter.43.cloned.1.call-done = f32[96,768]{1,0:T(8,128)} async-done(((f32[1536,768]{1,0:T(8,128)}), f32[96,768]{1,0:T(8,128)}) %reduce-scatter.43.cloned.1.call-update) | async-done | bytes 294928 | tf_op jit(solution)/shard_map/reduce_scatter | solution.py:398
  1768.7 76.6 %reduce-scatter.39.cloned.1.call-done = f32[24,3072]{1,0:T(8,128)} async-done(((f32[384,3072]{1,0:T(8,128)}), f32[24,3072]{1,0:T(8,128)}) %reduce-scatter.39.cloned.1.call-update) | async-done | bytes 294928 | tf_op jit(solution)/shard_map/reduce_scatter | solution.py:396
  1845.3 78.8 %reduce-scatter.35.cloned.1.call-done = f32[24,3072]{1,0:T(8,128)} async-done(((f32[384,3072]{1,0:T(8,128)}), f32[24,3072]{1,0:T(8,128)}) %reduce-scatter.35.cloned.1.call-update) | async-done | bytes 294928 | tf_op jit(solution)/shard_map/reduce_scatter | solution.py:396
  1926.0 69.1 %reduce-scatter.23.cloned.1.call-done = f32[24,2304]{1,0:T(8,128)} async-done(((f32[384,2304]{1,0:T(8,128)}), f32[24,2304]{1,0:T(8,128)}) %reduce-scatter.23.cloned.1.call-update) | async-done | bytes 221200 | tf_op jit(solution)/shard_map/reduce_scatter | solution.py:388
  1995.1 70.9 %reduce-scatter.19.cloned.1.call-done = f32[24,2304]{1,0:T(8,128)} async-done(((f32[384,2304]{1,0:T(8,128)}), f32[24,2304]{1,0:T(8,128)}) %reduce-scatter.19.cloned.1.call-update) | async-done | bytes 221200 | tf_op jit(solution)/shard_map/reduce_scatter | solution.py:388
  (628 shorter events, 816.6 us)
Async XLA Ops:
  81.7 179.6 %all-gather.59.cloned.1.call-start = ((), (), s32[]{:S(2)}) async-start(), calls=%async_computation.41 | async-start | bytes 1216512 | tf_op jit(solution)/shard_map/all_gather | solution.py:40
  82.4 244.8 %all-gather.61.cloned.1.call-start = ((), (), s32[]{:S(2)}) async-start(), calls=%async_computation.42 | async-start | bytes 4866048 | tf_op jit(solution)/shard_map/all_gather | solution.py:46
  83.2 309.8 %all-gather.63.cloned.1.call-start = ((), (), s32[]{:S(2)}) async-start(), calls=%async_computation.43 | async-start | bytes 4866048 | tf_op jit(solution)/shard_map/all_gather | solution.py:48
  84.0 370.9 %all-gather.65.cloned.1.call-start = ((), (), s32[]{:S(2)}) async-start(), calls=%async_computation.44 | async-start | bytes 3649536 | tf_op jit(solution)/shard_map/all_gather | solution.py:38
  84.8 437.8 %all-gather.47.cloned.1.call-start = ((), (), s32[]{:S(2)}) async-start(), calls=%async_computation.19 | async-start | bytes 6684672 | tf_op jit(solution)/shard_map/all_gather | solution.py:65
  466.4 240.6 %all-gather.69.cloned.1.call-start = ((), (), s32[]{:S(2)}) async-start(), calls=%async_computation.46 | async-start | bytes 4866048 | tf_op jit(solution)/shard_map/all_gather | solution.py:46
  467.2 305.7 %all-gather.71.cloned.1.call-start = ((), (), s32[]{:S(2)}) async-start(), calls=%async_computation.47 | async-start | bytes 4866048 | tf_op jit(solution)/shard_map/all_gather | solution.py:48
  467.7 414.7 %all-gather.49.cloned.1.call-start = ((), (), s32[]{:S(2)}) async-start(), calls=%async_computation.20 | async-start | bytes 6684672 | tf_op jit(solution)/shard_map/all_gather | solution.py:141
  471.3 432.3 %all-gather.51.cloned.1.call-start = ((), (), s32[]{:S(2)}) async-start(), calls=%async_computation.21 | async-start | bytes 6684672 | tf_op jit(solution)/shard_map/all_gather | solution.py:142
  788.2 227.9 %reduce-scatter.29.cloned.1.call-start = ((), (), s32[]{:S(2)}) async-start(), calls=%async_computation.30 | async-start | bytes 1769472 | tf_op jit(solution)/shard_map/reduce_scatter | solution.py:356
  988.3 210.5 %reduce-scatter.45.cloned.1.call-start = ((), (), s32[]{:S(2)}) async-start(), calls=%async_computation.38 | async-start | bytes 7077888 | tf_op jit(solution)/shard_map/reduce_scatter | solution.py:380
  996.2 265.0 %reduce-scatter.41.cloned.1.call-start = ((), (), s32[]{:S(2)}) async-start(), calls=%async_computation.36 | async-start | bytes 7077888 | tf_op jit(solution)/shard_map/reduce_scatter | solution.py:380
  1000.4 323.1 %reduce-scatter.37.cloned.1.call-start = ((), (), s32[]{:S(2)}) async-start(), calls=%async_computation.34 | async-start | bytes 7077888 | tf_op jit(solution)/shard_map/reduce_scatter | solution.py:374
  1005.6 380.3 %reduce-scatter.33.cloned.1.call-start = ((), (), s32[]{:S(2)}) async-start(), calls=%async_computation.32 | async-start | bytes 7077888 | tf_op jit(solution)/shard_map/reduce_scatter | solution.py:374
  1010.8 425.0 %reduce-scatter.21.cloned.1.call-start = ((), (), s32[]{:S(2)}) async-start(), calls=%async_computation.26 | async-start | bytes 5308416 | tf_op jit(solution)/shard_map/reduce_scatter | solution.py:350
  1016.0 482.0 %reduce-scatter.31.cloned.1.call-start = ((), (), s32[]{:S(2)}) async-start(), calls=%async_computation.31 | async-start | bytes 1253376 | tf_op jit(solution)/shard_map/reduce_scatter | solution.py:390
  1018.4 540.7 %reduce-scatter.27.cloned.1.call-start = ((), (), s32[]{:S(2)}) async-start(), calls=%async_computation.29 | async-start | bytes 1253376 | tf_op jit(solution)/shard_map/reduce_scatter | solution.py:390
  1020.7 587.3 %reduce-scatter.17.cloned.1.call-start = ((), (), s32[]{:S(2)}) async-start(), calls=%async_computation.24 | async-start | bytes 5308416 | tf_op jit(solution)/shard_map/reduce_scatter | solution.py:350
  1194.3 497.2 %reduce-scatter.47.cloned.1.call-start = ((), (), s32[]{:S(2)}) async-start(), calls=%async_computation.39 | async-start | bytes 5013504 | tf_op jit(solution)/shard_map/reduce_scatter | solution.py:398
  1203.1 563.7 %reduce-scatter.43.cloned.1.call-start = ((), (), s32[]{:S(2)}) async-start(), calls=%async_computation.37 | async-start | bytes 5013504 | tf_op jit(solution)/shard_map/reduce_scatter | solution.py:398
  1265.3 580.0 %reduce-scatter.39.cloned.1.call-start = ((), (), s32[]{:S(2)}) async-start(), calls=%async_computation.35 | async-start | bytes 5013504 | tf_op jit(solution)/shard_map/reduce_scatter | solution.py:396
  1327.9 596.1 %reduce-scatter.35.cloned.1.call-start = ((), (), s32[]{:S(2)}) async-start(), calls=%async_computation.33 | async-start | bytes 5013504 | tf_op jit(solution)/shard_map/reduce_scatter | solution.py:396
  1390.4 604.7 %reduce-scatter.23.cloned.1.call-start = ((), (), s32[]{:S(2)}) async-start(), calls=%async_computation.27 | async-start | bytes 3760128 | tf_op jit(solution)/shard_map/reduce_scatter | solution.py:388
  1439.4 626.5 %reduce-scatter.19.cloned.1.call-start = ((), (), s32[]{:S(2)}) async-start(), calls=%async_computation.25 | async-start | bytes 3760128 | tf_op jit(solution)/shard_map/reduce_scatter | solution.py:388
  (113 other events, 4878.9 us)
Sparse Core Ops, SparseCore 0:
  11.5 63.2 all-gather.56
  80.3 62.0 all-gather.42
  145.2 60.4 all-gather.40
  264.6 62.5 all-gather.60
  330.5 62.4 all-gather.62
  395.9 58.9 all-gather.64
  461.9 60.6 all-gather.46
  525.4 60.4 all-gather.44
  644.4 62.5 all-gather.68
  710.3 62.4 all-gather.70
  775.1 60.6 all-gather.48
  838.5 65.0 all-gather.50
  1005.4 64.7 all-gather.52
  1072.9 64.9 all-gather.54
  1140.2 58.5 reduce-scatter.44
  1201.1 59.9 reduce-scatter.40
  1263.4 59.9 reduce-scatter.36
  1325.9 59.9 reduce-scatter.32
  1611.7 76.0 reduce-scatter.46
  1692.2 74.5 reduce-scatter.42
  1770.7 74.5 reduce-scatter.38
  1849.5 74.5 reduce-scatter.34
  1928.0 67.0 reduce-scatter.22
  1998.9 66.9 reduce-scatter.18
  (8 shorter events, 355.3 us)
where the time goes:
time: 2090 us; the launch traced here: 2070 us
  waiting for transfers between devices  1410 us (67%)
  blocking collectives  216 us (10%)
  local copies, waits for them, and re-layouts  193 us (9%)
  matrix products  161 us (8%)
  other arithmetic  72.9 us (3%)
    reduce_scatter x2, waiting for transfers between devices, reduce_layer(): lax.psum_scatter(halves[8], 'ctx', scatter_dimension=0, tiled=True)  155 us
    reduce_scatter x2, waiting for transfers between devices, reduce_layer(): lax.psum_scatter(halves[0], 'ctx', scatter_dimension=0, tiled=True)  140 us
    all_gather x2, waiting for transfers between devices, fetch_layer(): lax.all_gather(local[8], ('ctx', 'fsdp'), axis=0, tiled=True)  128 us
    all_gather x2, waiting for transfers between devices, attend_forward(): lax.all_gather(keys, 'ctx', axis=1, tiled=True)  127 us
    all_gather x2, waiting for transfers between devices, fetch_layer(): lax.all_gather(local[10], ('ctx', 'fsdp'), axis=0, tiled=True)  123 us
    reduce_scatter x2, waiting for transfers between devices, reduce_layer(): lax.psum_scatter(moved[8].astype(jnp.bfloat16), 'fsdp', scatter_dimension...  116 us
    unnamed x3, blocking collectives  112 us
    reduce_scatter x2, waiting for transfers between devices, reduce_layer(): lax.psum_scatter(halves[2], 'ctx', scatter_dimension=0, tiled=True)  105 us
  transfers between devices with their start and end apart: 32, of which 26 were waited for; matrix products, arithmetic and copies ran while one was open for 20% of the time, Pallas kernels for 0%

commit v1 on v0

v1 whole, which is shorter than its diff:
```python
import math

import jax
import jax.numpy as jnp
import numpy as np
from jax import lax
from jax.sharding import Mesh, PartitionSpec as P

D = 768
H = 12
HD = 64
LAYERS = 2
TP = 4
PH = H // TP
PW = PH * HD
EPS = 1e-05
bf16 = jnp.bfloat16
f32 = jnp.float32

ALL = ("s", "g", "p", "c", "f")
REST = ("s", "g", "c", "f")


def dot(a, b, dims=((1,), (0,))):
    return lax.dot_general(a, b, (dims, ((), ())), preferred_element_type=f32)


def swap(value, axis, mask=1):
    size = lax.axis_size(axis)
    return lax.ppermute(value, axis, [(i, i ^ mask) for i in range(size)])


def norm_stats(values):
    center = values - jnp.mean(values, -1, keepdims=True)
    scale = lax.rsqrt(jnp.mean(center * center, -1, keepdims=True) + EPS)
    return center * scale, scale


def norm_low(values, gain, shift):
    unit, _ = norm_stats(values)
    return (unit * gain + shift).astype(bf16)


def norm_back(values, gain, cotangent):
    unit, scale = norm_stats(values)
    inner = cotangent * gain
    grad = scale * (
        inner
        - jnp.mean(inner, -1, keepdims=True)
        - unit * jnp.mean(inner * unit, -1, keepdims=True)
    )
    return grad, jnp.sum(cotangent * unit, 0), jnp.sum(cotangent, 0)


def gelu(u):
    return 0.5 * u * (1.0 + jnp.tanh(math.sqrt(2.0 / math.pi) * (u + 0.044715 * u * u * u)))


def gelu_slope(u):
    root = math.sqrt(2.0 / math.pi)
    t = jnp.tanh(root * (u + 0.044715 * u * u * u))
    return 0.5 * (1.0 + t) + 0.5 * u * (1.0 - t * t) * root * (1.0 + 3 * 0.044715 * u * u)


def attend(qkv, keys_values, mask):
    q, k, v = qkv[:, :PW], keys_values[:, :PW], keys_values[:, PW:]
    q, k, v = (item.reshape(-1, PH, HD) for item in (q, k, v))
    scores = jnp.einsum("qhe,khe->hqk", q, k, preferred_element_type=f32) * 0.125
    scores = jnp.where(mask, scores, -1e30)
    top = jnp.max(scores, -1, keepdims=True)
    weights = jnp.exp(scores - top)
    total = jnp.sum(weights, -1, keepdims=True)
    probs = (weights / total).astype(bf16)
    out = jnp.einsum("hqk,khe->qhe", probs, v, preferred_element_type=f32)
    return out.reshape(-1, PW), top + jnp.log(total)


def attend_back(qkv, keys_values, mask, out, log_total, grad_out):
    q, k, v = qkv[:, :PW], keys_values[:, :PW], keys_values[:, PW:]
    q, k, v, g = (item.reshape(-1, PH, HD) for item in (q, k, v, grad_out))
    scores = jnp.einsum("qhe,khe->hqk", q, k, preferred_element_type=f32) * 0.125
    probs = jnp.where(mask, jnp.exp(scores - log_total), 0.0)
    delta = jnp.sum((grad_out.astype(f32) * out).reshape(-1, PH, HD), -1).T[:, :, None]
    grad_probs = jnp.einsum("qhe,khe->hqk", g, v, preferred_element_type=f32)
    grad_scores = (probs * (grad_probs - delta)).astype(bf16)
    dq = 0.125 * jnp.einsum("hqk,khe->qhe", grad_scores, k, preferred_element_type=f32)
    dk = 0.125 * jnp.einsum("hqk,qhe->khe", grad_scores, q, preferred_element_type=f32)
    dv = jnp.einsum("hqk,qhe->khe", probs.astype(bf16), g, preferred_element_type=f32)
    dkv = jnp.concatenate([dk.reshape(-1, PW), dv.reshape(-1, PW)], 1)
    return dq.reshape(-1, PW), dkv


def share(own):
    return [own] + [swap(own, "p", k) for k in range(1, TP)]


def gather_sum(parts):
    total = parts[0]
    for k in range(1, TP):
        total = total + swap(parts[k].astype(bf16), "p", k).astype(f32)
    return total


def body(tokens, w_qkv, b_qv, w_proj, b_proj, ln1_gain, ln1_bias, ln2_gain, ln2_bias, w_fc, b_fc, w_out, b_out, d_out):
    size = {name: lax.axis_size(name) for name in ALL}
    devices = math.prod(size.values())
    copies = devices // TP
    blocks = devices // size["f"]
    rows = tokens.shape[1]
    shard = w_qkv.shape[1]
    ff = w_fc.shape[2]
    fs = ff // TP
    s, g, p, c = (lax.axis_index(name) for name in ("s", "g", "p", "c"))

    to_chip = []
    for e in range(copies):
        left, fi = divmod(e, size["f"])
        left, ci = divmod(left, size["c"])
        si, gi = divmod(left, size["g"])
        for q in range(TP):
            target = (((si * size["g"] + gi) * TP + q) * size["c"] + ci) * size["f"] + fi
            to_chip.append((q * copies + e, target))
    to_owner = [(b, a) for a, b in to_chip]

    def own_sequence(value):
        kept = lax.dynamic_index_in_dim(value, s, 0, keepdims=False)
        sent = lax.dynamic_index_in_dim(value, 1 - s, 0, keepdims=False)
        got = swap(sent, "s")
        return jnp.where(s == 0, jnp.stack([kept, got]), jnp.stack([got, kept])).reshape(-1, D)

    def back_to_blocks(value):
        value = value.reshape(2, rows, D)
        kept = lax.dynamic_index_in_dim(value, s, 0, keepdims=False)
        sent = lax.dynamic_index_in_dim(value, 1 - s, 0, keepdims=False)
        got = swap(sent, "s")
        return jnp.where(s == 0, jnp.stack([kept, got]), jnp.stack([got, kept]))

    def by_chip(pieces):
        sent = jnp.broadcast_to(
            pieces[None, None, :, None, None],
            (size["s"], size["g"], TP, size["c"], size["f"]) + pieces.shape[1:],
        ).reshape((devices,) + pieces.shape[1:])
        return lax.all_to_all(sent, ALL, 0, 0, tiled=True).reshape(devices * pieces.shape[1], -1)

    small = jnp.concatenate(
        [item.reshape(LAYERS, -1) for item in (b_proj, b_out, ln1_gain, ln1_bias, ln2_gain, ln2_bias, b_qv, b_fc)], 1
    )
    width = small.shape[1]
    small = jnp.broadcast_to(small.reshape(1, -1), (devices, LAYERS * width))
    small = lax.all_to_all(small, ALL, 0, 0, tiled=True).reshape(devices, LAYERS, width)

    qkv_cols = [
        w_qkv[l].reshape(shard, 3, TP, PW).transpose(2, 0, 1, 3).reshape(TP, shard, 3 * PW) for l in range(LAYERS)
    ]
    fc_cols = [w_fc[l].reshape(shard, TP, fs).transpose(1, 0, 2) for l in range(LAYERS)]
    wq = [None] * LAYERS
    wf = [None] * LAYERS
    wq[0] = by_chip(qkv_cols[0])
    x_own = own_sequence(tokens)
    x_all = jnp.concatenate(share(x_own), 0).astype(f32)
    wf[0] = by_chip(fc_cols[0])
    out_rows = lax.ppermute(w_out, ALL, to_chip)
    wo, wp = [], []
    for l in range(LAYERS):
        wp.append(lax.all_gather(w_proj[l], ALL, axis=0, tiled=True))
        wo.append(lax.all_gather(out_rows[l], REST, axis=0, tiled=True))
    for l in range(1, LAYERS):
        wq[l] = by_chip(qkv_cols[l])
        wf[l] = by_chip(fc_cols[l])

    def vector(l, start, count):
        return small[:, l, start : start + count].reshape(-1).astype(f32)

    vec = []
    for l in range(LAYERS):
        at = 0
        names = {}
        for name, count in (
            ("b_proj", shard), ("b_out", shard), ("g1", shard), ("s1", shard), ("g2", shard), ("s2", shard),
            ("b_qv", 2 * shard), ("b_fc", ff // devices),
        ):
            names[name] = vector(l, at, count)
            at += count
        zero = jnp.zeros((PW,), f32)
        names["b_qkv"] = jnp.concatenate(
            [
                lax.dynamic_slice_in_dim(names["b_qv"], p * PW, PW),
                zero,
                lax.dynamic_slice_in_dim(names["b_qv"], D + p * PW, PW),
            ]
        )
        names["b_up"] = lax.dynamic_slice_in_dim(names["b_fc"], p * fs, fs)
        vec.append(names)

    half = jnp.arange(2)[None, :, None]
    inside = jnp.arange(rows)[None, None, :]
    piece = jnp.arange(TP)[:, None, None]

    def positions(group, core):
        return (((group * TP + (p ^ piece)) * 2 + core + half * (blocks // 2)) * rows + inside).reshape(-1)

    q_pos = positions(g, c)
    k_pos = jnp.concatenate([positions(gi, core) for gi in range(size["g"]) for core in (0, 1)])
    mask = (k_pos[None, :] <= q_pos[:, None])[None]

    def all_keys(kv):
        other = swap(kv, "c")
        both = jnp.where(c == 0, jnp.stack([kv, other]), jnp.stack([other, kv])).reshape(-1, kv.shape[1])
        if size["g"] > 1:
            both = lax.all_gather(both, "g", axis=0, tiled=True)
        return both

    def own_keys_grad(dkv):
        if size["g"] > 1:
            dkv = lax.psum_scatter(dkv, "g", scatter_dimension=0, tiled=True)
        dkv = dkv.reshape(2, -1, dkv.shape[1])
        kept = lax.dynamic_index_in_dim(dkv, c, 0, keepdims=False)
        sent = lax.dynamic_index_in_dim(dkv, 1 - c, 0, keepdims=False)
        return kept + swap(sent.astype(bf16), "c").astype(f32)

    saved = []
    for l in range(LAYERS):
        v = vec[l]
        normed = norm_low(x_all, v["g1"], v["s1"])
        qkv = (dot(normed, wq[l]) + v["b_qkv"]).astype(bf16)
        kv = all_keys(qkv[:, PW:])
        out, log_total = attend(qkv, kv, mask)
        low = out.astype(bf16)
        heads = share(low.reshape(TP, -1, PW))
        heads = [jnp.stack([heads[k][m ^ k] for m in range(TP)]).reshape(-1, PW) for k in range(TP)]
        w_rows = [lax.dynamic_slice_in_dim(wp[l], (p ^ k) * PW, PW, 0) for k in range(TP)]
        proj = dot(jnp.concatenate(heads, 1), jnp.concatenate(w_rows, 0))
        mid = x_all + proj + v["b_proj"]
        normed2 = norm_low(mid, v["g2"], v["s2"])
        up = dot(normed2, wf[l]) + v["b_up"]
        act = gelu(up).astype(bf16)
        part = dot(act, wo[l]).reshape(TP, -1, D)
        mlp = gather_sum(part)
        saved.append((x_all, normed, qkv, kv, out, log_total, low, mid, normed2, up, act, w_rows[0]))
        if l + 1 < LAYERS:
            x_all = mid + jnp.concatenate(share(mlp.astype(bf16)), 0).astype(f32) + v["b_out"]
        else:
            tokens_out = mid[: mlp.shape[0]] + mlp + v["b_out"]
    own_rows = tokens_out.shape[0]
    output = back_to_blocks(tokens_out.astype(bf16))

    def send_columns(grad):
        got = lax.all_to_all(grad.astype(bf16).reshape(devices, shard, -1), ALL, 0, 0, tiled=True)
        got = got.reshape(size["s"], size["g"], TP, size["c"], size["f"], shard, -1).astype(f32)
        return jnp.sum(got, (0, 1, 3, 4))

    def send_rows(grad):
        got = lax.all_to_all(grad.astype(bf16).reshape(copies, -1, D), REST, 0, 0, tiled=True)
        return lax.ppermute(jnp.sum(got.astype(f32), 0), ALL, to_owner)

    grads = [None] * LAYERS
    small_grads = [None] * LAYERS
    g_own = own_sequence(d_out)
    g_all = jnp.concatenate(share(g_own), 0)
    g_own = g_own.astype(f32)
    for l in reversed(range(LAYERS)):
        v = vec[l]
        x_all, normed, qkv, kv, out, log_total, low, mid, normed2, up, act, wp_own = saved[l]
        d_b_out = jnp.sum(g_all[:own_rows].astype(f32), 0)
        d_wo = send_rows(dot(act, g_all, ((0,), (0,))))
        g_act = dot(g_all, wo[l], ((1,), (1,)))
        g_up = (gelu_slope(up) * g_act).astype(bf16)
        d_wf = send_columns(dot(normed2, g_up, ((0,), (0,))))
        d_b_fc = jnp.sum(g_up.astype(f32), 0)
        g_norm2 = gather_sum(dot(g_up, wf[l], ((1,), (1,))).reshape(TP, -1, D))
        g_mid, d_g2, d_s2 = norm_back(mid[:own_rows], v["g2"], g_norm2)
        g_mid = g_own + g_mid
        g_attn_own = g_mid.astype(bf16)
        g_attn = jnp.concatenate(share(g_attn_own), 0)
        d_b_proj = jnp.sum(g_attn_own.astype(f32), 0)
        d_wp = send_rows(dot(low, g_attn, ((0,), (0,))))
        g_out = dot(g_attn, wp_own, ((1,), (1,))).astype(bf16)
        dq, dkv = attend_back(qkv, kv, mask, out, log_total, g_out)
        dkv = own_keys_grad(dkv)
        g_qkv = jnp.concatenate([dq, dkv], 1).astype(bf16)
        d_wq = send_columns(dot(normed, g_qkv, ((0,), (0,))))
        d_b_qkv = jnp.sum(g_qkv.astype(f32), 0)
        g_norm = gather_sum(dot(g_qkv, wq[l], ((1,), (1,))).reshape(TP, -1, D))
        g_in, d_g1, d_s1 = norm_back(x_all[:own_rows], v["g1"], g_norm)
        g_own = g_mid + g_in
        if l > 0:
            g_all = jnp.concatenate(share(g_own.astype(bf16)), 0)
        grads[l] = (
            d_wq.reshape(TP, shard, 3, PW).transpose(1, 2, 0, 3).reshape(shard, 3 * D),
            d_wp,
            d_wf.transpose(1, 0, 2).reshape(shard, ff),
            d_wo,
        )
        whole_qv = lax.dynamic_update_slice_in_dim(jnp.zeros((2, D), f32), d_b_qkv.reshape(3, PW)[::2], p * PW, 1)
        whole_fc = lax.dynamic_update_slice_in_dim(jnp.zeros((ff,), f32), d_b_fc, p * fs, 0)
        small_grads[l] = [
            item.reshape(devices, -1)
            for item in (d_b_proj, d_b_out, d_g1, d_s1, d_g2, d_s2, whole_qv, whole_fc)
        ]
    grad_tokens = back_to_blocks(g_own)
    sent = jnp.concatenate([item for l in range(LAYERS) for item in small_grads[l]], 1)
    got = jnp.sum(lax.all_to_all(sent, ALL, 0, 0, tiled=True), 0).reshape(LAYERS, -1)
    parts = []
    at = 0
    for count in [shard] * 6 + [2 * shard, ff // devices]:
        parts.append(got[:, at : at + count])
        at += count
    d_b_proj, d_b_out, d_g1, d_s1, d_g2, d_s2, d_b_qv, d_b_fc = parts
    d_wq, d_wp, d_wf, d_wo = (jnp.stack([grads[l][i] for l in range(LAYERS)]) for i in range(4))
    return (output, grad_tokens, d_wq, d_b_qv, d_wp, d_b_proj, d_g1, d_s1, d_g2, d_s2, d_wf, d_b_fc, d_wo, d_b_out)


def solution(mesh):
    ctx, pair = mesh.shape["ctx"], mesh.shape["fsdp"]
    groups = ctx // (2 * TP * 2)
    view = Mesh(mesh.devices.reshape(2, groups, TP, 2, pair), ALL)
    along = ("s", "g", "p", "c")
    token = P("f", along, None)
    matrix = P(None, ALL, None)
    line = P(None, ALL)
    in_specs = (token, matrix, line, matrix, line, line, line, line, line, matrix, line, matrix, line, token)
    out_specs = (token, token, matrix, line, matrix, line, line, line, line, line, matrix, line, matrix, line)
    return jax.shard_map(body, mesh=view, in_specs=in_specs, out_specs=out_specs, check_vma=False)
```

time: 2090 us -> 705 us (0.34)
  the two profiles are of different devices: /device:TPU:0 before, /device:TPU:2 now
where the time goes in v1:
time: 705 us; the launch traced here: 696 us
  waiting for transfers between devices  256 us (36%)
  starting transfers between devices  144 us (20%)
  local copies, waits for them, and re-layouts  117 us (17%)
  matrix products  98.9 us (14%)
  other arithmetic  63.6 us (9%)
  between operations  16.4 us (2%)
    ppermute x50, waiting for transfers between devices, swap(): return lax.ppermute(value, axis, [(i, i ^ mask) for i in range(size)])  153 us
    ppermute x50, starting transfers between devices, swap(): return lax.ppermute(value, axis, [(i, i ^ mask) for i in range(size)])  66.2 us
    dot_general x24, matrix products, dot(): return lax.dot_general(a, b, (dims, ((), ())), preferred_element_type=f32)  58.4 us
    all_gather x2, waiting for transfers between devices, body(): wp.append(lax.all_gather(w_proj[l], ALL, axis=0, tiled=True))  33.7 us
    all_to_all x4, waiting for transfers between devices, send_rows(): lax.all_to_all(grad.astype(bf16).reshape(copies, -1, D), REST, 0, 0, tile...  29.4 us
    all_to_all x4, waiting for transfers between devices, send_columns(): lax.all_to_all(grad.astype(bf16).reshape(devices, shard, -1), ALL, 0, 0,...  21 us
    reshape x16, local copies, waits for them, and re-layouts, body(): item.reshape(devices, -1)  20.5 us
    concatenate x8, local copies, waits for them, and re-layouts, attend_back(): dkv = jnp.concatenate([dk.reshape(-1, PW), dv.reshape(-1, PW)], 1)  19.8 us
  transfers between devices with their start and end apart: 73, of which 40 were waited for; matrix products, arithmetic and copies ran while one was open for 32% of the time, Pallas kernels for 0%

profile of v1, /device:TPU:2, one launch (start us, length us, event | category | flops | bytes accessed | tf_op | source)
XLA Modules:
  0.0 695.8 jit_solution(10028496922805345212)
XLA Ops:
  13.3 7.3 %collective-permute-done.8 = bf16[2,96,768]{2,1,0:T(8,128)(2,1)S(1)} collective-permute-done((bf16[2,96,768]{2,1,0:T(8,128)(2,1)}, bf16[2,96,768]{2,1,0:T(8,128)(2,1)S(1)}, u32[]{:S(2)}, u32[]{:S(2)}) %collective-permute-start.8) | collective-permute-done | bytes 294944 | tf_op jit(solution)/shard_map/ppermute | solution.py:162
  22.3 8.4 %collective-permute-start = (bf16[64,768]{1,0:T(8,128)(2,1)S(1)}, bf16[64,768]{1,0:T(8,128)(2,1)S(1)}, u32[]{:S(2)}, u32[]{:S(2)}) collective-permute-start(bf16[64,768]{1,0:T(8,128)(2,1)S(1)} %get-tuple-element.143), channel_id=1, source_target_pairs={{0,16},{16,0},{1,17},{17,1},{2,18},{18,2},{3,19},{19,3},{4,20},{20... | collective-permute-start | bytes 294920 | tf_op jit(solution)/shard_map/ppermute | solution.py:30
  67.9 5.4 collective-permute-done.2
  73.3 6.0 collective-permute-done.3
  81.2 5.4 all-to-all-start.2
  103.5 10.4 %collective-permute-done.6 = bf16[4,128,192]{1,0,2:T(4,128)(2,1)S(1)} collective-permute-done((bf16[4,128,192]{1,0,2:T(4,128)(2,1)S(1)}, bf16[4,128,192]{1,0,2:T(4,128)(2,1)S(1)}, u32[]{:S(2)}, u32[]{:S(2)}) %collective-permute-start.6) | collective-permute-done | bytes 196640 | tf_op jit(solution)/shard_map/ppermute | solution.py:30
  115.1 5.3 collective-permute-done.7
  124.4 6.0 all-to-all-start.3
  140.4 33.7 %all-gather.13.cloned.1.call-done = bf16[1,768,768]{2,1,0:T(8,128)(2,1)} async-done(((bf16[1,24,768]{2,1,0:T(8,128)(2,1)}), bf16[1,768,768]{2,1,0:T(8,128)(2,1)}) %all-gather.13.cloned.1.call-update) | async-done | bytes 1179664 | tf_op jit(solution)/shard_map/all_gather | solution.py:165
  187.3 5.4 collective-permute-done.14
  217.0 8.0 %collective-permute-done.17 = bf16[4,128,192]{1,0,2:T(4,128)(2,1)S(1)} collective-permute-done((bf16[4,128,192]{1,0,2:T(4,128)(2,1)}, bf16[4,128,192]{1,0,2:T(4,128)(2,1)S(1)}, u32[]{:S(2)}, u32[]{:S(2)}) %collective-permute-start.17) | collective-permute-done | bytes 196640 | tf_op jit(solution)/shard_map/ppermute | solution.py:30
  282.7 5.5 fusion.28
  362.3 9.7 %collective-permute-done.41 = bf16[128,768]{1,0:T(8,128)(2,1)S(1)} collective-permute-done((bf16[128,768]{1,0:T(8,128)(2,1)S(1)}, bf16[128,768]{1,0:T(8,128)(2,1)S(1)}, u32[]{:S(2)}, u32[]{:S(2)}) %collective-permute-start.41) | collective-permute-done | bytes 196640 | tf_op jit(solution)/shard_map/ppermute | solution.py:30
  398.2 6.1 all-to-all-start.8
  404.3 7.0 %multiply_convert_fusion = bf16[3,512,1024]{2,1,0:T(8,128)(2,1)} fusion(f32[3,512,1024]{2,1,0:T(8,128)} %copy-done, f32[3,512]{1,0:T(4,128)} %bitcast.332, f32[3,512]{1,0:T(4,128)} %log_add_fusion, pred[512,1024]{1,0:T(8,128)(4,1)} %copy-done.6, bf16[512,3,64]{0,2,1:T(8,128)(2,1)} %bitcast.334, bf16[1024,3,64]{0,2,1:T(8,128)(2,1)} %bitcast.312), kind=kOutput, calls=%fused_computation | convolution fusion | flops 210763776 | bytes 10563584 | tf_op jit(solution)/shard_map/qhe,khe->hqk/dot_general | solution.py:84
  418.3 5.4 fusion.31
  498.8 5.7 all-to-all-start.7
  510.9 5.0 all-to-all-start.6
  519.4 21.0 %all-to-all-done.6 = bf16[32,24,576]{2,1,0:T(8,128)(2,1)S(1)} async-done(((bf16[32,24,576]{2,1,0:T(8,128)(2,1)}), bf16[32,24,576]{2,1,0:T(8,128)(2,1)S(1)}, u32[]{:S(2)}, u32[]{:S(2)}) %all-to-all-start.6) | async-done | bytes 884768 | tf_op jit(solution)/shard_map/all_to_all | solution.py:248
  548.1 26.1 %all-to-all-done.12 = bf16[8,96,768]{2,1,0:T(8,128)(2,1)S(1)} async-done(((bf16[8,96,768]{2,1,0:T(8,128)(2,1)}), bf16[8,96,768]{2,1,0:T(8,128)(2,1)S(1)}, u32[]{:S(2)}, u32[]{:S(2)}) %all-to-all-start.12) | async-done | bytes 1179680 | tf_op jit(solution)/shard_map/all_to_all | solution.py:253
  580.8 29.6 %collective-permute-done.22 = bf16[64,768]{1,0:T(8,128)(2,1)S(1)} collective-permute-done((bf16[64,768]{1,0:T(8,128)(2,1)S(1)}, bf16[64,768]{1,0:T(8,128)(2,1)S(1)}, u32[]{:S(2)}, u32[]{:S(2)}) %collective-permute-start.22) | collective-permute-done | bytes 98336 | tf_op jit(solution)/shard_map/ppermute | solution.py:30
  624.7 6.2 collective-permute-start.54
  646.2 21.6 %collective-permute-done.50 = f32[64,768]{1,0:T(8,128)} collective-permute-done((f32[64,768]{1,0:T(8,128)}, f32[64,768]{1,0:T(8,128)}, u32[]{:S(2)}, u32[]{:S(2)}) %collective-permute-start.50) | collective-permute-done | bytes 196640 | tf_op jit(solution)/shard_map/ppermute | solution.py:30
  675.5 9.0 %collective-permute-done.53 = f32[96,768]{1,0:T(8,128)S(1)} collective-permute-done((f32[96,768]{1,0:T(8,128)S(1)}, f32[96,768]{1,0:T(8,128)S(1)}, u32[]{:S(2)}, u32[]{:S(2)}) %collective-permute-start.53) | collective-permute-done | bytes 294944 | tf_op jit(solution)/shard_map/ppermute | solution.py:254
  (683 shorter events, 420.2 us)
Async XLA Ops:
  7.2 95.0 %all-gather.9.cloned.1.call-start = ((), (), s32[]{:S(2)}) async-start(), calls=%async_computation.14 | async-start | bytes 1216512 | tf_op jit(solution)/shard_map/all_gather | solution.py:165
  8.8 123.9 %all-gather.11.cloned.1.call-start = ((), (), s32[]{:S(2)}) async-start(), calls=%async_computation.15 | async-start | bytes 1327104 | tf_op jit(solution)/shard_map/all_gather | solution.py:166
  22.3 36.9 %collective-permute-start = (bf16[64,768]{1,0:T(8,128)(2,1)S(1)}, bf16[64,768]{1,0:T(8,128)(2,1)S(1)}, u32[]{:S(2)}, u32[]{:S(2)}) collective-permute-start(bf16[64,768]{1,0:T(8,128)(2,1)S(1)} %get-tuple-element.143), channel_id=1, source_target_pairs={{0,16},{16,0},{1,17},{17,1},{2,18},{18,2},{3,19},{19,3},{4,20},{20... | collective-permute-start | bytes 294920 | tf_op jit(solution)/shard_map/ppermute | solution.py:30
  37.0 137.1 %all-gather.13.cloned.1.call-start = ((), (), s32[]{:S(2)}) async-start(), calls=%async_computation.16 | async-start | bytes 1216512 | tf_op jit(solution)/shard_map/all_gather | solution.py:165
  44.6 35.4 %all-to-all-start.1 = ((bf16[32,24,576]{2,1,0:T(8,128)(2,1)}), bf16[32,24,576]{2,1,0:T(8,128)(2,1)S(1)}, u32[]{:S(2)}, u32[]{:S(2)}) async-start(bf16[32,24,576]{2,1,0:T(8,128)(2,1)} %bitcast.4), calls=%async_computation.1 | async-start | bytes 1966080 | tf_op jit(solution)/shard_map/all_to_all | solution.py:143
  48.8 191.3 %all-gather.15.cloned.1.call-start = ((), (), s32[]{:S(2)}) async-start(), calls=%async_computation.17 | async-start | bytes 1327104 | tf_op jit(solution)/shard_map/all_gather | solution.py:166
  64.3 175.8 %collective-permute-start.24 = (bf16[128,768]{1,0:T(8,128)(2,1)}, bf16[128,768]{1,0:T(8,128)(2,1)}, u32[]{:S(2)}, u32[]{:S(2)}) collective-permute-start(bf16[128,768]{1,0:T(8,128)(2,1)} %bitcast.54), channel_id=1, source_target_pairs={{0,4},{4,0},{8,12},{12,8},{1,5},{5,1},{9,13},{13,9},{2,6},{6,2},{1... | collective-permute-start | bytes 589832 | tf_op jit(solution)/shard_map/ppermute | solution.py:30
  64.7 175.4 %collective-permute-start.25 = (bf16[128,768]{1,0:T(8,128)(2,1)}, bf16[128,768]{1,0:T(8,128)(2,1)}, u32[]{:S(2)}, u32[]{:S(2)}) collective-permute-start(bf16[128,768]{1,0:T(8,128)(2,1)} %bitcast.54), channel_id=1, source_target_pairs={{0,8},{4,12},{8,0},{12,4},{1,9},{5,13},{9,1},{13,5},{2,10},{6,14},... | collective-permute-start | bytes 589832 | tf_op jit(solution)/shard_map/ppermute | solution.py:30
  81.2 41.5 %all-to-all-start.2 = ((bf16[32,24,768]{2,1,0:T(8,128)(2,1)}), bf16[32,24,768]{2,1,0:T(8,128)(2,1)}, u32[]{:S(2)}, u32[]{:S(2)}) async-start(bf16[32,24,768]{2,1,0:T(8,128)(2,1)} %bitcast.23), calls=%async_computation.2 | async-start | bytes 2359296 | tf_op jit(solution)/shard_map/all_to_all | solution.py:143
  124.4 69.1 %all-to-all-start.3 = ((bf16[32,24,576]{2,1,0:T(8,128)(2,1)}), bf16[32,24,576]{2,1,0:T(8,128)(2,1)}, u32[]{:S(2)}, u32[]{:S(2)}) async-start(bf16[32,24,576]{2,1,0:T(8,128)(2,1)} %bitcast.27), calls=%async_computation.3 | async-start | bytes 1966080 | tf_op jit(solution)/shard_map/all_to_all | solution.py:143
  136.8 39.7 %collective-permute-start.10 = (bf16[128,768]{1,0:T(8,128)(2,1)S(1)}, bf16[128,768]{1,0:T(8,128)(2,1)S(1)}, u32[]{:S(2)}, u32[]{:S(2)}) collective-permute-start(bf16[128,768]{1,0:T(8,128)(2,1)S(1)} %get-tuple-element.91), channel_id=1, source_target_pairs={{0,8},{4,12},{8,0},{12,4},{1,9},{5,13},{9,1},{13,5},{2,10},{6,14},... | collective-permute-start | bytes 589832 | tf_op jit(solution)/shard_map/ppermute | solution.py:30
  138.4 38.2 %collective-permute-start.11 = (bf16[128,768]{1,0:T(8,128)(2,1)S(1)}, bf16[128,768]{1,0:T(8,128)(2,1)S(1)}, u32[]{:S(2)}, u32[]{:S(2)}) collective-permute-start(bf16[128,768]{1,0:T(8,128)(2,1)S(1)} %get-tuple-element.90), channel_id=1, source_target_pairs={{0,12},{4,8},{8,4},{12,0},{1,13},{5,9},{9,5},{13,1},{2,14},{6,10},... | collective-permute-start | bytes 589832 | tf_op jit(solution)/shard_map/ppermute | solution.py:30
  138.5 38.0 %collective-permute-start.9 = (bf16[128,768]{1,0:T(8,128)(2,1)S(1)}, bf16[128,768]{1,0:T(8,128)(2,1)S(1)}, u32[]{:S(2)}, u32[]{:S(2)}) collective-permute-start(bf16[128,768]{1,0:T(8,128)(2,1)S(1)} %get-tuple-element.89), channel_id=1, source_target_pairs={{0,4},{4,0},{8,12},{12,8},{1,5},{5,1},{9,13},{13,9},{2,6},{6,2},{1... | collective-permute-start | bytes 589832 | tf_op jit(solution)/shard_map/ppermute | solution.py:30
  184.8 55.3 %collective-permute-start.26 = (bf16[128,768]{1,0:T(8,128)(2,1)}, bf16[128,768]{1,0:T(8,128)(2,1)}, u32[]{:S(2)}, u32[]{:S(2)}) collective-permute-start(bf16[128,768]{1,0:T(8,128)(2,1)} %bitcast.54), channel_id=1, source_target_pairs={{0,12},{4,8},{8,4},{12,0},{1,13},{5,9},{9,5},{13,1},{2,14},{6,10},... | collective-permute-start | bytes 589832 | tf_op jit(solution)/shard_map/ppermute | solution.py:30
  195.3 40.6 %all-to-all-start.4 = ((bf16[32,24,768]{2,1,0:T(8,128)(2,1)}), bf16[32,24,768]{2,1,0:T(8,128)(2,1)}, u32[]{:S(2)}, u32[]{:S(2)}) async-start(bf16[32,24,768]{2,1,0:T(8,128)(2,1)} %bitcast.46), calls=%async_computation.4 | async-start | bytes 2359296 | tf_op jit(solution)/shard_map/all_to_all | solution.py:143
  349.5 48.8 %all-to-all-start.13 = ((bf16[8,96,768]{2,1,0:T(8,128)(2,1)}), bf16[8,96,768]{2,1,0:T(8,128)(2,1)}, u32[]{:S(2)}, u32[]{:S(2)}) async-start(bf16[8,96,768]{2,1,0:T(8,128)(2,1)} %bitcast.293), calls=%async_computation.13 | async-start | bytes 2359296 | tf_op jit(solution)/shard_map/all_to_all | solution.py:253
  414.6 84.3 %all-to-all-start.11 = ((bf16[32,24,768]{2,1,0:T(8,128)(2,1)}), bf16[32,24,768]{2,1,0:T(8,128)(2,1)}, u32[]{:S(2)}, u32[]{:S(2)}) async-start(bf16[32,24,768]{2,1,0:T(8,128)(2,1)} %bitcast.292), calls=%async_computation.11 | async-start | bytes 2359296 | tf_op jit(solution)/shard_map/all_to_all | solution.py:248
  451.0 39.0 %collective-permute-start.47 = (bf16[128,768]{1,0:T(8,128)(2,1)}, bf16[128,768]{1,0:T(8,128)(2,1)}, u32[]{:S(2)}, u32[]{:S(2)}) collective-permute-start(bf16[128,768]{1,0:T(8,128)(2,1)} %get-tuple-element.72), channel_id=1, source_target_pairs={{0,4},{4,0},{8,12},{12,8},{1,5},{5,1},{9,13},{13,9},{2,6},{6,2},{1... | collective-permute-start | bytes 589832 | tf_op jit(solution)/shard_map/ppermute | solution.py:30
  451.4 38.6 %collective-permute-start.48 = (bf16[128,768]{1,0:T(8,128)(2,1)}, bf16[128,768]{1,0:T(8,128)(2,1)}, u32[]{:S(2)}, u32[]{:S(2)}) collective-permute-start(bf16[128,768]{1,0:T(8,128)(2,1)} %get-tuple-element.74), channel_id=1, source_target_pairs={{0,8},{4,12},{8,0},{12,4},{1,9},{5,13},{9,1},{13,5},{2,10},{6,14},... | collective-permute-start | bytes 589832 | tf_op jit(solution)/shard_map/ppermute | solution.py:30
  453.1 36.9 %collective-permute-start.49 = (bf16[128,768]{1,0:T(8,128)(2,1)}, bf16[128,768]{1,0:T(8,128)(2,1)}, u32[]{:S(2)}, u32[]{:S(2)}) collective-permute-start(bf16[128,768]{1,0:T(8,128)(2,1)} %get-tuple-element.73), channel_id=1, source_target_pairs={{0,12},{4,8},{8,4},{12,0},{1,13},{5,9},{9,5},{13,1},{2,14},{6,10},... | collective-permute-start | bytes 589832 | tf_op jit(solution)/shard_map/ppermute | solution.py:30
  541.3 32.9 %all-to-all-start.12 = ((bf16[8,96,768]{2,1,0:T(8,128)(2,1)}), bf16[8,96,768]{2,1,0:T(8,128)(2,1)S(1)}, u32[]{:S(2)}, u32[]{:S(2)}) async-start(bf16[8,96,768]{2,1,0:T(8,128)(2,1)} %bitcast.295), calls=%async_computation.12 | async-start | bytes 2359296 | tf_op jit(solution)/shard_map/all_to_all | solution.py:253
  574.2 57.4 %all-to-all-start.10 = ((bf16[32,24,768]{2,1,0:T(8,128)(2,1)}), bf16[32,24,768]{2,1,0:T(8,128)(2,1)S(1)}, u32[]{:S(2)}, u32[]{:S(2)}) async-start(bf16[32,24,768]{2,1,0:T(8,128)(2,1)} %bitcast.294), calls=%async_computation.10 | async-start | bytes 2359296 | tf_op jit(solution)/shard_map/all_to_all | solution.py:248
  624.7 50.8 %collective-permute-start.54 = (f32[96,768]{1,0:T(8,128)}, f32[96,768]{1,0:T(8,128)}, u32[]{:S(2)}, u32[]{:S(2)}) collective-permute-start(f32[96,768]{1,0:T(8,128)} %convert_reduce_fusion.2), channel_id=1, source_target_pairs={{0,0},{4,8},{8,16},{12,24},{1,1},{5,9},{9,17},{13,25},{2,2},{6,10}... | collective-permute-start | bytes 884744 | tf_op jit(solution)/shard_map/ppermute | solution.py:254
  631.6 54.7 %all-to-all-start.5 = ((bf16[32,24,576]{2,1,0:T(8,128)(2,1)}), bf16[32,24,576]{2,1,0:T(8,128)(2,1)}, u32[]{:S(2)}, u32[]{:S(2)}) async-start(bf16[32,24,576]{2,1,0:T(8,128)(2,1)} %bitcast.78), calls=%async_computation.5 | async-start | bytes 1966080 | tf_op jit(solution)/shard_map/all_to_all | solution.py:248
  (185 other events, 2160.3 us)
Sparse Core Ops, SparseCore 0:
  10.9 61.0 all-gather.8
  74.5 41.2 all-gather.10
  119.3 54.7 all-gather.12
  175.8 29.2 all-gather.14

commit v2 on v1

v2 whole, which is shorter than its diff:
```python
import functools
import math

import jax
import jax.numpy as jnp
from jax import lax
from jax.experimental import pallas as pl
from jax.experimental.pallas import tpu as pltpu
from jax.sharding import Mesh, PartitionSpec as P

D = 768
H = 12
HD = 64
LAYERS = 2
TP = 4
PH = H // TP
PW = PH * HD
EPS = 1e-05
ROOT = math.sqrt(2.0 / math.pi)
bf16 = jnp.bfloat16
f32 = jnp.float32

ALL = ("h", "g", "x", "c", "f")
COPIES = ("h", "g")
SLOTS = 12


def dot(a, b, dims=((1,), (0,)), precision=None):
    return lax.dot_general(a, b, (dims, ((), ())), preferred_element_type=f32, precision=precision)


NT = ((1,), (1,))
TN = ((0,), (0,))


def swap(value, axis, mask=1):
    names = (axis,) if isinstance(axis, str) else axis
    size = math.prod(lax.axis_size(name) for name in names)
    return lax.ppermute(value, axis, [(i, i ^ mask) for i in range(size)])


def chip_swap(value, mask):
    return swap(value, ("x", "f"), mask % 2 * 2 + mask // 2)


def share(own):
    return [own] + [chip_swap(own, k) for k in range(1, TP)]


def launch(kernel, name, outs, scalars, *args, scratch=(), flops=0):
    shapes = [jax.ShapeDtypeStruct(shape, kind) for shape, kind in outs]
    moved = sum(a.size * a.dtype.itemsize for a in args) + sum(math.prod(o.shape) * o.dtype.itemsize for o in shapes)
    return pl.pallas_call(
        kernel,
        name=name,
        out_shape=shapes,
        in_specs=[pl.BlockSpec(memory_space=pltpu.SMEM)] + [pl.BlockSpec(memory_space=pltpu.VMEM)] * len(args),
        out_specs=[pl.BlockSpec(memory_space=pltpu.VMEM)] * len(shapes),
        scratch_shapes=list(scratch),
        cost_estimate=pl.CostEstimate(flops=flops, bytes_accessed=moved, transcendentals=0),
        compiler_params=pltpu.CompilerParams(vmem_limit_bytes=56 * 1024 * 1024),
    )(scalars, *args)


def unit_rows(values):
    center = values - jnp.mean(values, -1, keepdims=True)
    scale = lax.rsqrt(jnp.mean(center * center, -1, keepdims=True) + EPS)
    return center * scale, scale


def interleave(shard):
    block = D // 2
    per = block // (TP * shard)
    row = lax.broadcasted_iota(jnp.int32, (block, block), 0)
    col = lax.broadcasted_iota(jnp.int32, (block, block), 1)
    chip, rest = lax.div(row, per * shard), lax.rem(row, per * shard)
    target = lax.div(rest, shard) * (TP * shard) + chip * shard + lax.rem(rest, shard)
    return (col == target).astype(bf16)


def first_pieces_kernel(where, w_qkv, *refs):
    small, outs, (lines, cols) = refs[:8], refs[8 : 8 + TP], refs[8 + TP :]
    p = where[1]
    shard = cols.shape[1]
    lines[...] = jnp.zeros_like(lines)
    at = 0
    for l in range(LAYERS):
        for item in small:
            for first in range(0, item.shape[1], shard):
                lines[at : at + 1, :shard] = item[l : l + 1, first : first + shard].astype(f32)
                at += 1
    columns = lines[...].T[:shard, :HD]
    for q in range(TP):
        parts = [w_qkv[0, :, j * D + q * PW : j * D + (q + 1) * PW].astype(f32) for j in range(3)]
        cols[q] = jnp.concatenate(parts + [columns], 1).astype(bf16)
    for k, out in enumerate(outs):
        out[...] = cols[jnp.bitwise_xor(p, k)]


def layer_pieces_kernel(layer, qkv):
    def kernel(where, w_fc, w_out, w_proj, w_qkv, *refs):
        outs, (cols,) = refs[:TP], refs[TP:]
        p = where[1]
        shard = w_proj.shape[1]
        block = D // 2
        order = interleave(shard)
        fc = [dot(w_fc[layer, :, b * block : (b + 1) * block], order, NT) for b in range(w_fc.shape[2] // block)]
        for q in range(TP):
            lanes = slice(q * block // TP, (q + 1) * block // TP)
            cols[q, :, :D] = jnp.concatenate([item[:, lanes] for item in fc], 1).astype(bf16)
            if qkv is not None:
                parts = [w_qkv[qkv, :, j * D + q * PW : j * D + (q + 1) * PW] for j in range(3)]
                cols[q, :, D:] = jnp.concatenate(parts, 1)
        for k, out in enumerate(outs):
            q = jnp.bitwise_xor(p, k)
            out[:, :D] = cols[q, :, :D]
            out[:, D : 2 * D] = w_out[layer, q]
            out[:, 2 * D : 3 * D] = w_proj[layer]
            if qkv is not None:
                out[:, 3 * D :] = cols[q, :, D:]

    return kernel


def arrange_first_kernel(sizes):
    def kernel(where, got, w_out, table, columns, blocks):
        p, c = where[1], where[2]
        devices, shard = w_out.shape[:2]
        groups = sizes["g"]
        columns[...] = jnp.zeros_like(columns)
        for d in range(devices):
            rest, fi = divmod(d, 2)
            rest, ci = divmod(rest, 2)
            rest, xi = divmod(rest, 2)
            copy = jnp.bitwise_xor(c, ci) * sizes["h"] * groups + rest
            one = got[copy * TP + jnp.bitwise_xor(p, 2 * fi + xi)].astype(f32)
            w_out[d] = one[:, : 3 * PW].astype(bf16)
            columns[d * shard : (d + 1) * shard, :HD] = one[:, 3 * PW :]
            blocks[d] = one[:, 3 * PW :]
        lines = columns[...].T
        per = PW // (2 * shard)
        for l in range(LAYERS):
            base = SLOTS * l
            table[8 * l : 8 * l + 6, :] = lines[base : base + 6]
            parts = []
            for first in (0, devices // 2):
                for j in range(per):
                    block = blocks[first + p * per + j]
                    parts += [block[:, base + 6 : base + 7], block[:, base + 7 : base + 8]]
                if first == 0:
                    parts.append(jnp.zeros((PW, 1), f32))
            parts.append(jnp.zeros((D - 3 * PW, 1), f32))
            bias = jnp.broadcast_to(jnp.concatenate(parts, 0), (D, 128)).T
            table[8 * l + 6 : 8 * l + 7, :] = bias[0:1]
            row = lines[base + 8 : base + 9]
            for q in range(1, TP):
                row = jnp.where(p == q, lines[base + 8 + q : base + 9 + q], row)
            table[8 * l + 7 : 8 * l + 8, :] = row

    return kernel


def finish_feed_kernel(where, *refs):
    pieces, (wf_out, wo_out, cols) = refs[: LAYERS * TP], refs[LAYERS * TP :]
    p = where[1]
    shard = wf_out.shape[1]
    block = D // 2
    order = interleave(shard)
    for l in range(LAYERS):
        for k in range(TP):
            cols[jnp.bitwise_xor(p, k)] = pieces[l * TP + k][...]
        fc = [cols[q, :, :D].astype(f32) for q in range(TP)]
        for b in range(wf_out.shape[2] // block):
            lanes = slice(b * block // TP, (b + 1) * block // TP)
            joined = jnp.concatenate([item[:, lanes] for item in fc], 1).astype(bf16)
            wf_out[l, :, b * block : (b + 1) * block] = dot(joined, order)
        for q in range(TP):
            wo_out[l, q] = cols[q, :, D:].astype(f32)


def finish_mixed_kernel(where, last, m0, m1, m2, m3, wq_out, wp_out, *refs):
    small_outs, (cols, square) = refs[:8], refs[8:]
    p = where[1]
    shard = wq_out.shape[1]
    columns = jnp.zeros((shard, 128), f32)
    for q in range(TP):
        total = jnp.zeros((shard, D + 128), f32)
        for copy in range(last.shape[0] // TP):
            total = total + last[(copy * 2 + q % 2) * 2 + q // 2].astype(f32)
        columns = columns + total[:, D:]
        cols[0, q] = total[:, :D]
    for k, m in enumerate((m0, m1, m2, m3)):
        cols[1, jnp.bitwise_xor(p, k)] = m[...].astype(f32)
    for l in range(LAYERS):
        for j in range(3):
            wq_out[l, :, j * D : (j + 1) * D] = jnp.concatenate(
                [cols[l, q, :, j * PW : (j + 1) * PW] for q in range(TP)], 1
            )
        wp_out[l] = jnp.concatenate([cols[l, q, :, 3 * PW :] for q in range(TP)], 1)
    square[...] = jnp.zeros_like(square)
    square[:shard, :] = columns
    lines = square[...].T
    at = 0
    for l in range(LAYERS):
        for out in small_outs:
            for first in range(0, out.shape[1], shard):
                out[l : l + 1, first : first + shard] = lines[at : at + 1, :shard]
                at += 1


def enter_kernel(first, index):
    def kernel(where, table, wq, *refs):
        *inputs, x_out, xo_out, n_out, q_out, kv_out = refs
        if not first:
            mid, *inputs = inputs
        t = table
        gain, shift, bias = (t[8 * index + i : 8 * index + i + 1, :] for i in (2, 3, 6))
        rows = n_out.shape[0] // TP
        for k in range(TP):
            at = slice(k * rows, (k + 1) * rows)
            x = inputs[k][...].astype(f32)
            if not first:
                x = mid[at, :] + x + t[8 * (index - 1) + 1 : 8 * (index - 1) + 2, :]
            x_out[at, :] = x
            if k == 0:
                xo_out[...] = x
            unit, _ = unit_rows(x)
            n_out[at, :] = (unit * gain + shift).astype(bf16)
        got = (dot(n_out[...], wq[...]) + bias[:, : 3 * PW]).astype(bf16)
        q_out[...] = got[:, :PW]
        kv_out[...] = got[:, PW:]

    return kernel


def tile_rows(p, t, size):
    return pl.multiple_of((jnp.bitwise_xor(t % TP, p) * 2 + t // TP) * size, size)


def masks(c, chunk, size):
    a = lax.broadcasted_iota(jnp.int32, (chunk, chunk), 0)
    b = lax.broadcasted_iota(jnp.int32, (chunk, chunk), 1)
    return b <= a, lax.div(b, size) < lax.div(a, size) + c


def attend_kernel(where, q_ref, own_ref, oth_ref, out_ref, lse_ref, qn, kn, on, outn):
    p, c = where[1], where[2]
    count = q_ref.shape[0]
    size = count // (2 * TP)
    chunk = 2 * size
    for t in range(2 * TP):
        at = pl.ds(tile_rows(p, t, size), size)
        here = slice(t * size, (t + 1) * size)
        qn[here, :] = q_ref[at, :]
        kn[here, :] = own_ref[at, :]
        on[here, :] = oth_ref[at, :]
    ok_own, ok_oth = masks(c, chunk, size)
    for j in range(count // chunk):
        rows = slice(j * chunk, (j + 1) * chunk)
        outs = []
        for h in range(PH):
            lanes = slice(h * HD, (h + 1) * HD)
            vlanes = slice(PW + h * HD, PW + (h + 1) * HD)
            q = qn[rows, lanes]
            scores = []
            for keys, ok in ((kn, ok_own), (on, ok_oth)):
                if j > 0:
                    scores.append(dot(q, keys[: j * chunk, lanes], NT) * 0.125)
                scores.append(jnp.where(ok, dot(q, keys[rows, lanes], NT) * 0.125, -1e30))
            top = functools.reduce(jnp.maximum, [jnp.max(v, -1, keepdims=True) for v in scores])
            weights = [jnp.exp(v - top) for v in scores]
            total = sum(jnp.sum(v, -1, keepdims=True) for v in weights)
            low = [v.astype(bf16) for v in weights]
            out = jnp.zeros((chunk, HD), f32)
            for i, keys in enumerate((kn, on)):
                if j > 0:
                    out = out + dot(low[2 * i], keys[: j * chunk, vlanes])
                    out = out + dot(low[2 * i + 1], keys[rows, vlanes])
                else:
                    out = out + dot(low[i], keys[rows, vlanes])
            outs.append(out / total)
            lse_ref[rows, h : h + 1] = top + jnp.log(total)
        outn[rows, :] = jnp.concatenate(outs, 1).astype(bf16)
    for t in range(2 * TP):
        out_ref[pl.ds(tile_rows(p, t, size), size), :] = outn[t * size : (t + 1) * size, :]


def middle_kernel(index):
    def kernel(where, table, x, o0, o1, o2, o3, wp, wf, wo, mid_out, mo_out, heads_out, n_out, up_out, act_out, y0, y1, y2, y3, got):
        p = where[1]
        t = table
        b_proj, gain, shift, b_up = (t[8 * index + i : 8 * index + i + 1, :] for i in (0, 4, 5, 7))
        rows = x.shape[0] // TP
        for k, o in enumerate((o0, o1, o2, o3)):
            for m in range(TP):
                got[k, m * rows : (m + 1) * rows, :] = o[(m ^ k) * rows : ((m ^ k) + 1) * rows, :]
        heads_out[...] = jnp.concatenate([got[jnp.bitwise_xor(p, q)] for q in range(TP)], 1)
        for m, y in enumerate((y0, y1, y2, y3)):
            at = slice(m * rows, (m + 1) * rows)
            mid = x[at, :] + dot(heads_out[at, :], wp[...]) + b_proj
            mid_out[at, :] = mid
            if m == 0:
                mo_out[...] = mid
            unit, _ = unit_rows(mid)
            n_out[at, :] = (unit * gain + shift).astype(bf16)
        up = dot(n_out[...], wf[...]) + b_up
        up_out[...] = up
        act_out[...] = (0.5 * up * (1.0 + jnp.tanh(ROOT * (up + 0.044715 * up * up * up)))).astype(bf16)
        for m, y in enumerate((y0, y1, y2, y3)):
            at = slice(m * rows, (m + 1) * rows)
            y[...] = dot(act_out[at, :], wo[...]).astype(y.dtype)

    return kernel


def part_sums(part, unit, acc):
    acc[0:1, :] += jnp.sum(part * unit, 0, keepdims=True)
    acc[1:2, :] += jnp.sum(part, 0, keepdims=True)


def feed_back_kernel(where, g0, g1, g2, g3, up, mid, wo, wf, g_out, gu_out, bfc_out, sums_out, y0, y1, y2, y3):
    rows = g0.shape[0]
    for k, g in enumerate((g0, g1, g2, g3)):
        g_out[k * rows : (k + 1) * rows, :] = g[...]
    bfc_out[...] = jnp.zeros_like(bfc_out)
    sums_out[...] = jnp.zeros_like(sums_out)
    for k, y in enumerate((y0, y1, y2, y3)):
        at = slice(k * rows, (k + 1) * rows)
        g_act = dot(g_out[at, :], wo[...], NT)
        u = up[at, :]
        t = jnp.tanh(ROOT * (u + 0.044715 * u * u * u))
        slope = 0.5 * (1.0 + t) + 0.5 * u * (1.0 - t * t) * (ROOT * (1.0 + 3 * 0.044715 * u * u))
        g_up = (slope * g_act).astype(bf16)
        gu_out[at, :] = g_up
        bfc_out[0:1, :] += jnp.sum(g_up.astype(f32), 0, keepdims=True)
        part = dot(g_up, wf[...], NT)
        y[...] = part.astype(y.dtype)
        unit, _ = unit_rows(mid[at, :])
        part_sums(part, unit, sums_out)


def norm_back_kernel(index, which):
    def kernel(where, table, grad, value, r0, r1, r2, r3, g_out, low_out, sum_out):
        gain = table[8 * index + which : 8 * index + which + 1, :]
        cot = r0[...] + r1[...].astype(f32) + r2[...].astype(f32) + r3[...].astype(f32)
        unit, scale = unit_rows(value[...])
        inner = cot * gain
        moved = scale * (
            inner - jnp.mean(inner, -1, keepdims=True) - unit * jnp.mean(inner * unit, -1, keepdims=True)
        )
        total = grad[...].astype(f32) + moved
        g_out[...] = total
        low = total.astype(bf16)
        low_out[...] = low
        sum_out[...] = jnp.zeros_like(sum_out)
        sum_out[0:1, :] = jnp.sum(low.astype(f32), 0, keepdims=True)

    return kernel


def attend_back_kernel(where, g0, g1, g2, g3, wp, q_ref, own_ref, oth_ref, lse_ref, ga_out, dq_ref, down_ref, doth_ref, local, gn, qn, kn, on, dqn, dkn, don):
    p, c = where[1], where[2]
    count = q_ref.shape[0]
    size = count // (2 * TP)
    chunk = 2 * size
    rows_of = g0.shape[0]
    for k, g in enumerate((g0, g1, g2, g3)):
        ga_out[k * rows_of : (k + 1) * rows_of, :] = g[...]
    mine = wp[pl.ds(pl.multiple_of(p * PW, PW), PW), :]
    local[...] = dot(ga_out[...], mine, NT)
    for t in range(2 * TP):
        at = pl.ds(tile_rows(p, t, size), size)
        here = slice(t * size, (t + 1) * size)
        gn[here, :] = local[at, :].astype(bf16)
        qn[here, :] = q_ref[at, :]
        kn[here, :] = own_ref[at, :]
        on[here, :] = oth_ref[at, :]
    dkn[...] = jnp.zeros_like(dkn)
    don[...] = jnp.zeros_like(don)
    ok_own, ok_oth = masks(c, chunk, size)
    for j in range(count // chunk):
        rows = slice(j * chunk, (j + 1) * chunk)
        dqs = []
        for h in range(PH):
            lanes = slice(h * HD, (h + 1) * HD)
            vlanes = slice(PW + h * HD, PW + (h + 1) * HD)
            q, g = qn[rows, lanes], gn[rows, lanes]
            lse = lse_ref[rows, h : h + 1]
            work = []
            for keys, sums, ok in ((kn, dkn, ok_own), (on, don, ok_oth)):
                if j > 0:
                    work.append((keys, sums, slice(0, j * chunk), None))
                work.append((keys, sums, rows, ok))
            probs, grads = [], []
            delta = jnp.zeros((chunk, 1), f32)
            for keys, sums, span, ok in work:
                scores = dot(q, keys[span, lanes], NT) * 0.125 - lse
                if ok is not None:
                    scores = jnp.where(ok, scores, -1e30)
                prob = jnp.exp(scores)
                grad = dot(g, keys[span, vlanes], NT)
                delta = delta + jnp.sum(prob * grad, -1, keepdims=True)
                probs.append(prob)
                grads.append(grad)
            dq = jnp.zeros((chunk, HD), f32)
            for (keys, sums, span, ok), prob, grad in zip(work, probs, grads):
                ds = (prob * (grad - delta)).astype(bf16)
                dq = dq + dot(ds, keys[span, lanes])
                sums[span, lanes] += 0.125 * dot(ds, q, TN)
                sums[span, vlanes] += dot(prob.astype(bf16), g, TN)
            dqs.append(0.125 * dq)
        dqn[rows, :] = jnp.concatenate(dqs, 1)
    for t in range(2 * TP):
        at = pl.ds(tile_rows(p, t, size), size)
        here = slice(t * size, (t + 1) * size)
        dq_ref[at, :] = dqn[here, :].astype(bf16)
        down_ref[at, :] = dkn[here, :]
        doth_ref[at, :] = don[here, :].astype(bf16)


def leave_kernel(where, dq, dkv, more, wq, x, gq_out, bq_out, sums_out, y0, y1, y2, y3):
    gq_out[:, :PW] = dq[...]
    gq_out[:, PW:] = (dkv[...] + more[...].astype(f32)).astype(bf16)
    bq_out[...] = jnp.zeros_like(bq_out)
    bq_out[0:1, : 3 * PW] = jnp.sum(gq_out[...].astype(f32), 0, keepdims=True)
    sums_out[...] = jnp.zeros_like(sums_out)
    rows = x.shape[0] // TP
    for k, y in enumerate((y0, y1, y2, y3)):
        at = slice(k * rows, (k + 1) * rows)
        part = dot(gq_out[at, :], wq[...], NT)
        y[...] = part.astype(y.dtype)
        unit, _ = unit_rows(x[at, :])
        part_sums(part, unit, sums_out)


def arrange_kernel(widths):
    def kernel(where, own, oth, *outs):
        p, c = where[1], where[2]
        devices = outs[0].shape[0]

        def one(d, carry):
            core = lax.rem(lax.div(d, 2), 2)
            chip = lax.rem(d, 2) * 2 + lax.rem(lax.div(d, 4), 2)
            block = lax.div(d, 8) * TP + jnp.bitwise_xor(chip, p)
            for source, here in ((own, core == c), (oth, core != c)):

                @pl.when(here)
                def _():
                    at = 0
                    for out, width in zip(outs, widths):
                        out[d] = source[block, :, at : at + width]
                        at += width

            return carry

        lax.fori_loop(0, devices, one, 0)

    return kernel


def scatter_blocks(where, blocks, keep, give):
    p, c = where[1], where[2]
    for i in range(keep.shape[0]):
        copy, k = divmod(i, TP)
        chip = jnp.bitwise_xor(p, k)
        for out, core in ((keep, c), (give, 1 - c)):
            out[i] = blocks[((copy * 2 + lax.rem(chip, 2)) * 2 + core) * 2 + lax.div(chip, 2)]


def feed_weights_kernel(where, act, g, normed, g_up, keep, give, blocks):
    width = normed.shape[1]
    shard = keep.shape[1]
    for at, (a, b) in ((0, (normed, g_up)), (width, (act, g))):
        value = dot(a[...], b[...], TN)
        for d in range(blocks.shape[0]):
            blocks[d, :, at : at + width] = value[d * shard : (d + 1) * shard].astype(bf16)
    scatter_blocks(where, blocks, keep, give)


def mixed_weights(where, normed, g_qkv, heads, g_attn):
    p = where[1]
    value = dot(normed[...], g_qkv[...], TN)
    whole = dot(heads[...], g_attn[...], TN)
    mine = whole[:, :PW]
    for q in range(1, TP):
        mine = jnp.where(p == q, whole[:, q * PW : (q + 1) * PW], mine)
    return jnp.concatenate([value, mine], 1)


def mixed_weights_kernel(where, normed, g_qkv, heads, g_attn, keep, give, blocks):
    value = mixed_weights(where, normed, g_qkv, heads, g_attn)
    shard = blocks.shape[1]
    for d in range(blocks.shape[0]):
        blocks[d] = value[d * shard : (d + 1) * shard].astype(bf16)
    scatter_blocks(where, blocks, keep, give)


def last_weights_kernel(where, normed, g_qkv, heads, g_attn, *refs):
    sums, (keep, give, blocks, lines, more) = refs[: 6 * LAYERS], refs[6 * LAYERS :]
    p, c = where[1], where[2]
    devices, shard = blocks.shape[:2]
    per = PW // (2 * shard)
    lines[...] = jnp.zeros_like(lines)
    more[...] = jnp.zeros_like(more)
    for l in range(LAYERS):
        b_proj, b_out, norm1, norm2, qkv, fc = sums[6 * l : 6 * l + 6]
        base = SLOTS * l
        rows = (b_proj[0:1, :], b_out[0:1, :], norm1[0:1, :], norm1[1:2, :], norm2[0:1, :], norm2[1:2, :])
        for i, row in enumerate(rows):
            lines[base + i : base + i + 1, :] = row
        for q in range(TP):
            lines[base + 8 + q : base + 9 + q, :] = jnp.where(p == q, fc[0:1, :], 0.0)
        bias = jnp.broadcast_to(qkv[0:1, :], (128, D)).T
        for first, start in ((0, 0), (devices // 2, 2 * PW)):
            for j in range(2 * per):
                lane = base + 6 + j % 2
                more[first + p * per + j // 2, :, lane : lane + 1] = bias[
                    start + j * shard : start + (j + 1) * shard, 0:1
                ]
    columns = lines[...].T
    value = mixed_weights(where, normed, g_qkv, heads, g_attn)
    for d in range(devices):
        at = slice(d * shard, (d + 1) * shard)
        blocks[d] = jnp.concatenate([value[at], columns[at] + more[d]], 1).astype(bf16)
    for i in range(keep.shape[0]):
        rest, f = divmod(i, 2)
        keep[i] = blocks[(rest * 2 + c) * 2 + f]
        give[i] = blocks[(rest * 2 + 1 - c) * 2 + f]


def attend(q, keys_values, mask):
    k, v = keys_values[:, :PW], keys_values[:, PW:]
    q, k, v = (item.reshape(-1, PH, HD) for item in (q, k, v))
    scores = jnp.einsum("qhe,khe->hqk", q, k, preferred_element_type=f32) * 0.125
    scores = jnp.where(mask, scores, -1e30)
    top = jnp.max(scores, -1, keepdims=True)
    weights = jnp.exp(scores - top)
    total = jnp.sum(weights, -1, keepdims=True)
    out = jnp.einsum("hqk,khe->qhe", (weights / total).astype(bf16), v, preferred_element_type=f32)
    return out.reshape(-1, PW).astype(bf16), top + jnp.log(total)


def attend_back(q, keys_values, mask, log_total, grad_out):
    k, v = keys_values[:, :PW], keys_values[:, PW:]
    q, k, v, g = (item.reshape(-1, PH, HD) for item in (q, k, v, grad_out))
    scores = jnp.einsum("qhe,khe->hqk", q, k, preferred_element_type=f32) * 0.125
    probs = jnp.where(mask, jnp.exp(scores - log_total), 0.0)
    grad_probs = jnp.einsum("qhe,khe->hqk", g, v, preferred_element_type=f32)
    delta = jnp.sum(probs * grad_probs, -1, keepdims=True)
    grad_scores = (probs * (grad_probs - delta)).astype(bf16)
    dq = 0.125 * jnp.einsum("hqk,khe->qhe", grad_scores, k, preferred_element_type=f32)
    dk = 0.125 * jnp.einsum("hqk,qhe->khe", grad_scores, q, preferred_element_type=f32)
    dv = jnp.einsum("hqk,qhe->khe", probs.astype(bf16), g, preferred_element_type=f32)
    dkv = jnp.concatenate([dk.reshape(-1, PW), dv.reshape(-1, PW)], 1)
    return dq.reshape(-1, PW).astype(bf16), dkv


def body(tokens, w_qkv, b_qv, w_proj, b_proj, ln1_gain, ln1_bias, ln2_gain, ln2_bias, w_fc, b_fc, w_out, b_out, d_out):
    size = {name: lax.axis_size(name) for name in ALL}
    devices = math.prod(size.values())
    rows = tokens.shape[1]
    shard = w_qkv.shape[1]
    ff = w_fc.shape[2]
    h, g, x_at, c, f = (lax.axis_index(name) for name in ALL)
    p = 2 * f + x_at
    where = jnp.stack([h, p, c, g, f]).astype(jnp.int32)
    many = size["g"] > 1

    homes = [(a, b) for a in range(size["h"]) for b in range(size["f"])]
    outward = [
        [(a * 2 + b, (2 * b + (a // 2 + turn) % 2) * 2 + a % 2) for a, b in homes] for turn in range(2)
    ]

    def both_ways(value, low, moves):
        sent = [lax.dynamic_index_in_dim(value, i, 0, keepdims=False) for i in (low, 1 - low)]
        return [lax.ppermute(item, ("h", "f"), move) for item, move in zip(sent, moves)]

    def own_sequence(value):
        one, two = both_ways(value, h // 2, outward)
        return jnp.where(h % 2 == 0, jnp.stack([one, two]), jnp.stack([two, one])).reshape(-1, D)

    def back_to_blocks(value):
        moves = [[(b, a) for a, b in move] for move in outward]
        one, two = both_ways(value.reshape(2, rows, D), h % 2, moves)
        return jnp.where(h // 2 == 0, jnp.stack([one, two]), jnp.stack([two, one]))

    smalls = (b_proj, b_out, ln1_gain, ln1_bias, ln2_gain, ln2_bias, b_qv, b_fc)
    by_part = w_out.reshape(LAYERS, TP, shard, D)

    def plane(pieces):
        return jnp.stack([pieces[0]] + [chip_swap(pieces[k], k) for k in range(1, TP)])

    def layer_pieces(where, layer, qkv):
        extra = 0 if qkv is None else 3 * PW
        pieces = launch(
            layer_pieces_kernel(layer, qkv), f"layer_pieces_{layer}", [((shard, 3 * D + extra), bf16)] * TP,
            where, w_fc, by_part, w_proj, w_qkv,
            scratch=[pltpu.VMEM((TP, shard, D + 3 * PW), bf16)],
        )
        return lax.all_gather(plane(pieces), COPIES, axis=0, tiled=True)

    def arrange(own, *widths):
        return [
            item.reshape(D, -1)
            for item in launch(
                arrange_kernel(widths), "arrange", [((devices, shard, width), bf16) for width in widths],
                where, own, swap(own, "c"),
            )
        ]

    feed = layer_pieces(where, 0, None)
    x_own, later = lax.optimization_barrier((own_sequence(tokens), where))
    first = plane(launch(
        first_pieces_kernel, "first_pieces", [((shard, 3 * PW + HD), bf16)] * TP, later, w_qkv, *smalls,
        scratch=[pltpu.VMEM((128, 128), f32), pltpu.VMEM((TP, shard, 3 * PW + HD), bf16)],
    ))
    first, x_pieces = lax.optimization_barrier((first, share(x_own)))
    first = lax.all_gather(first, COPIES, axis=0, tiled=True)
    first = jnp.concatenate([first, swap(first, "c")], 0)
    wq, table = launch(
        arrange_first_kernel(size), "arrange_first",
        [((devices, shard, 3 * PW), bf16), ((LAYERS * 8, D), f32)], where, first,
        scratch=[pltpu.VMEM((D, 128), f32), pltpu.VMEM((devices, shard, HD), f32)],
    )
    wq = [wq.reshape(D, 3 * PW), None]
    wf, wo, wp = [None] * LAYERS, [None] * LAYERS, [None] * LAYERS
    count = TP * x_pieces[0].shape[0]
    own = count // TP
    if many:
        second = jnp.arange(2)[None, :, None]
        inside = jnp.arange(rows)[None, None, :]
        chip = p ^ jnp.arange(TP)[:, None, None]

        def positions(group, core):
            place = (chip // 2 + 2 * second) * size["g"] + group
            return (((place * 2 + chip % 2) * 2 + core) * rows + inside).reshape(-1)

        q_pos = positions(g, c)
        k_pos = jnp.concatenate([positions(gi, core) for gi in range(size["g"]) for core in (0, 1)])
        mask = (k_pos[None, :] <= q_pos[:, None])[None]

    def all_keys(kv, other):
        both = jnp.where(c == 0, jnp.stack([kv, other]), jnp.stack([other, kv])).reshape(-1, kv.shape[1])
        return lax.all_gather(both, "g", axis=0, tiled=True)

    saved = []
    state = tuple(x_pieces)
    for l in range(LAYERS):
        x, x_own, normed, q, kv = launch(
            enter_kernel(l == 0, l), f"enter_{l}",
            [((count, D), f32), ((own, D), f32), ((count, D), bf16), ((count, PW), bf16), ((count, 2 * PW), bf16)],
            where, table, wq[l], *state, flops=2 * count * D * 3 * PW,
        )
        other = swap(kv, "c")
        if l + 1 == LAYERS:
            g_low, x_own = lax.optimization_barrier((own_sequence(d_out), x_own))
            pieces = share(g_low)
        if l == 0:
            feed, other, later = lax.optimization_barrier((feed, other, where))
        wf[l], wo[l], wp[l] = arrange(feed, D, D, D) if l == 0 else after
        if l == 0:
            feed = layer_pieces(later, 1, 1)
        if many:
            keys = all_keys(kv, other)
            out, lse = attend(q, keys, mask)
        else:
            keys = None
            out, lse = launch(
                attend_kernel, f"attend_{l}", [((count, PW), bf16), ((count, PH), f32)], where, q, kv, other,
                scratch=[pltpu.VMEM((count, PW), bf16), pltpu.VMEM((count, 2 * PW), bf16),
                         pltpu.VMEM((count, 2 * PW), bf16), pltpu.VMEM((count, PW), bf16)],
                flops=4 * count * 2 * count * PW,
            )
        if l + 1 == LAYERS:
            out, pieces = lax.optimization_barrier((out, pieces))
        outs = [out] + [chip_swap(out, k) for k in range(1, TP)]
        mid, mid_own, heads, normed2, up, act, y0, y1, y2, y3 = launch(
            middle_kernel(l), f"middle_{l}",
            [((count, D), f32), ((own, D), f32), ((count, D), bf16), ((count, D), bf16), ((count, D), f32), ((count, D), bf16)]
            + [((own, D), f32)] + [((own, D), bf16)] * 3,
            where, table, x, *outs, wp[l], wf[l], wo[l],
            scratch=[pltpu.VMEM((TP, count, PW), bf16)], flops=6 * count * D * D,
        )
        total = y0
        for k, y in ((1, y1), (2, y2), (3, y3)):
            total = total + chip_swap(y, k).astype(f32)
        saved.append((x, x_own, normed, q, kv, other, keys, lse, heads, mid, mid_own, normed2, up, act))
        if l + 1 < LAYERS:
            state = (mid, *share(total.astype(bf16)))
            feed, state = lax.optimization_barrier((feed, state))
            *after, wq[l + 1] = arrange(feed, D, D, D, 3 * PW)
        else:
            tokens_out = mid_own + total + table[8 * l + 1 : 8 * l + 2]
    output = back_to_blocks(tokens_out.astype(bf16))

    copies = devices // (2 * TP)
    halves = [((copies * TP, shard, 2 * D), bf16)] * 2

    def reduce_copies(keep, give):
        total = (keep.astype(f32) + swap(give, "c").astype(f32)).astype(bf16)
        return lax.psum_scatter(total, COPIES, scatter_dimension=0, tiled=True)

    def by_owner(sums):
        return [sums[0]] + [chip_swap(sums[k], k) for k in range(1, TP)]

    line = ((8, D), f32)
    parts = [((own, D), f32)] + [((own, D), bf16)] * 3
    g_own = g_low
    b_out_sum = jnp.broadcast_to(jnp.sum(g_low.astype(f32), 0, keepdims=True), (8, D))
    sums = [None] * LAYERS
    feed_grads = [None] * LAYERS
    for l in reversed(range(LAYERS)):
        x, x_own, normed, q, kv, other, keys, lse, heads, mid, mid_own, normed2, up, act = saved[l]
        if l + 1 < LAYERS:
            pieces = share(g_low)
        g_all, g_up, b_fc_sum, norm2_sum, y0, y1, y2, y3 = launch(
            feed_back_kernel, f"feed_back_{l}", [((count, D), bf16), ((count, D), bf16), line, line] + parts,
            where, *pieces, up, mid, wo[l], wf[l], flops=4 * count * D * D,
        )
        got = [chip_swap(y, k) for k, y in ((1, y1), (2, y2), (3, y3))]
        keep, give = launch(
            feed_weights_kernel, f"feed_weights_{l}", halves, where, act, g_all, normed2, g_up,
            scratch=[pltpu.VMEM((devices, shard, 2 * D), bf16)], flops=4 * count * D * D,
        )
        if l + 1 == LAYERS:
            got, keep, give, output = lax.optimization_barrier((got, keep, give, output))
        else:
            got, keep, give, mixed = lax.optimization_barrier((got, keep, give, mixed))
        feed = reduce_copies(keep, give)
        g_own, g_low, b_proj_sum = launch(
            norm_back_kernel(l, 4), f"norm2_back_{l}", [((own, D), f32), ((own, D), bf16), line],
            where, table, g_own, mid_own, y0, *got,
        )
        pieces = share(g_low)
        if many:
            g_attn = jnp.concatenate(pieces, 0)
            mine = lax.dynamic_slice_in_dim(wp[l], p * PW, PW, 0)
            dq, dkv = attend_back(q, keys, mask, lse, dot(g_attn, mine, NT).astype(bf16))
            dkv = lax.psum_scatter(dkv, "g", scatter_dimension=0, tiled=True).reshape(2, count, 2 * PW)
            dkv, give = (lax.dynamic_index_in_dim(dkv, i, 0, keepdims=False) for i in (c, 1 - c))
            give = give.astype(bf16)
        else:
            g_attn, dq, dkv, give = launch(
                attend_back_kernel, f"attend_back_{l}",
                [((count, D), bf16), ((count, PW), bf16), ((count, 2 * PW), f32), ((count, 2 * PW), bf16)],
                where, *pieces, wp[l], q, kv, other, lse,
                scratch=[pltpu.VMEM((count, PW), f32), pltpu.VMEM((count, PW), bf16), pltpu.VMEM((count, PW), bf16),
                         pltpu.VMEM((count, 2 * PW), bf16), pltpu.VMEM((count, 2 * PW), bf16),
                         pltpu.VMEM((count, PW), f32), pltpu.VMEM((count, 2 * PW), f32), pltpu.VMEM((count, 2 * PW), f32)],
                flops=10 * count * 2 * count * PW,
            )
        more = swap(give, "c")
        if l == 0:
            more, feed = lax.optimization_barrier((more, feed))
        g_qkv, b_qkv_sum, norm1_sum, y0, y1, y2, y3 = launch(
            leave_kernel, f"leave_{l}", [((count, 3 * PW), bf16), line, line] + parts,
            where, dq, dkv, more, wq[l], x, flops=2 * count * D * 3 * PW,
        )
        got = [chip_swap(y, k) for k, y in ((1, y1), (2, y2), (3, y3))]
        sums[l] = (b_proj_sum, b_out_sum, norm1_sum, norm2_sum, b_qkv_sum, b_fc_sum)
        if l > 0:
            keep, give = launch(
                mixed_weights_kernel, f"mixed_weights_{l}", [((copies * TP, shard, D), bf16)] * 2,
                where, normed, g_qkv, heads, g_attn,
                scratch=[pltpu.VMEM((devices, shard, D), bf16)], flops=4 * count * D * D,
            )
            got, keep, give, feed = lax.optimization_barrier((got, keep, give, feed))
            mixed = reduce_copies(keep, give)
        else:
            keep, give = launch(
                last_weights_kernel, "last_weights", [((copies * TP, shard, D + 128), bf16)] * 2,
                where, normed, g_qkv, heads, g_attn, *[item for per_layer in sums for item in per_layer],
                scratch=[pltpu.VMEM((devices, shard, D + 128), bf16), pltpu.VMEM((128, D), f32),
                         pltpu.VMEM((devices, shard, 128), f32)],
                flops=4 * count * D * D,
            )
            last = (keep.astype(f32) + swap(give, "c").astype(f32)).astype(bf16)
            got, last = lax.optimization_barrier((got, last))
            last = lax.all_to_all(last, ("h", "g", "x", "f"), 0, 0, tiled=True)
        feed_grads[l] = feed
        g_own, g_low, b_out_sum = launch(
            norm_back_kernel(l, 2), f"norm1_back_{l}", [((own, D), f32), ((own, D), bf16), line],
            where, table, g_own, x_own, y0, *got,
        )
    grad_tokens = back_to_blocks(g_own)
    d_wf, d_wo = launch(
        finish_feed_kernel, "finish_feed", [((LAYERS, shard, ff), f32), ((LAYERS, TP, shard, D), f32)],
        where, *[item for l in range(LAYERS) for item in by_owner(feed_grads[l])],
        scratch=[pltpu.VMEM((TP, shard, 2 * D), bf16)],
    )
    d_wo = d_wo.reshape(w_out.shape)
    d_wq, d_wp, d_b_proj, d_b_out, d_g1, d_s1, d_g2, d_s2, d_b_qv, d_b_fc = launch(
        finish_mixed_kernel, "finish_mixed",
        [((LAYERS, shard, 3 * D), f32), ((LAYERS, shard, D), f32)] + [(item.shape, f32) for item in smalls],
        where, last, *by_owner(mixed), scratch=[pltpu.VMEM((LAYERS, TP, shard, D), f32), pltpu.VMEM((128, 128), f32)],
    )
    return (output, grad_tokens, d_wq, d_b_qv, d_wp, d_b_proj, d_g1, d_s1, d_g2, d_s2, d_wf, d_b_fc, d_wo, d_b_out)


def solution(mesh):
    ctx, pair = mesh.shape["ctx"], mesh.shape["fsdp"]
    view = Mesh(mesh.devices.reshape(4, ctx // 16, 2, 2, pair), ALL)
    along = ("h", "g", "x", "c")
    token = P("f", along, None)
    matrix = P(None, ALL, None)
    line = P(None, ALL)
    in_specs = (token, matrix, line, matrix, line, line, line, line, line, matrix, line, matrix, line, token)
    out_specs = (token, token, matrix, line, matrix, line, line, line, line, line, matrix, line, matrix, line)
    return jax.shard_map(body, mesh=view, in_specs=in_specs, out_specs=out_specs, check_vma=False)
```

time: 705 us -> 451 us (0.64)
  the two profiles are of different devices: /device:TPU:2 before, /device:TPU:0 now
where the time goes in v2:
time: 451 us; the launch traced here: 446 us
  waiting for transfers between devices  141 us (31%)
  Pallas kernels  135 us (30%)
  starting transfers between devices  106 us (24%)
  other arithmetic  17.4 us (4%)
  blocking collectives  16.2 us (4%)
  between operations  14.9 us (3%)
  local copies, waits for them, and re-layouts  14.6 us (3%)
    pallas_call x28, Pallas kernels, launch(): pl.pallas_call(kernel, name=name, out_shape=shapes, in_specs=[pl.BlockSpe...  135 us
    ppermute x71, waiting for transfers between devices, swap(): return lax.ppermute(value, axis, [(i, i ^ mask) for i in range(size)])  113 us
    ppermute x71, starting transfers between devices, swap(): return lax.ppermute(value, axis, [(i, i ^ mask) for i in range(size)])  76.8 us
    ppermute x8, waiting for transfers between devices, both_ways(): lax.ppermute(item, ('h', 'f'), move)  27.9 us
    ppermute x8, starting transfers between devices, both_ways(): lax.ppermute(item, ('h', 'f'), move)  23.5 us
    all_gather x1, blocking collectives, body(): first = lax.all_gather(first, COPIES, axis=0, tiled=True)  16.2 us
    unnamed x134, local copies, waits for them, and re-layouts  9.58 us
  transfers between devices with their start and end apart: 85, of which 39 were waited for; matrix products, arithmetic and copies ran while one was open for 2% of the time, Pallas kernels for 23%

profile of v2, /device:TPU:0, one launch (start us, length us, event | category | flops | bytes accessed | tf_op | source)
XLA Modules:
  0.0 445.8 jit_solution(5197469939332870826)
XLA Ops:
  28.3 6.1 %collective-permute-start.1 = (bf16[64,768]{1,0:T(8,128)(2,1)S(1)}, bf16[64,768]{1,0:T(8,128)(2,1)S(1)}, u32[]{:S(2)}, u32[]{:S(2)}) collective-permute-start(bf16[64,768]{1,0:T(8,128)(2,1)S(1)} %get-tuple-element.369), channel_id=1, source_target_pairs={{0,8},{1,24},{8,9},{9,25},{16,0},{17,16},{24,1},{25,17},{2,10},{3,... | collective-permute-start | bytes 294920 | tf_op jit(solution)/shard_map/ppermute | solution.py:576
  34.5 15.4 %collective-permute-done.29 = bf16[64,768]{1,0:T(8,128)(2,1)S(1)} collective-permute-done((bf16[64,768]{1,0:T(8,128)(2,1)S(1)}, bf16[64,768]{1,0:T(8,128)(2,1)S(1)}, u32[]{:S(2)}, u32[]{:S(2)}) %collective-permute-start.29) | collective-permute-done | bytes 98336 | tf_op jit(solution)/shard_map/ppermute | solution.py:576
  49.8 12.6 %collective-permute-done.1 = bf16[64,768]{1,0:T(8,128)(2,1)S(1)} collective-permute-done((bf16[64,768]{1,0:T(8,128)(2,1)S(1)}, bf16[64,768]{1,0:T(8,128)(2,1)S(1)}, u32[]{:S(2)}, u32[]{:S(2)}) %collective-permute-start.1) | collective-permute-done | bytes 98336 | tf_op jit(solution)/shard_map/ppermute | solution.py:576
  77.8 16.2 %all_gather.9 = bf16[16,24,640]{2,1,0:T(8,128)(2,1)S(1)} all-gather(bf16[4,24,640]{2,1,0:T(8,128)(2,1)S(1)} %pad_maximum_fusion.3), channel_id=1, replica_groups=mesh['h'=4,'g'=1,'x'=2,'c'=2,'f'=2] {'h','g'}, dimensions={0}, use_global_device_ids=true | all-gather | bytes 614400 | tf_op jit(solution)/shard_map/all_gather | solution.py:618
  121.0 6.6 %attend_0.1 = (bf16[512,192]{1,0:T(8,128)(2,1)}, f32[512,3]{1,0:T(8,128)}) custom-call(s32[5]{0:T(128)} %stack.121.where, bf16[512,192]{1,0:T(8,128)(2,1)} %get-tuple-element.208.q_ref, bf16[512,384]{1,0:T(8,128)(2,1)} %get-tuple-element.201.own_ref, bf16[512,384]{1,0:T(8,128)(2,1)} %copy-done.50), custom_call_target="tpu_custom_call" | custom-call | flops 402653184 | bytes 1185792 | tf_op jit(solution)/shard_map/attend_0/pallas_call | solution.py:53
  132.4 4.7 %arrange.2 = (bf16[32,24,768]{2,1,0:T(8,128)(2,1)}, bf16[32,24,768]{2,1,0:T(8,128)(2,1)}, bf16[32,24,768]{2,1,0:T(8,128)(2,1)}) custom-call(s32[5]{0:T(128)} %stack.121.where, bf16[16,24,2304]{2,1,0:T(8,128)(2,1)} %all-gather.3.cloned.1.call-done.own, bf16[16,24,2304]{2,1,0:T(8,128)(2,1)} %copy-done.5), custom_call_target="tpu_custom_call" | custom-call | bytes 7077888 | tf_op jit(solution)/shard_map/arrange/pallas_call | solution.py:53
  144.0 6.8 %middle_0.1 = (f32[512,768]{1,0:T(8,128)}, f32[128,768]{1,0:T(8,128)}, bf16[512,768]{1,0:T(8,128)(2,1)}, bf16[512,768]{1,0:T(8,128)(2,1)}, f32[512,768]{1,0:T(8,...) custom-call(s32[5]{0:T(128)} %stack.121.where, ...), custom_call_target="tpu_custom_call" | custom-call | flops 1811939328 | bytes 12828672 | tf_op jit(solution)/shard_map/middle_0/pallas_call | solution.py:53
  174.5 4.6 %collective-permute-done.26.oth = bf16[16,24,2880]{2,1,0:T(8,128)(2,1)S(1)} collective-permute-done((bf16[16,24,2880]{2,1,0:T(8,128)(2,1)}, bf16[16,24,2880]{2,1,0:T(8,128)(2,1)S(1)}, u32[]{:S(2)}, u32[]{:S(2)}) %collective-permute-start.26) | collective-permute-done | bytes 2211872 | tf_op jit(solution)/shard_map/ppermute | solution.py:39
  180.5 5.5 %arrange.3 = (bf16[32,24,768]{2,1,0:T(8,128)(2,1)}, bf16[32,24,768]{2,1,0:T(8,128)(2,1)}, bf16[32,24,768]{2,1,0:T(8,128)(2,1)}, bf16[32,24,576]{2,1,0:T(8,128)(2,1)}) custom-call(s32[5]{0:T(128)} %stack.121.where, bf16[16,24,2880]{2,1,0:T(8,128)(2,1)} %all-gather.5.cloned.1.call-done.own, bf16[16,24,2880]{2,1,0:T(8,128)(2,1)} %copy-done.3), custom_call_target="tpu_custom_call" | custom-call | bytes 8847360 | tf_op jit(solution)/shard_map/arrange/pallas_call | solution.py:53
  194.3 6.6 %attend_1.1 = (bf16[512,192]{1,0:T(8,128)(2,1)}, f32[512,3]{1,0:T(8,128)}) custom-call(s32[5]{0:T(128)} %stack.121.where, bf16[512,192]{1,0:T(8,128)(2,1)} %get-tuple-element.227.q_ref, bf16[512,384]{1,0:T(8,128)(2,1)} %get-tuple-element.228.own_ref, bf16[512,384]{1,0:T(8,128)(2,1)} %copy-done.51), custom_call_target="tpu_custom_call" | custom-call | flops 402653184 | bytes 1185792 | tf_op jit(solution)/shard_map/attend_1/pallas_call | solution.py:53
  205.3 6.0 %collective-permute-done.33.o1 = bf16[512,192]{1,0:T(8,128)(2,1)S(1)} collective-permute-done((bf16[512,192]{1,0:T(8,128)(2,1)}, bf16[512,192]{1,0:T(8,128)(2,1)S(1)}, u32[]{:S(2)}, u32[]{:S(2)}) %collective-permute-start.33) | collective-permute-done | bytes 196640 | tf_op jit(solution)/shard_map/ppermute | solution.py:39
  211.2 5.0 %collective-permute-done.34.o2 = bf16[512,192]{1,0:T(8,128)(2,1)S(1)} collective-permute-done((bf16[512,192]{1,0:T(8,128)(2,1)}, bf16[512,192]{1,0:T(8,128)(2,1)S(1)}, u32[]{:S(2)}, u32[]{:S(2)}) %collective-permute-start.34) | collective-permute-done | bytes 196640 | tf_op jit(solution)/shard_map/ppermute | solution.py:39
  217.0 6.7 %middle_1.1 = (f32[512,768]{1,0:T(8,128)}, f32[128,768]{1,0:T(8,128)}, bf16[512,768]{1,0:T(8,128)(2,1)}, bf16[512,768]{1,0:T(8,128)(2,1)}, f32[512,768]{1,0:T(8,...) custom-call(s32[5]{0:T(128)} %stack.121.where, ...), custom_call_target="tpu_custom_call" | custom-call | flops 1811939328 | bytes 12828672 | tf_op jit(solution)/shard_map/middle_1/pallas_call | solution.py:53
  228.1 6.8 %feed_back_1.1 = (bf16[512,768]{1,0:T(8,128)(2,1)}, bf16[512,768]{1,0:T(8,128)(2,1)}, f32[8,768]{1,0:T(8,128)}, f32[8,768]{1,0:T(8,128)}, f32[128,768]{1,0:T(8,1...) custom-call(s32[5]{0:T(128)} %stack.121.where, bf16[128,768]{1,0:T(8,128)(2,1)} %bitcast.85, ...), custom_call_target="tpu_custom_call" | custom-call | flops 1207959552 | bytes 8896512 | tf_op jit(solution)/shard_map/feed_back_1/pallas_call | solution.py:53
  243.6 4.8 %feed_weights_1.1 = (bf16[16,24,1536]{2,1,0:T(8,128)(2,1)}, bf16[16,24,1536]{2,1,0:T(8,128)(2,1)}) custom-call(s32[5]{0:T(128)} %stack.121.where, bf16[512,768]{1,0:T(8,128)(2,1)} %get-tuple-element.246.act, bf16[512,768]{1,0:T(8,128)(2,1)} %get-tuple-element.247.g, bf16[512,768]{1,0:T(8,128)(2,1)} %get-tuple-element.248.normed, ...), custom_call_target="tpu_custom_call" | custom-call | flops 1207959552 | bytes 5505024 | tf_op jit(solution)/shard_map/feed_weights_1/pallas_call | solution.py:53
  272.1 11.6 %attend_back_1.1 = (bf16[512,768]{1,0:T(8,128)(2,1)}, bf16[512,192]{1,0:T(8,128)(2,1)}, f32[512,384]{1,0:T(8,128)}, bf16[512,384]{1,0:T(8,128)(2,1)}) custom-call(s32[5]{0:T(128)} %stack.121.where, bf16[128,768]{1,0:T(8,128)(2,1)} %get-tuple-element.264.g0, bf16[128,768]{1,0:T(8,128)(2,1)} %copy-done.61, bf16[128,768]{1,0:T(8,128)(2,1)} %copy-done.63, ...), custom_call_target="tpu_custom_call" | custom-call | flops 1006632960 | bytes 5117952 | tf_op jit(solution)/shard_map/attend_back_1/pallas_call | solution.py:53
  323.1 6.7 %feed_back_0.1 = (bf16[512,768]{1,0:T(8,128)(2,1)}, bf16[512,768]{1,0:T(8,128)(2,1)}, f32[8,768]{1,0:T(8,128)}, f32[8,768]{1,0:T(8,128)}, f32[128,768]{1,0:T(8,1...) custom-call(s32[5]{0:T(128)} %stack.121.where, ...), custom_call_target="tpu_custom_call" | custom-call | flops 1207959552 | bytes 8896512 | tf_op jit(solution)/shard_map/feed_back_0/pallas_call | solution.py:53
  333.3 4.7 %feed_weights_0.1 = (bf16[16,24,1536]{2,1,0:T(8,128)(2,1)}, bf16[16,24,1536]{2,1,0:T(8,128)(2,1)}) custom-call(s32[5]{0:T(128)} %stack.121.where, bf16[512,768]{1,0:T(8,128)(2,1)} %get-tuple-element.292.act, bf16[512,768]{1,0:T(8,128)(2,1)} %get-tuple-element.293.g, bf16[512,768]{1,0:T(8,128)(2,1)} %get-tuple-element.294.normed, ...), custom_call_target="tpu_custom_call" | custom-call | flops 1207959552 | bytes 5505024 | tf_op jit(solution)/shard_map/feed_weights_0/pallas_call | solution.py:53
  357.1 4.7 %collective-permute-done.60.g2 = bf16[128,768]{1,0:T(8,128)(2,1)S(1)} collective-permute-done((bf16[128,768]{1,0:T(8,128)(2,1)}, bf16[128,768]{1,0:T(8,128)(2,1)S(1)}, u32[]{:S(2)}, u32[]{:S(2)}) %collective-permute-start.60) | collective-permute-done | bytes 196640 | tf_op jit(solution)/shard_map/ppermute | solution.py:39
  362.5 11.9 %attend_back_0.1 = (bf16[512,768]{1,0:T(8,128)(2,1)}, bf16[512,192]{1,0:T(8,128)(2,1)}, f32[512,384]{1,0:T(8,128)}, bf16[512,384]{1,0:T(8,128)(2,1)}) custom-call(s32[5]{0:T(128)} %stack.121.where, bf16[128,768]{1,0:T(8,128)(2,1)} %get-tuple-element.305.g0, bf16[128,768]{1,0:T(8,128)(2,1)} %copy-done.62, bf16[128,768]{1,0:T(8,128)(2,1)} %copy-done.64, ...), custom_call_target="tpu_custom_call" | custom-call | flops 1006632960 | bytes 5117952 | tf_op jit(solution)/shard_map/attend_back_0/pallas_call | solution.py:53
  382.0 4.7 %last_weights.1 = (bf16[16,24,896]{2,1,0:T(8,128)(2,1)}, bf16[16,24,896]{2,1,0:T(8,128)(2,1)}) custom-call(s32[5]{0:T(128)} %stack.121.where, bf16[512,768]{1,0:T(8,128)(2,1)} %get-tuple-element.317.normed, bf16[512,576]{1,0:T(8,128)(2,1)} %get-tuple-element.318.g_qkv, bf16[512,768]{1,0:T(8,128)(2,1)} %get-tuple-element.319.heads, ...), custom_call_target="tpu_custom_call" | custom-call | flops 1207959552 | bytes 4620288 | tf_op jit(solution)/shard_map/last_weights/pallas_call | solution.py:53
  398.5 4.8 %all-to-all-start = ((bf16[16,24,896]{2,1,0:T(8,128)(2,1)}), bf16[16,24,896]{2,1,0:T(8,128)(2,1)S(1)}, u32[]{:S(2)}, u32[]{:S(2)}) async-start(bf16[16,24,896]{2,1,0:T(8,128)(2,1)} %add_convert_fusion.2), calls=%async_computation.3 | async-start | bytes 1376256 | tf_op jit(solution)/shard_map/all_to_all | solution.py:779
  416.2 6.4 %collective-permute-start.69 = (f32[64,768]{1,0:T(8,128)S(1)}, f32[64,768]{1,0:T(8,128)S(1)}, u32[]{:S(2)}, u32[]{:S(2)}) collective-permute-start(f32[64,768]{1,0:T(8,128)S(1)} %get-tuple-element.355), channel_id=1, source_target_pairs={{8,0},{24,1},{9,8},{25,9},{0,16},{16,17},{1,24},{17,25},{10,2},{26... | collective-permute-start | bytes 589832 | tf_op jit(solution)/shard_map/ppermute | solution.py:576
  423.9 6.4 %collective-permute-start.71 = (bf16[24,768]{1,0:T(8,128)(2,1)S(1)}, bf16[24,768]{1,0:T(8,128)(2,1)S(1)}, u32[]{:S(2)}, u32[]{:S(2)}) collective-permute-start(bf16[24,768]{1,0:T(8,128)(2,1)S(1)} %get-tuple-element.371), channel_id=1, source_target_pairs={{0,1},{1,0},{4,5},{5,4},{2,3},{3,2},{6,7},{7,6},{8,9},{9,8},{12,13... | collective-permute-start | bytes 110600 | tf_op jit(solution)/shard_map/ppermute | solution.py:39
  (338 shorter events, 254.7 us)
Async XLA Ops:
  7.2 98.0 %all-gather.3.cloned.1.call-start = ((), (), s32[]{:S(2)}) async-start(), calls=%async_computation.4 | async-start | bytes 2211840 | tf_op jit(solution)/shard_map/all_gather | solution.py:600
  22.9 151.5 %all-gather.5.cloned.1.call-start = ((), (), s32[]{:S(2)}) async-start(), calls=%async_computation.5 | async-start | bytes 2826240 | tf_op jit(solution)/shard_map/all_gather | solution.py:600
  23.6 26.2 %collective-permute-start.29 = (bf16[64,768]{1,0:T(8,128)(2,1)S(1)}, bf16[64,768]{1,0:T(8,128)(2,1)S(1)}, u32[]{:S(2)}, u32[]{:S(2)}) collective-permute-start(bf16[64,768]{1,0:T(8,128)(2,1)S(1)} %get-tuple-element.367), channel_id=1, source_target_pairs={{0,8},{1,24},{8,9},{9,25},{16,0},{17,16},{24,1},{25,17},{2,10},{3,... | collective-permute-start | bytes 294920 | tf_op jit(solution)/shard_map/ppermute | solution.py:576
  27.7 22.2 %collective-permute-start = (bf16[64,768]{1,0:T(8,128)(2,1)S(1)}, bf16[64,768]{1,0:T(8,128)(2,1)S(1)}, u32[]{:S(2)}, u32[]{:S(2)}) collective-permute-start(bf16[64,768]{1,0:T(8,128)(2,1)S(1)} %get-tuple-element.368), channel_id=1, source_target_pairs={{0,0},{1,16},{8,1},{9,17},{16,8},{17,24},{24,9},{25,25},{2,2},{3,1... | collective-permute-start | bytes 294920 | tf_op jit(solution)/shard_map/ppermute | solution.py:576
  28.3 34.0 %collective-permute-start.1 = (bf16[64,768]{1,0:T(8,128)(2,1)S(1)}, bf16[64,768]{1,0:T(8,128)(2,1)S(1)}, u32[]{:S(2)}, u32[]{:S(2)}) collective-permute-start(bf16[64,768]{1,0:T(8,128)(2,1)S(1)} %get-tuple-element.369), channel_id=1, source_target_pairs={{0,8},{1,24},{8,9},{9,25},{16,0},{17,16},{24,1},{25,17},{2,10},{3,... | collective-permute-start | bytes 294920 | tf_op jit(solution)/shard_map/ppermute | solution.py:576
  62.5 15.3 %collective-permute-start.5 = (bf16[128,768]{1,0:T(8,128)(2,1)S(1)}, bf16[128,768]{1,0:T(8,128)(2,1)S(1)}, u32[]{:S(2)}, u32[]{:S(2)}) collective-permute-start(bf16[128,768]{1,0:T(8,128)(2,1)S(1)} %bitcast.99), channel_id=1, source_target_pairs={{0,4},{1,5},{4,0},{5,1},{2,6},{3,7},{6,2},{7,3},{8,12},{9,13},{12,... | collective-permute-start | bytes 589832 | tf_op jit(solution)/shard_map/ppermute | solution.py:39
  63.9 13.9 %collective-permute-start.6 = (bf16[128,768]{1,0:T(8,128)(2,1)S(1)}, bf16[128,768]{1,0:T(8,128)(2,1)S(1)}, u32[]{:S(2)}, u32[]{:S(2)}) collective-permute-start(bf16[128,768]{1,0:T(8,128)(2,1)S(1)} %bitcast.100), channel_id=1, source_target_pairs={{0,1},{1,0},{4,5},{5,4},{2,3},{3,2},{6,7},{7,6},{8,9},{9,8},{12,13... | collective-permute-start | bytes 589832 | tf_op jit(solution)/shard_map/ppermute | solution.py:39
  63.9 13.9 %collective-permute-start.7 = (bf16[128,768]{1,0:T(8,128)(2,1)S(1)}, bf16[128,768]{1,0:T(8,128)(2,1)S(1)}, u32[]{:S(2)}, u32[]{:S(2)}) collective-permute-start(bf16[128,768]{1,0:T(8,128)(2,1)S(1)} %bitcast.101), channel_id=1, source_target_pairs={{0,5},{1,4},{4,1},{5,0},{2,7},{3,6},{6,3},{7,2},{8,13},{9,12},{12,... | collective-permute-start | bytes 589832 | tf_op jit(solution)/shard_map/ppermute | solution.py:39
  120.6 182.0 %reduce-scatter.4.cloned.1.call-start = ((), (), s32[]{:S(2)}) async-start(), calls=%async_computation.6 | async-start | bytes 1474560 | tf_op jit(solution)/shard_map/reduce_scatter | solution.py:701
  129.6 13.7 %collective-permute-start.18 = (bf16[512,192]{1,0:T(8,128)(2,1)}, bf16[512,192]{1,0:T(8,128)(2,1)S(1)}, u32[]{:S(2)}, u32[]{:S(2)}) collective-permute-start(bf16[512,192]{1,0:T(8,128)(2,1)} %get-tuple-element.210.o0), channel_id=1, source_target_pairs={{0,5},{1,4},{4,1},{5,0},{2,7},{3,6},{6,3},{7,2},{8,13},{9,12},{12,... | collective-permute-start | bytes 589832 | tf_op jit(solution)/shard_map/ppermute | solution.py:39
  203.3 13.0 %collective-permute-start.34 = (bf16[512,192]{1,0:T(8,128)(2,1)}, bf16[512,192]{1,0:T(8,128)(2,1)S(1)}, u32[]{:S(2)}, u32[]{:S(2)}) collective-permute-start(bf16[512,192]{1,0:T(8,128)(2,1)} %get-tuple-element.237.o0), channel_id=1, source_target_pairs={{0,1},{1,0},{4,5},{5,4},{2,3},{3,2},{6,7},{7,6},{8,9},{9,8},{12,13... | collective-permute-start | bytes 589832 | tf_op jit(solution)/shard_map/ppermute | solution.py:39
  203.5 12.7 %collective-permute-start.35 = (bf16[512,192]{1,0:T(8,128)(2,1)}, bf16[512,192]{1,0:T(8,128)(2,1)S(1)}, u32[]{:S(2)}, u32[]{:S(2)}) collective-permute-start(bf16[512,192]{1,0:T(8,128)(2,1)} %get-tuple-element.237.o0), channel_id=1, source_target_pairs={{0,5},{1,4},{4,1},{5,0},{2,7},{3,6},{6,3},{7,2},{8,13},{9,12},{12,... | collective-permute-start | bytes 589832 | tf_op jit(solution)/shard_map/ppermute | solution.py:39
  223.8 13.2 %collective-permute-start.39 = (bf16[128,768]{1,0:T(8,128)(2,1)}, bf16[128,768]{1,0:T(8,128)(2,1)S(1)}, u32[]{:S(2)}, u32[]{:S(2)}) collective-permute-start(bf16[128,768]{1,0:T(8,128)(2,1)} %get-tuple-element.254), channel_id=1, source_target_pairs={{0,4},{1,5},{4,0},{5,1},{2,6},{3,7},{6,2},{7,3},{8,12},{9,13},{12,... | collective-permute-start | bytes 589832 | tf_op jit(solution)/shard_map/ppermute | solution.py:39
  224.1 14.3 %collective-permute-start.40 = (bf16[128,768]{1,0:T(8,128)(2,1)}, bf16[128,768]{1,0:T(8,128)(2,1)S(1)}, u32[]{:S(2)}, u32[]{:S(2)}) collective-permute-start(bf16[128,768]{1,0:T(8,128)(2,1)} %get-tuple-element.255), channel_id=1, source_target_pairs={{0,1},{1,0},{4,5},{5,4},{2,3},{3,2},{6,7},{7,6},{8,9},{9,8},{12,13... | collective-permute-start | bytes 589832 | tf_op jit(solution)/shard_map/ppermute | solution.py:39
  234.9 14.2 %collective-permute-start.36 = (bf16[128,768]{1,0:T(8,128)(2,1)}, bf16[128,768]{1,0:T(8,128)(2,1)S(1)}, u32[]{:S(2)}, u32[]{:S(2)}) collective-permute-start(bf16[128,768]{1,0:T(8,128)(2,1)} %get-tuple-element.243), channel_id=1, source_target_pairs={{0,4},{1,5},{4,0},{5,1},{2,6},{3,7},{6,2},{7,3},{8,12},{9,13},{12,... | collective-permute-start | bytes 589832 | tf_op jit(solution)/shard_map/ppermute | solution.py:39
  235.2 13.9 %collective-permute-start.37 = (bf16[128,768]{1,0:T(8,128)(2,1)}, bf16[128,768]{1,0:T(8,128)(2,1)S(1)}, u32[]{:S(2)}, u32[]{:S(2)}) collective-permute-start(bf16[128,768]{1,0:T(8,128)(2,1)} %get-tuple-element.244), channel_id=1, source_target_pairs={{0,1},{1,0},{4,5},{5,4},{2,3},{3,2},{6,7},{7,6},{8,9},{9,8},{12,13... | collective-permute-start | bytes 589832 | tf_op jit(solution)/shard_map/ppermute | solution.py:39
  254.9 85.8 %reduce-scatter.6.cloned.1.call-start = ((), (), s32[]{:S(2)}) async-start(), calls=%async_computation.7 | async-start | bytes 737280 | tf_op jit(solution)/shard_map/reduce_scatter | solution.py:701
  307.0 69.3 %reduce-scatter.8.cloned.1.call-start = ((), (), s32[]{:S(2)}) async-start(), calls=%async_computation.8 | async-start | bytes 1474560 | tf_op jit(solution)/shard_map/reduce_scatter | solution.py:701
  398.5 37.2 %all-to-all-start = ((bf16[16,24,896]{2,1,0:T(8,128)(2,1)}), bf16[16,24,896]{2,1,0:T(8,128)(2,1)S(1)}, u32[]{:S(2)}, u32[]{:S(2)}) async-start(bf16[16,24,896]{2,1,0:T(8,128)(2,1)} %add_convert_fusion.2), calls=%async_computation.3 | async-start | bytes 1376256 | tf_op jit(solution)/shard_map/all_to_all | solution.py:779
  408.1 15.1 %collective-permute-start.73 = (bf16[24,1536]{1,0:T(8,128)(2,1)S(1)}, bf16[24,1536]{1,0:T(8,128)(2,1)S(1)}, u32[]{:S(2)}, u32[]{:S(2)}) collective-permute-start(bf16[24,1536]{1,0:T(8,128)(2,1)S(1)} %get-tuple-element.362), channel_id=1, source_target_pairs={{0,4},{1,5},{4,0},{5,1},{2,6},{3,7},{6,2},{7,3},{8,12},{9,13},{12,... | collective-permute-start | bytes 221192 | tf_op jit(solution)/shard_map/ppermute | solution.py:39
  410.1 13.7 %collective-permute-start.74 = (bf16[24,1536]{1,0:T(8,128)(2,1)S(1)}, bf16[24,1536]{1,0:T(8,128)(2,1)S(1)}, u32[]{:S(2)}, u32[]{:S(2)}) collective-permute-start(bf16[24,1536]{1,0:T(8,128)(2,1)S(1)} %get-tuple-element.361), channel_id=1, source_target_pairs={{0,1},{1,0},{4,5},{5,4},{2,3},{3,2},{6,7},{7,6},{8,9},{9,8},{12,13... | collective-permute-start | bytes 221192 | tf_op jit(solution)/shard_map/ppermute | solution.py:39
  415.3 14.9 %collective-permute-start.75 = (bf16[24,1536]{1,0:T(8,128)(2,1)S(1)}, bf16[24,1536]{1,0:T(8,128)(2,1)S(1)}, u32[]{:S(2)}, u32[]{:S(2)}) collective-permute-start(bf16[24,1536]{1,0:T(8,128)(2,1)S(1)} %get-tuple-element.360), channel_id=1, source_target_pairs={{0,5},{1,4},{4,1},{5,0},{2,7},{3,6},{6,3},{7,2},{8,13},{9,12},{12,... | collective-permute-start | bytes 221192 | tf_op jit(solution)/shard_map/ppermute | solution.py:39
  415.5 19.4 %collective-permute-start.68 = (f32[64,768]{1,0:T(8,128)S(1)}, f32[64,768]{1,0:T(8,128)S(1)}, u32[]{:S(2)}, u32[]{:S(2)}) collective-permute-start(f32[64,768]{1,0:T(8,128)S(1)} %get-tuple-element.354), channel_id=1, source_target_pairs={{0,0},{16,1},{1,8},{17,9},{8,16},{24,17},{9,24},{25,25},{2,2},{18,... | collective-permute-start | bytes 589832 | tf_op jit(solution)/shard_map/ppermute | solution.py:576
  416.2 18.7 %collective-permute-start.69 = (f32[64,768]{1,0:T(8,128)S(1)}, f32[64,768]{1,0:T(8,128)S(1)}, u32[]{:S(2)}, u32[]{:S(2)}) collective-permute-start(f32[64,768]{1,0:T(8,128)S(1)} %get-tuple-element.355), channel_id=1, source_target_pairs={{8,0},{24,1},{9,8},{25,9},{0,16},{16,17},{1,24},{17,25},{10,2},{26... | collective-permute-start | bytes 589832 | tf_op jit(solution)/shard_map/ppermute | solution.py:576
  (128 other events, 1194.2 us)
Sparse Core Ops, SparseCore 0:
  23.0 49.5 all-gather.2
  120.7 49.7 all-gather.4
  255.0 29.8 reduce-scatter.3
  307.1 21.1 reduce-scatter.5
  346.6 28.3 reduce-scatter.7

commit v3 on v2

--- a/solution.py
+++ b/solution.py
@@ -41,6 +41,10 @@
 
 def chip_swap(value, mask):
     return swap(value, ("x", "f"), mask % 2 * 2 + mask // 2)
+
+
+def after(value, event):
+    return lax.optimization_barrier((value, event))[0]
 
 
 def share(own):
@@ -97,7 +101,7 @@
         out[...] = cols[jnp.bitwise_xor(p, k)]
 
 
-def layer_pieces_kernel(layer, qkv):
+def layer_pieces_kernel(layer):
     def kernel(where, w_fc, w_out, w_proj, w_qkv, *refs):
         outs, (cols,) = refs[:TP], refs[TP:]
         p = where[1]
@@ -108,33 +112,34 @@
         for q in range(TP):
             lanes = slice(q * block // TP, (q + 1) * block // TP)
             cols[q, :, :D] = jnp.concatenate([item[:, lanes] for item in fc], 1).astype(bf16)
-            if qkv is not None:
-                parts = [w_qkv[qkv, :, j * D + q * PW : j * D + (q + 1) * PW] for j in range(3)]
-                cols[q, :, D:] = jnp.concatenate(parts, 1)
+            if layer:
+                parts = [w_qkv[layer, :, j * D + q * PW : j * D + (q + 1) * PW] for j in range(3)]
+                cols[q, :, D:] = jnp.concatenate(parts + [jnp.zeros((shard, HD), bf16)], 1)
         for k, out in enumerate(outs):
             q = jnp.bitwise_xor(p, k)
             out[:, :D] = cols[q, :, :D]
             out[:, D : 2 * D] = w_out[layer, q]
             out[:, 2 * D : 3 * D] = w_proj[layer]
-            if qkv is not None:
+            if layer:
                 out[:, 3 * D :] = cols[q, :, D:]
 
     return kernel
 
 
 def arrange_first_kernel(sizes):
-    def kernel(where, got, w_out, table, columns, blocks):
-        p, c = where[1], where[2]
-        devices, shard = w_out.shape[:2]
+    def kernel(where, got, w_first, table, columns, blocks):
+        h, p, c = where[0], where[1], where[2]
+        devices, shard = w_first.shape[:2]
         groups = sizes["g"]
         columns[...] = jnp.zeros_like(columns)
         for d in range(devices):
             rest, fi = divmod(d, 2)
             rest, ci = divmod(rest, 2)
             rest, xi = divmod(rest, 2)
-            copy = jnp.bitwise_xor(c, ci) * sizes["h"] * groups + rest
+            hi, gi = divmod(rest, groups)
+            copy = (jnp.bitwise_xor(c, ci) * sizes["h"] + jnp.bitwise_xor(h, hi)) * groups + gi
             one = got[copy * TP + jnp.bitwise_xor(p, 2 * fi + xi)].astype(f32)
-            w_out[d] = one[:, : 3 * PW].astype(bf16)
+            w_first[d] = one[:, : 3 * PW].astype(bf16)
             columns[d * shard : (d + 1) * shard, :HD] = one[:, 3 * PW :]
             blocks[d] = one[:, 3 * PW :]
         lines = columns[...].T
@@ -161,14 +166,14 @@
 
 
 def finish_feed_kernel(where, *refs):
-    pieces, (wf_out, wo_out, cols) = refs[: LAYERS * TP], refs[LAYERS * TP :]
+    pieces, (wf_out, wo_out, cols) = refs[:TP], refs[TP:]
     p = where[1]
     shard = wf_out.shape[1]
     block = D // 2
     order = interleave(shard)
     for l in range(LAYERS):
         for k in range(TP):
-            cols[jnp.bitwise_xor(p, k)] = pieces[l * TP + k][...]
+            cols[jnp.bitwise_xor(p, k)] = pieces[k][:, 2 * D * l : 2 * D * (l + 1)]
         fc = [cols[q, :, :D].astype(f32) for q in range(TP)]
         for b in range(wf_out.shape[2] // block):
             lanes = slice(b * block // TP, (b + 1) * block // TP)
@@ -190,7 +195,7 @@
         columns = columns + total[:, D:]
         cols[0, q] = total[:, :D]
     for k, m in enumerate((m0, m1, m2, m3)):
-        cols[1, jnp.bitwise_xor(p, k)] = m[...].astype(f32)
+        cols[1, jnp.bitwise_xor(p, k)] = m[:, 2 * D * LAYERS :].astype(f32)
     for l in range(LAYERS):
         for j in range(3):
             wq_out[l, :, j * D : (j + 1) * D] = jnp.concatenate(
@@ -324,6 +329,7 @@
         g_out[k * rows : (k + 1) * rows, :] = g[...]
     bfc_out[...] = jnp.zeros_like(bfc_out)
     sums_out[...] = jnp.zeros_like(sums_out)
+    sums_out[2:3, :] = jnp.sum(g0[...].astype(f32), 0, keepdims=True)
     for k, y in enumerate((y0, y1, y2, y3)):
         at = slice(k * rows, (k + 1) * rows)
         g_act = dot(g_out[at, :], wo[...], NT)
@@ -495,17 +501,19 @@
     scatter_blocks(where, blocks, keep, give)
 
 
-def last_weights_kernel(where, normed, g_qkv, heads, g_attn, *refs):
-    sums, (keep, give, blocks, lines, more) = refs[: 6 * LAYERS], refs[6 * LAYERS :]
+def leave_last_kernel(where, dq, dkv, more_keys, wq, x, normed, heads, g_attn, *refs):
+    sums, refs = refs[: 5 * LAYERS - 2], refs[5 * LAYERS - 2 :]
+    keep, give, y0, y1, y2, y3, blocks, lines, more, g_qkv, b_qkv, norm1_first = refs
+    leave_kernel(where, dq, dkv, more_keys, wq, x, g_qkv, b_qkv, norm1_first, y0, y1, y2, y3)
     p, c = where[1], where[2]
     devices, shard = blocks.shape[:2]
     per = PW // (2 * shard)
     lines[...] = jnp.zeros_like(lines)
     more[...] = jnp.zeros_like(more)
     for l in range(LAYERS):
-        b_proj, b_out, norm1, norm2, qkv, fc = sums[6 * l : 6 * l + 6]
+        b_proj, norm2, fc, norm1, qkv = (tuple(sums[:3]) + (norm1_first, b_qkv)) if l == 0 else sums[3:]
         base = SLOTS * l
-        rows = (b_proj[0:1, :], b_out[0:1, :], norm1[0:1, :], norm1[1:2, :], norm2[0:1, :], norm2[1:2, :])
+        rows = (b_proj[0:1, :], norm2[2:3, :], norm1[0:1, :], norm1[1:2, :], norm2[0:1, :], norm2[1:2, :])
         for i, row in enumerate(rows):
             lines[base + i : base + i + 1, :] = row
         for q in range(TP):
@@ -568,7 +576,7 @@
 
     homes = [(a, b) for a in range(size["h"]) for b in range(size["f"])]
     outward = [
-        [(a * 2 + b, (2 * b + (a // 2 + turn) % 2) * 2 + a % 2) for a, b in homes] for turn in range(2)
+        [(a * 2 + b, (2 * ((a // 2 + turn) % 2) + b) * 2 + a % 2) for a, b in homes] for turn in range(2)
     ]
 
     def both_ways(value, low, moves):
@@ -577,11 +585,12 @@
 
     def own_sequence(value):
         one, two = both_ways(value, h // 2, outward)
-        return jnp.where(h % 2 == 0, jnp.stack([one, two]), jnp.stack([two, one])).reshape(-1, D)
+        both = jnp.where(h // 2 == 0, jnp.stack([one, two]), jnp.stack([two, one]))
+        return [both[:, i].reshape(-1, D) for i in range(2)]
 
     def back_to_blocks(value):
         moves = [[(b, a) for a, b in move] for move in outward]
-        one, two = both_ways(value.reshape(2, rows, D), h % 2, moves)
+        one, two = both_ways(value.reshape(2, rows, -1), h // 2, moves)
         return jnp.where(h // 2 == 0, jnp.stack([one, two]), jnp.stack([two, one]))
 
     smalls = (b_proj, b_out, ln1_gain, ln1_bias, ln2_gain, ln2_bias, b_qv, b_fc)
@@ -590,14 +599,15 @@
     def plane(pieces):
         return jnp.stack([pieces[0]] + [chip_swap(pieces[k], k) for k in range(1, TP)])
 
-    def layer_pieces(where, layer, qkv):
-        extra = 0 if qkv is None else 3 * PW
-        pieces = launch(
-            layer_pieces_kernel(layer, qkv), f"layer_pieces_{layer}", [((shard, 3 * D + extra), bf16)] * TP,
-            where, w_fc, by_part, w_proj, w_qkv,
-            scratch=[pltpu.VMEM((TP, shard, D + 3 * PW), bf16)],
+    def layer_pieces(where, layer):
+        return launch(
+            layer_pieces_kernel(layer), f"layer_pieces_{layer}",
+            [((shard, 3 * D + (3 * PW + HD if layer else 0)), bf16)] * TP,
+            where, w_fc, by_part, w_proj, w_qkv, scratch=[pltpu.VMEM((TP, shard, D + 3 * PW + HD), bf16)],
         )
-        return lax.all_gather(plane(pieces), COPIES, axis=0, tiled=True)
+
+    def fetch(pieces):
+        return lax.all_gather(pieces, COPIES, axis=0, tiled=True)
 
     def arrange(own, *widths):
         return [
@@ -608,14 +618,21 @@
             )
         ]
 
-    feed = layer_pieces(where, 0, None)
-    x_own, later = lax.optimization_barrier((own_sequence(tokens), where))
-    first = plane(launch(
-        first_pieces_kernel, "first_pieces", [((shard, 3 * PW + HD), bf16)] * TP, later, w_qkv, *smalls,
+    feed = layer_pieces(where, 0)
+    first = launch(
+        first_pieces_kernel, "first_pieces", [((shard, 3 * PW + HD), bf16)] * TP, where, w_qkv, *smalls,
         scratch=[pltpu.VMEM((128, 128), f32), pltpu.VMEM((TP, shard, 3 * PW + HD), bf16)],
-    ))
-    first, x_pieces = lax.optimization_barrier((first, share(x_own)))
-    first = lax.all_gather(first, COPIES, axis=0, tiled=True)
+    )
+    x_own, g_low = own_sequence(jnp.stack([tokens, d_out], 1))
+    feed, first, x_own, g_low = lax.optimization_barrier((feed, first, x_own, g_low))
+    first, feed, x_own = lax.optimization_barrier((plane(first), feed, x_own))
+    x_pieces = share(x_own)
+    feed = fetch(plane(feed))
+    if many:
+        first = lax.all_gather(first, "g", axis=0, tiled=True)
+    first = jnp.concatenate([first] + [swap(first, "h", k) for k in range(1, size["h"])], 0)
+    later, x_pieces = lax.optimization_barrier((where, x_pieces))
+    first, next_feed = lax.optimization_barrier((first, plane(layer_pieces(later, 1))))
     first = jnp.concatenate([first, swap(first, "c")], 0)
     wq, table = launch(
         arrange_first_kernel(size), "arrange_first",
@@ -653,13 +670,9 @@
         )
         other = swap(kv, "c")
         if l + 1 == LAYERS:
-            g_low, x_own = lax.optimization_barrier((own_sequence(d_out), x_own))
             pieces = share(g_low)
-        if l == 0:
-            feed, other, later = lax.optimization_barrier((feed, other, where))
-        wf[l], wo[l], wp[l] = arrange(feed, D, D, D) if l == 0 else after
-        if l == 0:
-            feed = layer_pieces(later, 1, 1)
+            other, next_feed = lax.optimization_barrier((other, next_feed))
+            prepared = *arrange(next_feed, D, D), prepared
         if many:
             keys = all_keys(kv, other)
             out, lse = attend(q, keys, mask)
@@ -671,6 +684,10 @@
                          pltpu.VMEM((count, 2 * PW), bf16), pltpu.VMEM((count, PW), bf16)],
                 flops=4 * count * 2 * count * PW,
             )
+        if l == 0:
+            next_mixed, next_feed = fetch(next_feed[..., 2 * D :]), fetch(next_feed[..., : 2 * D])
+            prepared = arrange(after(feed, out), D, D, D)
+        wf[l], wo[l], wp[l] = prepared
         if l + 1 == LAYERS:
             out, pieces = lax.optimization_barrier((out, pieces))
         outs = [out] + [chip_swap(out, k) for k in range(1, TP)]
@@ -681,23 +698,22 @@
             where, table, x, *outs, wp[l], wf[l], wo[l],
             scratch=[pltpu.VMEM((TP, count, PW), bf16)], flops=6 * count * D * D,
         )
-        total = y0
-        for k, y in ((1, y1), (2, y2), (3, y3)):
-            total = total + chip_swap(y, k).astype(f32)
+        if l + 1 < LAYERS:
+            total = y0
+            for k, y in ((1, y1), (2, y2), (3, y3)):
+                total = total + chip_swap(y, k).astype(f32)
         saved.append((x, x_own, normed, q, kv, other, keys, lse, heads, mid, mid_own, normed2, up, act))
         if l + 1 < LAYERS:
             state = (mid, *share(total.astype(bf16)))
-            feed, state = lax.optimization_barrier((feed, state))
-            *after, wq[l + 1] = arrange(feed, D, D, D, 3 * PW)
-        else:
-            tokens_out = mid_own + total + table[8 * l + 1 : 8 * l + 2]
-    output = back_to_blocks(tokens_out.astype(bf16))
+            next_mixed, state = lax.optimization_barrier((next_mixed, state))
+            prepared, wq[l + 1] = arrange(next_mixed, D, 3 * PW)
+    last_parts = [y0, y1, y2, y3]
 
     copies = devices // (2 * TP)
     halves = [((copies * TP, shard, 2 * D), bf16)] * 2
 
-    def reduce_copies(keep, give):
-        total = (keep.astype(f32) + swap(give, "c").astype(f32)).astype(bf16)
+    def reduce_copies(keep, got):
+        total = (keep.astype(f32) + got.astype(f32)).astype(bf16)
         return lax.psum_scatter(total, COPIES, scatter_dimension=0, tiled=True)
 
     def by_owner(sums):
@@ -706,13 +722,9 @@
     line = ((8, D), f32)
     parts = [((own, D), f32)] + [((own, D), bf16)] * 3
     g_own = g_low
-    b_out_sum = jnp.broadcast_to(jnp.sum(g_low.astype(f32), 0, keepdims=True), (8, D))
     sums = [None] * LAYERS
-    feed_grads = [None] * LAYERS
     for l in reversed(range(LAYERS)):
         x, x_own, normed, q, kv, other, keys, lse, heads, mid, mid_own, normed2, up, act = saved[l]
-        if l + 1 < LAYERS:
-            pieces = share(g_low)
         g_all, g_up, b_fc_sum, norm2_sum, y0, y1, y2, y3 = launch(
             feed_back_kernel, f"feed_back_{l}", [((count, D), bf16), ((count, D), bf16), line, line] + parts,
             where, *pieces, up, mid, wo[l], wf[l], flops=4 * count * D * D,
@@ -723,15 +735,23 @@
             scratch=[pltpu.VMEM((devices, shard, 2 * D), bf16)], flops=4 * count * D * D,
         )
         if l + 1 == LAYERS:
-            got, keep, give, output = lax.optimization_barrier((got, keep, give, output))
+            got, keep, give = lax.optimization_barrier((got, keep, give))
         else:
             got, keep, give, mixed = lax.optimization_barrier((got, keep, give, mixed))
-        feed = reduce_copies(keep, give)
+        give = swap(give, "c")
         g_own, g_low, b_proj_sum = launch(
             norm_back_kernel(l, 4), f"norm2_back_{l}", [((own, D), f32), ((own, D), bf16), line],
             where, table, g_own, mid_own, y0, *got,
         )
+        give, g_low = lax.optimization_barrier((give, g_low))
+        feed = reduce_copies(keep, give)
         pieces = share(g_low)
+        if l + 1 == LAYERS:
+            last_parts, pieces[1] = lax.optimization_barrier((last_parts, pieces[1]))
+            total = last_parts[0]
+            for k in range(1, TP):
+                total = total + chip_swap(last_parts[k], k).astype(f32)
+            meanwhile = (mid_own + total + table[8 * l + 1 : 8 * l + 2]).astype(bf16)
         if many:
             g_attn = jnp.concatenate(pieces, 0)
             mine = lax.dynamic_slice_in_dim(wp[l], p * PW, PW, 0)
@@ -750,49 +770,58 @@
                 flops=10 * count * 2 * count * PW,
             )
         more = swap(give, "c")
-        if l == 0:
-            more, feed = lax.optimization_barrier((more, feed))
-        g_qkv, b_qkv_sum, norm1_sum, y0, y1, y2, y3 = launch(
-            leave_kernel, f"leave_{l}", [((count, 3 * PW), bf16), line, line] + parts,
-            where, dq, dkv, more, wq[l], x, flops=2 * count * D * 3 * PW,
-        )
-        got = [chip_swap(y, k) for k, y in ((1, y1), (2, y2), (3, y3))]
-        sums[l] = (b_proj_sum, b_out_sum, norm1_sum, norm2_sum, b_qkv_sum, b_fc_sum)
         if l > 0:
+            more, output = lax.optimization_barrier((more, meanwhile))
+        leave_outs = [((count, 3 * PW), bf16), line, line] + parts
+        sums[l] = (b_proj_sum, norm2_sum, b_fc_sum)
+        if l > 0:
+            g_qkv, b_qkv_sum, norm1_sum, y0, y1, y2, y3 = launch(
+                leave_kernel, f"leave_{l}", leave_outs, where, dq, dkv, more, wq[l], x, flops=2 * count * D * 3 * PW,
+            )
+            got = [chip_swap(y, k) for k, y in ((1, y1), (2, y2), (3, y3))]
             keep, give = launch(
                 mixed_weights_kernel, f"mixed_weights_{l}", [((copies * TP, shard, D), bf16)] * 2,
                 where, normed, g_qkv, heads, g_attn,
                 scratch=[pltpu.VMEM((devices, shard, D), bf16)], flops=4 * count * D * D,
             )
-            got, keep, give, feed = lax.optimization_barrier((got, keep, give, feed))
-            mixed = reduce_copies(keep, give)
+            got, keep, give, feed_last = lax.optimization_barrier((got, keep, give, feed))
+            give = swap(give, "c")
+            sums[l] = sums[l] + (norm1_sum, b_qkv_sum)
         else:
-            keep, give = launch(
-                last_weights_kernel, "last_weights", [((copies * TP, shard, D + 128), bf16)] * 2,
-                where, normed, g_qkv, heads, g_attn, *[item for per_layer in sums for item in per_layer],
+            keep, give, y0, y1, y2, y3 = launch(
+                leave_last_kernel, "leave_last", [((copies * TP, shard, D + 128), bf16)] * 2 + parts,
+                where, dq, dkv, more, wq[l], x, normed, heads, g_attn, *sums[0], *sums[1],
                 scratch=[pltpu.VMEM((devices, shard, D + 128), bf16), pltpu.VMEM((128, D), f32),
-                         pltpu.VMEM((devices, shard, 128), f32)],
-                flops=4 * count * D * D,
+                         pltpu.VMEM((devices, shard, 128), f32), pltpu.VMEM((count, 3 * PW), bf16),
+                         pltpu.VMEM((8, D), f32), pltpu.VMEM((8, D), f32)],
+                flops=6 * count * D * D,
             )
+            give, feed = lax.optimization_barrier((give, feed))
             last = (keep.astype(f32) + swap(give, "c").astype(f32)).astype(bf16)
-            got, last = lax.optimization_barrier((got, last))
-            last = lax.all_to_all(last, ("h", "g", "x", "f"), 0, 0, tiled=True)
-        feed_grads[l] = feed
-        g_own, g_low, b_out_sum = launch(
+            got = [chip_swap(y, k) for k, y in ((1, y1), (2, y2), (3, y3))]
+            last = lax.all_to_all(after(last, got[0]), ("h", "g", "x", "f"), 0, 0, tiled=True)
+            reduced = by_owner(after(jnp.concatenate([feed, feed_last, mixed], 2), got[0]))
+        g_own, g_low, _ = launch(
             norm_back_kernel(l, 2), f"norm1_back_{l}", [((own, D), f32), ((own, D), bf16), line],
             where, table, g_own, x_own, y0, *got,
         )
-    grad_tokens = back_to_blocks(g_own)
+        if l > 0:
+            give, g_low = lax.optimization_barrier((give, g_low))
+            mixed = reduce_copies(keep, give)
+            pieces = share(g_low)
+    g_low, reduced = lax.optimization_barrier((g_low, reduced))
+    tokens_back = back_to_blocks(jnp.concatenate([output, g_low], 1))
+    output, grad_tokens = tokens_back[..., :D], tokens_back[..., D:].astype(f32)
     d_wf, d_wo = launch(
         finish_feed_kernel, "finish_feed", [((LAYERS, shard, ff), f32), ((LAYERS, TP, shard, D), f32)],
-        where, *[item for l in range(LAYERS) for item in by_owner(feed_grads[l])],
+        where, *reduced,
         scratch=[pltpu.VMEM((TP, shard, 2 * D), bf16)],
     )
     d_wo = d_wo.reshape(w_out.shape)
     d_wq, d_wp, d_b_proj, d_b_out, d_g1, d_s1, d_g2, d_s2, d_b_qv, d_b_fc = launch(
         finish_mixed_kernel, "finish_mixed",
         [((LAYERS, shard, 3 * D), f32), ((LAYERS, shard, D), f32)] + [(item.shape, f32) for item in smalls],
-        where, last, *by_owner(mixed), scratch=[pltpu.VMEM((LAYERS, TP, shard, D), f32), pltpu.VMEM((128, 128), f32)],
+        where, last, *reduced, scratch=[pltpu.VMEM((LAYERS, TP, shard, D), f32), pltpu.VMEM((128, 128), f32)],
     )
     return (output, grad_tokens, d_wq, d_b_qv, d_wp, d_b_proj, d_g1, d_s1, d_g2, d_s2, d_wf, d_b_fc, d_wo, d_b_out)
 

time: 451 us -> 388 us (0.86)
  waiting for transfers between devices: 141 us -> 108 us
  starting transfers between devices: 106 us -> 89.1 us
  blocking collectives: 16.2 us -> 0 us
    ppermute x71 -> x69, waiting for transfers between devices: 113 us -> 85.6 us  [swap(): return lax.ppermute(value, axis, [(i, i ^ mask) for i in range(size)])]
    all_gather x1 -> x0, blocking collectives: 16.2 us -> none  [body(): first = lax.all_gather(first, COPIES, axis=0, tiled=True)]
    ppermute x8 -> x4, starting transfers between devices: 23.5 us -> 8.32 us  [both_ways(): lax.ppermute(item, ('h', 'f'), move)]
    ppermute x8 -> x4, waiting for transfers between devices: 27.9 us -> 17.8 us  [both_ways(): lax.ppermute(item, ('h', 'f'), move)]
    unnamed x134 -> x146, local copies, waits for them, and re-layouts: 9.58 us -> 14.5 us
    all_gather x2 -> x3, waiting for transfers between devices: 0.02 us -> 4.84 us  [fetch(): return lax.all_gather(pieces, COPIES, axis=0, tiled=True)]
    ppermute x71 -> x69, starting transfers between devices: 76.8 us -> 76 us  [swap(): return lax.ppermute(value, axis, [(i, i ^ mask) for i in range(size)])]
  transfers between devices with their start and end apart: 85 -> 80, of which waited for: 39 -> 35; matrix products, arithmetic and copies ran while one was open for 2% -> 3% of each run, Pallas kernels for 23% -> 32%
where the time goes in v3:
time: 388 us; the launch traced here: 380 us
  Pallas kernels  136 us (35%)
  waiting for transfers between devices  108 us (28%)
  starting transfers between devices  89.1 us (23%)
  local copies, waits for them, and re-layouts  18.2 us (5%)
  between operations  15.2 us (4%)
  other arithmetic  13 us (3%)
    pallas_call x28, Pallas kernels, launch(): pl.pallas_call(kernel, name=name, out_shape=shapes, in_specs=[pl.BlockSpe...  136 us
    ppermute x69, waiting for transfers between devices, swap(): return lax.ppermute(value, axis, [(i, i ^ mask) for i in range(size)])  85.6 us
    ppermute x69, starting transfers between devices, swap(): return lax.ppermute(value, axis, [(i, i ^ mask) for i in range(size)])  76 us
    ppermute x4, waiting for transfers between devices, both_ways(): lax.ppermute(item, ('h', 'f'), move)  17.8 us
    unnamed x146, local copies, waits for them, and re-layouts  14.5 us
    ppermute x4, starting transfers between devices, both_ways(): lax.ppermute(item, ('h', 'f'), move)  8.32 us
  transfers between devices with their start and end apart: 80, of which 35 were waited for; matrix products, arithmetic and copies ran while one was open for 3% of the time, Pallas kernels for 32%

profile of v3, /device:TPU:0, one launch (start us, length us, event | category | flops | bytes accessed | tf_op | source)
XLA Modules:
  0.0 380.0 jit_solution(6905875924572439049)
XLA Ops:
  8.3 4.1 %collective-permute-start.1 = (bf16[2,64,768]{2,1,0:T(8,128)(2,1)S(1)}, bf16[2,64,768]{2,1,0:T(8,128)(2,1)S(1)}, u32[]{:S(2)}, u32[]{:S(2)}) collective-permute-start(bf16[2,64,768]{2,1,0:T(8,128)(2,1)S(1)} %get-tuple-element.415), channel_id=1, source_target_pairs={{0,16},{1,24},{8,17},{9,25},{16,0},{17,8},{24,1},{25,9},{2,18},{3,... | collective-permute-start | bytes 589832 | tf_op jit(solution)/shard_map/ppermute | solution.py:584
  23.4 5.6 %collective-permute-start.3 = (bf16[24,640]{1,0:T(8,128)(2,1)S(1)}, bf16[24,640]{1,0:T(8,128)(2,1)S(1)}, u32[]{:S(2)}, u32[]{:S(2)}) collective-permute-start(bf16[24,640]{1,0:T(8,128)(2,1)S(1)} %copy-done.71), channel_id=1, source_target_pairs={{0,1},{1,0},{4,5},{5,4},{2,3},{3,2},{6,7},{7,6},{8,9},{9,8},{12,13... | collective-permute-start | bytes 92168 | tf_op jit(solution)/shard_map/ppermute | solution.py:39
  77.8 6.6 %attend_0.1 = (bf16[512,192]{1,0:T(8,128)(2,1)}, f32[512,3]{1,0:T(8,128)}) custom-call(s32[5]{0:T(128)} %stack.102.where, bf16[512,192]{1,0:T(8,128)(2,1)} %get-tuple-element.242.q_ref, bf16[512,384]{1,0:T(8,128)(2,1)} %get-tuple-element.243.own_ref, bf16[512,384]{1,0:T(8,128)(2,1)} %copy-done.47), custom_call_target="tpu_custom_call" | custom-call | flops 402653184 | bytes 1185792 | tf_op jit(solution)/shard_map/attend_0/pallas_call | solution.py:57
  92.5 4.8 %arrange.3 = (bf16[32,24,768]{2,1,0:T(8,128)(2,1)}, bf16[32,24,768]{2,1,0:T(8,128)(2,1)}, bf16[32,24,768]{2,1,0:T(8,128)(2,1)}) custom-call(s32[5]{0:T(128)} %stack.102.where, bf16[16,24,2304]{2,1,0:T(8,128)(2,1)} %all-gather.6.cloned.1.call-done.own, bf16[16,24,2304]{2,1,0:T(8,128)(2,1)} %copy-done.2), custom_call_target="tpu_custom_call" | custom-call | bytes 7077888 | tf_op jit(solution)/shard_map/arrange/pallas_call | solution.py:57
  97.3 6.4 %collective-permute-done.17.o2 = bf16[512,192]{1,0:T(8,128)(2,1)S(1)} collective-permute-done((bf16[512,192]{1,0:T(8,128)(2,1)}, bf16[512,192]{1,0:T(8,128)(2,1)S(1)}, u32[]{:S(2)}, u32[]{:S(2)}) %collective-permute-start.17) | collective-permute-done | bytes 196640 | tf_op jit(solution)/shard_map/ppermute | solution.py:39
  104.5 6.8 %middle_0.1 = (f32[512,768]{1,0:T(8,128)}, f32[128,768]{1,0:T(8,128)}, bf16[512,768]{1,0:T(8,128)(2,1)}, bf16[512,768]{1,0:T(8,128)(2,1)}, f32[512,768]{1,0:T(8,...) custom-call(s32[5]{0:T(128)} %stack.102.where, ...), custom_call_target="tpu_custom_call" | custom-call | flops 1811939328 | bytes 12828672 | tf_op jit(solution)/shard_map/middle_0/pallas_call | solution.py:57
  152.3 6.6 %attend_1.1 = (bf16[512,192]{1,0:T(8,128)(2,1)}, f32[512,3]{1,0:T(8,128)}) custom-call(s32[5]{0:T(128)} %stack.102.where, bf16[512,192]{1,0:T(8,128)(2,1)} %get-tuple-element.265.q_ref, bf16[512,384]{1,0:T(8,128)(2,1)} %get-tuple-element.266.own_ref, bf16[512,384]{1,0:T(8,128)(2,1)} %copy-done.48), custom_call_target="tpu_custom_call" | custom-call | flops 402653184 | bytes 1185792 | tf_op jit(solution)/shard_map/attend_1/pallas_call | solution.py:57
  171.0 5.1 %collective-permute-done.35.o2 = bf16[512,192]{1,0:T(8,128)(2,1)S(1)} collective-permute-done((bf16[512,192]{1,0:T(8,128)(2,1)}, bf16[512,192]{1,0:T(8,128)(2,1)S(1)}, u32[]{:S(2)}, u32[]{:S(2)}) %collective-permute-start.35) | collective-permute-done | bytes 196640 | tf_op jit(solution)/shard_map/ppermute | solution.py:39
  176.9 6.8 %middle_1.1 = (f32[512,768]{1,0:T(8,128)}, f32[128,768]{1,0:T(8,128)}, bf16[512,768]{1,0:T(8,128)(2,1)}, bf16[512,768]{1,0:T(8,128)(2,1)}, f32[512,768]{1,0:T(8,...) custom-call(s32[5]{0:T(128)} %stack.102.where, ...), custom_call_target="tpu_custom_call" | custom-call | flops 1811939328 | bytes 12828672 | tf_op jit(solution)/shard_map/middle_1/pallas_call | solution.py:57
  183.7 6.8 %feed_back_1.1 = (bf16[512,768]{1,0:T(8,128)(2,1)}, bf16[512,768]{1,0:T(8,128)(2,1)}, f32[8,768]{1,0:T(8,128)}, f32[8,768]{1,0:T(8,128)}, f32[128,768]{1,0:T(8,1...) custom-call(s32[5]{0:T(128)} %stack.102.where, bf16[128,768]{1,0:T(8,128)(2,1)} %bitcast.56, ...), custom_call_target="tpu_custom_call" | custom-call | flops 1207959552 | bytes 8896512 | tf_op jit(solution)/shard_map/feed_back_1/pallas_call | solution.py:57
  194.0 4.7 %feed_weights_1.1 = (bf16[16,24,1536]{2,1,0:T(8,128)(2,1)}, bf16[16,24,1536]{2,1,0:T(8,128)(2,1)}) custom-call(s32[5]{0:T(128)} %stack.102.where, bf16[512,768]{1,0:T(8,128)(2,1)} %get-tuple-element.285.act, bf16[512,768]{1,0:T(8,128)(2,1)} %get-tuple-element.286.g, bf16[512,768]{1,0:T(8,128)(2,1)} %get-tuple-element.287.normed, ...), custom_call_target="tpu_custom_call" | custom-call | flops 1207959552 | bytes 5505024 | tf_op jit(solution)/shard_map/feed_weights_1/pallas_call | solution.py:57
  209.9 4.3 %collective-permute-done.42.g1 = bf16[128,768]{1,0:T(8,128)(2,1)S(1)} collective-permute-done((bf16[128,768]{1,0:T(8,128)(2,1)S(1)}, bf16[128,768]{1,0:T(8,128)(2,1)S(1)}, u32[]{:S(2)}, u32[]{:S(2)}) %collective-permute-start.42) | collective-permute-done | bytes 196640 | tf_op jit(solution)/shard_map/ppermute | solution.py:39
  219.8 11.7 %attend_back_1.1 = (bf16[512,768]{1,0:T(8,128)(2,1)}, bf16[512,192]{1,0:T(8,128)(2,1)}, f32[512,384]{1,0:T(8,128)}, bf16[512,384]{1,0:T(8,128)(2,1)}) custom-call(s32[5]{0:T(128)} %stack.102.where, bf16[128,768]{1,0:T(8,128)(2,1)} %get-tuple-element.298.g0, bf16[128,768]{1,0:T(8,128)(2,1)} %copy-done.61, bf16[128,768]{1,0:T(8,128)(2,1)} %copy-done.62, ...), custom_call_target="tpu_custom_call" | custom-call | flops 1006632960 | bytes 5117952 | tf_op jit(solution)/shard_map/attend_back_1/pallas_call | solution.py:57
  234.1 4.3 %leave_1.1 = (bf16[512,576]{1,0:T(8,128)(2,1)}, f32[8,768]{1,0:T(8,128)}, f32[8,768]{1,0:T(8,128)}, f32[128,768]{1,0:T(8,128)}, bf16[128,768]{1,0:T(8,128)(2,1)}...) custom-call(s32[5]{0:T(128)} %stack.102.where, bf16[512,192]{1,0:T(8,128)(2,1)} %get-tuple-element.313.dq, ...), custom_call_target="tpu_custom_call" | custom-call | flops 452984832 | bytes 5455872 | tf_op jit(solution)/shard_map/leave_1/pallas_call | solution.py:57
  242.0 4.4 %mixed_weights_1.1 = (bf16[16,24,768]{2,1,0:T(8,128)(2,1)}, bf16[16,24,768]{2,1,0:T(8,128)(2,1)}) custom-call(s32[5]{0:T(128)} %stack.102.where, bf16[512,768]{1,0:T(8,128)(2,1)} %get-tuple-element.320.normed, bf16[512,576]{1,0:T(8,128)(2,1)} %get-tuple-element.321.g_qkv, bf16[512,768]{1,0:T(8,128)(2,1)} %get-tuple-element.322.heads, ...), custom_call_target="tpu_custom_call" | custom-call | flops 1207959552 | bytes 4128768 | tf_op jit(solution)/shard_map/mixed_weights_1/pallas_call | solution.py:57
  258.2 4.3 %collective-permute-done.53.g1 = bf16[128,768]{1,0:T(8,128)(2,1)S(1)} collective-permute-done((bf16[128,768]{1,0:T(8,128)(2,1)S(1)}, bf16[128,768]{1,0:T(8,128)(2,1)S(1)}, u32[]{:S(2)}, u32[]{:S(2)}) %collective-permute-start.53) | collective-permute-done | bytes 196640 | tf_op jit(solution)/shard_map/ppermute | solution.py:39
  262.5 4.4 %collective-permute-done.54.g2 = bf16[128,768]{1,0:T(8,128)(2,1)S(1)} collective-permute-done((bf16[128,768]{1,0:T(8,128)(2,1)S(1)}, bf16[128,768]{1,0:T(8,128)(2,1)S(1)}, u32[]{:S(2)}, u32[]{:S(2)}) %collective-permute-start.54) | collective-permute-done | bytes 196640 | tf_op jit(solution)/shard_map/ppermute | solution.py:39
  267.7 6.8 %feed_back_0.1 = (bf16[512,768]{1,0:T(8,128)(2,1)}, bf16[512,768]{1,0:T(8,128)(2,1)}, f32[8,768]{1,0:T(8,128)}, f32[8,768]{1,0:T(8,128)}, f32[128,768]{1,0:T(8,1...) custom-call(s32[5]{0:T(128)} %stack.102.where, ...), custom_call_target="tpu_custom_call" | custom-call | flops 1207959552 | bytes 8896512 | tf_op jit(solution)/shard_map/feed_back_0/pallas_call | solution.py:57
  278.0 4.8 %feed_weights_0.1 = (bf16[16,24,1536]{2,1,0:T(8,128)(2,1)}, bf16[16,24,1536]{2,1,0:T(8,128)(2,1)}) custom-call(s32[5]{0:T(128)} %stack.102.where, bf16[512,768]{1,0:T(8,128)(2,1)} %get-tuple-element.341.act, bf16[512,768]{1,0:T(8,128)(2,1)} %get-tuple-element.342.g, bf16[512,768]{1,0:T(8,128)(2,1)} %get-tuple-element.343.normed, ...), custom_call_target="tpu_custom_call" | custom-call | flops 1207959552 | bytes 5505024 | tf_op jit(solution)/shard_map/feed_weights_0/pallas_call | solution.py:57
  294.0 4.3 %collective-permute-done.60.g1 = bf16[128,768]{1,0:T(8,128)(2,1)S(1)} collective-permute-done((bf16[128,768]{1,0:T(8,128)(2,1)S(1)}, bf16[128,768]{1,0:T(8,128)(2,1)S(1)}, u32[]{:S(2)}, u32[]{:S(2)}) %collective-permute-start.60) | collective-permute-done | bytes 196640 | tf_op jit(solution)/shard_map/ppermute | solution.py:39
  298.3 4.1 %collective-permute-done.61.g2 = bf16[128,768]{1,0:T(8,128)(2,1)S(1)} collective-permute-done((bf16[128,768]{1,0:T(8,128)(2,1)S(1)}, bf16[128,768]{1,0:T(8,128)(2,1)S(1)}, u32[]{:S(2)}, u32[]{:S(2)}) %collective-permute-start.61) | collective-permute-done | bytes 196640 | tf_op jit(solution)/shard_map/ppermute | solution.py:39
  303.2 11.9 %attend_back_0.1 = (bf16[512,768]{1,0:T(8,128)(2,1)}, bf16[512,192]{1,0:T(8,128)(2,1)}, f32[512,384]{1,0:T(8,128)}, bf16[512,384]{1,0:T(8,128)(2,1)}) custom-call(s32[5]{0:T(128)} %stack.102.where, bf16[128,768]{1,0:T(8,128)(2,1)} %get-tuple-element.356.g0, bf16[128,768]{1,0:T(8,128)(2,1)} %copy-done.64, bf16[128,768]{1,0:T(8,128)(2,1)} %copy-done.65, ...), custom_call_target="tpu_custom_call" | custom-call | flops 1006632960 | bytes 5117952 | tf_op jit(solution)/shard_map/attend_back_0/pallas_call | solution.py:57
  317.7 7.4 %leave_last.1 = (bf16[16,24,896]{2,1,0:T(8,128)(2,1)}, bf16[16,24,896]{2,1,0:T(8,128)(2,1)}, f32[128,768]{1,0:T(8,128)}, bf16[128,768]{1,0:T(8,128)(2,1)}, bf16[...) custom-call(s32[5]{0:T(128)} %stack.102.where, bf16[512,192]{1,0:T(8,128)(2,1)} %get-tuple-element.358.dq, ...), custom_call_target="tpu_custom_call" | custom-call | flops 1811939328 | bytes 8749056 | tf_op jit(solution)/shard_map/leave_last/pallas_call | solution.py:57
  353.7 14.8 %collective-permute-done.71 = bf16[64,1536]{1,0:T(8,128)(2,1)S(1)} collective-permute-done((bf16[64,1536]{1,0:T(8,128)(2,1)S(1)}, bf16[64,1536]{1,0:T(8,128)(2,1)S(1)}, u32[]{:S(2)}, u32[]{:S(2)}) %collective-permute-start.71) | collective-permute-done | bytes 196640 | tf_op jit(solution)/shard_map/ppermute | solution.py:584
  (340 shorter events, 213.1 us)
Async XLA Ops:
  7.2 79.3 %all-gather.6.cloned.1.call-start = ((), (), s32[]{:S(2)}) async-start(), calls=%async_computation.5 | async-start | bytes 2211840 | tf_op jit(solution)/shard_map/all_gather | solution.py:610
  8.3 13.3 %collective-permute-start.1 = (bf16[2,64,768]{2,1,0:T(8,128)(2,1)S(1)}, bf16[2,64,768]{2,1,0:T(8,128)(2,1)S(1)}, u32[]{:S(2)}, u32[]{:S(2)}) collective-permute-start(bf16[2,64,768]{2,1,0:T(8,128)(2,1)S(1)} %get-tuple-element.415), channel_id=1, source_target_pairs={{0,16},{1,24},{8,17},{9,25},{16,0},{17,8},{24,1},{25,9},{2,18},{3,... | collective-permute-start | bytes 589832 | tf_op jit(solution)/shard_map/ppermute | solution.py:584
  41.1 86.5 %all-gather.4.cloned.1.call-start = ((), (), s32[]{:S(2)}) async-start(), calls=%async_computation.4 | async-start | bytes 1351680 | tf_op jit(solution)/shard_map/all_gather | solution.py:610
  44.7 14.1 %collective-permute-start.5 = (bf16[4,24,640]{2,1,0:T(8,128)(2,1)S(1)}, bf16[4,24,640]{2,1,0:T(8,128)(2,1)S(1)}, u32[]{:S(2)}, u32[]{:S(2)}) collective-permute-start(bf16[4,24,640]{2,1,0:T(8,128)(2,1)S(1)} %pad_maximum_fusion.6), channel_id=1, source_target_pairs={{0,8},{8,0},{16,24},{24,16},{1,9},{9,1},{17,25},{25,17},{2,10},{10... | collective-permute-start | bytes 368648 | tf_op jit(solution)/shard_map/ppermute | solution.py:39
  47.5 12.3 %collective-permute-start.6 = (bf16[4,24,640]{2,1,0:T(8,128)(2,1)S(1)}, bf16[4,24,640]{2,1,0:T(8,128)(2,1)S(1)}, u32[]{:S(2)}, u32[]{:S(2)}) collective-permute-start(bf16[4,24,640]{2,1,0:T(8,128)(2,1)S(1)} %pad_maximum_fusion.6), channel_id=1, source_target_pairs={{0,16},{8,24},{16,0},{24,8},{1,17},{9,25},{17,1},{25,9},{2,18},{10... | collective-permute-start | bytes 368648 | tf_op jit(solution)/shard_map/ppermute | solution.py:39
  87.4 61.4 %all-gather.8.cloned.1.call-start = ((), (), s32[]{:S(2)}) async-start(), calls=%async_computation.6 | async-start | bytes 1474560 | tf_op jit(solution)/shard_map/all_gather | solution.py:610
  89.4 14.2 %collective-permute-start.17 = (bf16[512,192]{1,0:T(8,128)(2,1)}, bf16[512,192]{1,0:T(8,128)(2,1)S(1)}, u32[]{:S(2)}, u32[]{:S(2)}) collective-permute-start(bf16[512,192]{1,0:T(8,128)(2,1)} %get-tuple-element.244.o0), channel_id=1, source_target_pairs={{0,1},{1,0},{4,5},{5,4},{2,3},{3,2},{6,7},{7,6},{8,9},{9,8},{12,13... | collective-permute-start | bytes 589832 | tf_op jit(solution)/shard_map/ppermute | solution.py:39
  90.8 12.9 %collective-permute-start.18 = (bf16[512,192]{1,0:T(8,128)(2,1)}, bf16[512,192]{1,0:T(8,128)(2,1)S(1)}, u32[]{:S(2)}, u32[]{:S(2)}) collective-permute-start(bf16[512,192]{1,0:T(8,128)(2,1)} %get-tuple-element.244.o0), channel_id=1, source_target_pairs={{0,5},{1,4},{4,1},{5,0},{2,7},{3,6},{6,3},{7,2},{8,13},{9,12},{12,... | collective-permute-start | bytes 589832 | tf_op jit(solution)/shard_map/ppermute | solution.py:39
  115.5 134.5 %reduce-scatter.4.cloned.1.call-start = ((), (), s32[]{:S(2)}) async-start(), calls=%async_computation.7 | async-start | bytes 1474560 | tf_op jit(solution)/shard_map/reduce_scatter | solution.py:717
  148.8 16.3 %collective-permute-start.37 = (bf16[16,24,1536]{2,1,0:T(8,128)(2,1)}, bf16[16,24,1536]{2,1,0:T(8,128)(2,1)S(1)}, u32[]{:S(2)}, u32[]{:S(2)}) collective-permute-start(bf16[16,24,1536]{2,1,0:T(8,128)(2,1)} %all-gather.8.cloned.1.call-done.own), channel_id=1, source_target_pairs={{0,2},{2,0},{1,3},{3,1},{4,6},{6,4},{5,7},{7,5},{8,10},{10,8},{9,1... | collective-permute-start | bytes 3538952 | tf_op jit(solution)/shard_map/ppermute | solution.py:39
  150.3 11.2 %collective-permute-start.32 = (bf16[128,768]{1,0:T(8,128)(2,1)S(1)}, bf16[128,768]{1,0:T(8,128)(2,1)S(1)}, u32[]{:S(2)}, u32[]{:S(2)}) collective-permute-start(bf16[128,768]{1,0:T(8,128)(2,1)S(1)} %bitcast.54), channel_id=1, source_target_pairs={{0,1},{1,0},{4,5},{5,4},{2,3},{3,2},{6,7},{7,6},{8,9},{9,8},{12,13... | collective-permute-start | bytes 589832 | tf_op jit(solution)/shard_map/ppermute | solution.py:39
  162.7 13.4 %collective-permute-start.35 = (bf16[512,192]{1,0:T(8,128)(2,1)}, bf16[512,192]{1,0:T(8,128)(2,1)S(1)}, u32[]{:S(2)}, u32[]{:S(2)}) collective-permute-start(bf16[512,192]{1,0:T(8,128)(2,1)} %get-tuple-element.275.o0), channel_id=1, source_target_pairs={{0,1},{1,0},{4,5},{5,4},{2,3},{3,2},{6,7},{7,6},{8,9},{9,8},{12,13... | collective-permute-start | bytes 589832 | tf_op jit(solution)/shard_map/ppermute | solution.py:39
  163.6 12.5 %collective-permute-start.36 = (bf16[512,192]{1,0:T(8,128)(2,1)}, bf16[512,192]{1,0:T(8,128)(2,1)S(1)}, u32[]{:S(2)}, u32[]{:S(2)}) collective-permute-start(bf16[512,192]{1,0:T(8,128)(2,1)} %get-tuple-element.275.o0), channel_id=1, source_target_pairs={{0,5},{1,4},{4,1},{5,0},{2,7},{3,6},{6,3},{7,2},{8,13},{9,12},{12,... | collective-permute-start | bytes 589832 | tf_op jit(solution)/shard_map/ppermute | solution.py:39
  205.5 79.4 %reduce-scatter.6.cloned.1.call-start = ((), (), s32[]{:S(2)}) async-start(), calls=%async_computation.8 | async-start | bytes 737280 | tf_op jit(solution)/shard_map/reduce_scatter | solution.py:717
  214.2 18.0 %collective-permute-start.46 = (bf16[128,768]{1,0:T(8,128)(2,1)S(1)}, bf16[128,768]{1,0:T(8,128)(2,1)S(1)}, u32[]{:S(2)}, u32[]{:S(2)}) collective-permute-start(bf16[128,768]{1,0:T(8,128)(2,1)S(1)} %copy-done.58), channel_id=1, source_target_pairs={{0,4},{1,5},{4,0},{5,1},{2,6},{3,7},{6,2},{7,3},{8,12},{9,13},{12,... | collective-permute-start | bytes 589832 | tf_op jit(solution)/shard_map/ppermute | solution.py:39
  215.4 16.9 %collective-permute-start.47 = (bf16[128,768]{1,0:T(8,128)(2,1)S(1)}, bf16[128,768]{1,0:T(8,128)(2,1)S(1)}, u32[]{:S(2)}, u32[]{:S(2)}) collective-permute-start(bf16[128,768]{1,0:T(8,128)(2,1)S(1)} %copy-done.57), channel_id=1, source_target_pairs={{0,1},{1,0},{4,5},{5,4},{2,3},{3,2},{6,7},{7,6},{8,9},{9,8},{12,13... | collective-permute-start | bytes 589832 | tf_op jit(solution)/shard_map/ppermute | solution.py:39
  215.9 16.3 %collective-permute-start.48 = (bf16[128,768]{1,0:T(8,128)(2,1)S(1)}, bf16[128,768]{1,0:T(8,128)(2,1)S(1)}, u32[]{:S(2)}, u32[]{:S(2)}) collective-permute-start(bf16[128,768]{1,0:T(8,128)(2,1)S(1)} %copy-done.56), channel_id=1, source_target_pairs={{0,5},{1,4},{4,1},{5,0},{2,7},{3,6},{6,3},{7,2},{8,13},{9,12},{12,... | collective-permute-start | bytes 589832 | tf_op jit(solution)/shard_map/ppermute | solution.py:39
  254.4 74.3 %reduce-scatter.8.cloned.1.call-start = ((), (), s32[]{:S(2)}) async-start(), calls=%async_computation.9 | async-start | bytes 1474560 | tf_op jit(solution)/shard_map/reduce_scatter | solution.py:717
  326.0 16.3 %collective-permute-start.65 = (bf16[128,768]{1,0:T(8,128)(2,1)}, bf16[128,768]{1,0:T(8,128)(2,1)S(1)}, u32[]{:S(2)}, u32[]{:S(2)}) collective-permute-start(bf16[128,768]{1,0:T(8,128)(2,1)} %get-tuple-element.374), channel_id=1, source_target_pairs={{0,1},{1,0},{4,5},{5,4},{2,3},{3,2},{6,7},{7,6},{8,9},{9,8},{12,13... | collective-permute-start | bytes 589832 | tf_op jit(solution)/shard_map/ppermute | solution.py:39
  327.2 15.1 %collective-permute-start.66 = (bf16[128,768]{1,0:T(8,128)(2,1)}, bf16[128,768]{1,0:T(8,128)(2,1)S(1)}, u32[]{:S(2)}, u32[]{:S(2)}) collective-permute-start(bf16[128,768]{1,0:T(8,128)(2,1)} %get-tuple-element.375), channel_id=1, source_target_pairs={{0,5},{1,4},{4,1},{5,0},{2,7},{3,6},{6,3},{7,2},{8,13},{9,12},{12,... | collective-permute-start | bytes 589832 | tf_op jit(solution)/shard_map/ppermute | solution.py:39
  333.9 11.8 %collective-permute-start.67 = (bf16[24,3840]{1,0:T(8,128)(2,1)S(1)}, bf16[24,3840]{1,0:T(8,128)(2,1)S(1)}, u32[]{:S(2)}, u32[]{:S(2)}) collective-permute-start(bf16[24,3840]{1,0:T(8,128)(2,1)S(1)} %get-tuple-element.406), channel_id=1, source_target_pairs={{0,4},{1,5},{4,0},{5,1},{2,6},{3,7},{6,2},{7,3},{8,12},{9,13},{12,... | collective-permute-start | bytes 552968 | tf_op jit(solution)/shard_map/ppermute | solution.py:39
  334.7 11.0 %collective-permute-start.68 = (bf16[24,3840]{1,0:T(8,128)(2,1)S(1)}, bf16[24,3840]{1,0:T(8,128)(2,1)S(1)}, u32[]{:S(2)}, u32[]{:S(2)}) collective-permute-start(bf16[24,3840]{1,0:T(8,128)(2,1)S(1)} %get-tuple-element.405), channel_id=1, source_target_pairs={{0,1},{1,0},{4,5},{5,4},{2,3},{3,2},{6,7},{7,6},{8,9},{9,8},{12,13... | collective-permute-start | bytes 552968 | tf_op jit(solution)/shard_map/ppermute | solution.py:39
  338.4 31.0 %all-to-all-start = ((bf16[16,24,896]{2,1,0:T(8,128)(2,1)}), bf16[16,24,896]{2,1,0:T(8,128)(2,1)S(1)}, u32[]{:S(2)}, u32[]{:S(2)}) async-start(bf16[16,24,896]{2,1,0:T(8,128)(2,1)} %add_convert_fusion.2), calls=%async_computation.3 | async-start | bytes 1376256 | tf_op jit(solution)/shard_map/all_to_all | solution.py:802
  347.6 20.9 %collective-permute-start.71 = (bf16[64,1536]{1,0:T(8,128)(2,1)S(1)}, bf16[64,1536]{1,0:T(8,128)(2,1)S(1)}, u32[]{:S(2)}, u32[]{:S(2)}) collective-permute-start(bf16[64,1536]{1,0:T(8,128)(2,1)S(1)} %get-tuple-element.411), channel_id=1, source_target_pairs={{16,0},{24,1},{17,8},{25,9},{0,16},{8,17},{1,24},{9,25},{18,2},{26... | collective-permute-start | bytes 589832 | tf_op jit(solution)/shard_map/ppermute | solution.py:584
  (129 other events, 1031.7 us)
Sparse Core Ops, SparseCore 0:
  41.2 45.2 all-gather.5
  88.1 28.5 all-gather.3
  118.8 29.9 all-gather.7
  205.6 27.1 reduce-scatter.3
  254.5 20.4 reduce-scatter.5
  289.8 27.4 reduce-scatter.7
